TPU v7x, 128 devices: a whole 4x4x4 slice. The times are simulated.
128 devices in a mesh: group: 16 (over y, x_hi, core), blk: 8 (over x_lo, z).
Axes of the slice: x: 4 (x_hi: 2, x_lo: 2; x = x_hi * 2 + x_lo), y: 4, z: 4, core: 2. Of those that a mesh axis runs over, the one named last changes fastest.
Arguments:
- embeddings: float32 [65536, 768], P(('group', 'blk')), may hold values from -6 to 6
- clusters: int32 [65536], P(('group', 'blk')), may hold values from 0 to 63, as said below
- indices: int32 [65536], P(('group', 'blk')), may hold values from 0 to 65535, each once
Outputs:
- nearest: float32 [65536], P(('group', 'blk'))
Inputs may be any that keep to these rules, and one draw needn't show every extreme that they name: The cluster c is owned by group c mod 16. Of one device's 512 points at most 64 lie in clusters of one owner group, and every device has exactly 64 points in clusters of one owner group, the same group for all devices. Of one device's points at most 16 lie in any one cluster, and exactly that many in each cluster of that group. `indices`: each number appears once.
All inputs are finite; a program needn't handle non-finite values.
Results may differ from a plain program's by a relative error of at most 0.0003.
Values sent between devices are 32-bit elements; how exact they have to be, the bound alone decides.
No kernel may reach another device: no remote copies, remote signals or barrier semaphores. Data moves between devices by JAX's collectives and lax.ppermute only.
A program may use at most 128 MiB of HBM per device.

v0:
```python
import math

import jax
import jax.numpy as jnp
from jax import lax
from jax.sharding import PartitionSpec as P

EPS = 1e-06


def inner_tile(rows, cols):
    return lax.dot_general(
        rows,
        cols,
        (((1,), (1,)), ((), ())),
        precision=lax.Precision.HIGHEST,
        preferred_element_type=jnp.float32,
    )


def earlier_mask(row_cl, row_ix, col_cl, col_ix):
    return (
        (row_cl[:, None] == col_cl[None, :])
        & (col_cl[None, :] >= 0)
        & (col_ix[None, :] < row_ix[:, None])
    )


def on_device(embeddings, clusters, indices):
    groups = lax.axis_size("group")
    count = embeddings.shape[0]
    width = embeddings.shape[1]
    capacity = 2 * count // groups
    unit = embeddings * lax.rsqrt(jnp.sum(embeddings * embeddings, axis=1, keepdims=True) + EPS)
    owner = clusters % groups
    onehot = (owner[:, None] == jnp.arange(groups)[None, :]).astype(jnp.int32)
    place = jnp.sum((jnp.cumsum(onehot, axis=0) - onehot) * onehot, axis=1)
    target = owner * capacity + place
    sending = jnp.zeros((groups * capacity, width), jnp.float32).at[target].set(unit)
    send_cl = jnp.full((groups * capacity,), -1, jnp.int32).at[target].set(clusters)
    send_ix = jnp.full((groups * capacity,), -1, jnp.int32).at[target].set(indices)
    send_tags = jnp.stack(
        [send_cl.reshape(groups, capacity), send_ix.reshape(groups, capacity)], axis=1
    )
    held, held_tags = (
        lax.all_to_all(
            sending.reshape(groups, capacity, width),
            "group",
            split_axis=0,
            concat_axis=0,
            tiled=True,
        ),
        lax.all_to_all(send_tags, "group", split_axis=0, concat_axis=0, tiled=True),
    )
    held = held.reshape(groups * capacity, width)
    held_cl = held_tags[:, 0, :].reshape(groups * capacity)
    held_ix = held_tags[:, 1, :].reshape(groups * capacity)
    total = groups * capacity
    start_best = jnp.full((total,), -1.0, jnp.float32)
    cols = lax.all_gather(held, "blk", axis=0, tiled=True)
    col_cl = lax.all_gather(held_cl, "blk", axis=0, tiled=True)
    col_ix = lax.all_gather(held_ix, "blk", axis=0, tiled=True)
    length = cols.shape[0]
    step = math.gcd(length, 1024)
    pieces = length // step

    def one_step(current, number):
        part_cols = lax.dynamic_slice_in_dim(cols, number * step, step, 0)
        part_cl = lax.dynamic_slice_in_dim(col_cl, number * step, step, 0)
        part_ix = lax.dynamic_slice_in_dim(col_ix, number * step, step, 0)
        sims = inner_tile(held, part_cols)
        masked = jnp.where(earlier_mask(held_cl, held_ix, part_cl, part_ix), sims, -1.0)
        return (jnp.maximum(current, jnp.max(masked, axis=1)), None)

    result, unused = lax.scan(one_step, start_best, jnp.arange(pieces))
    answered = lax.all_to_all(
        result.reshape(groups, capacity), "group", split_axis=0, concat_axis=0, tiled=True
    )
    return answered.reshape(groups * capacity)[target]


def solution(mesh):
    return jax.shard_map(
        on_device,
        mesh=mesh,
        in_specs=(P(("group", "blk"), None), P(("group", "blk")), P(("group", "blk"))),
        out_specs=P(("group", "blk")),
        check_vma=False,
    )
```

profile of v0, /device:TPU:1, one launch (start us, length us, event | category | flops | bytes accessed | tf_op | source)
XLA Modules:
  0.0 463.7 jit_solution(3168402638740357752)
XLA Ops:
  6.5 0.7 add_select_fusion
  7.2 0.7 fusion.20
  7.9 1.2 reduce-window.6
  9.4 0.7 compare_select_fusion
  10.1 1.6 multiply_reduce_fusion
  11.7 4.0 scatter_custom_fusion.2
  15.8 47.7 %all_to_all.19 = f32[16,64,768]{2,1,0:T(8,128)} all-to-all(f32[16,64,768]{2,1,0:T(8,128)S(1)} %bitcast.37), channel_id=1, replica_groups=mesh['group'=16,'blk'=8] {'group'}, dimensions={0} | all-to-all | bytes 6291456 | tf_op jit(solution)/shard_map/all_to_all | solution.py:46
  63.5 2.7 scatter_custom_fusion
  66.3 2.6 scatter_custom_fusion.1
  69.1 0.7 reshape.128
  69.7 4.4 all-to-all-start
  74.2 7.0 %all-to-all-done = s32[16,1,128]{2,1,0:T(1,128)S(1)} async-done(((s32[16,1,128]{2,1,0:T(1,128)}), s32[16,1,128]{2,1,0:T(1,128)S(1)}, u32[]{:S(2)}, u32[]{:S(2)}) %all-to-all-start) | async-done | bytes 8224 | tf_op jit(solution)/shard_map/all_to_all | solution.py:53
  81.8 0.7 reduce.22
  82.8 24.6 %all_gather.9 = s32[8192]{0:T(1024)S(1)} all-gather(s32[1024]{0:T(1024)S(1)} %reshape_squeeze.6), channel_id=1, replica_groups=mesh['group'=16,'blk'=8] {'blk'}, dimensions={0}, use_global_device_ids=true | all-gather | bytes 36864 | tf_op jit(solution)/shard_map/all_gather | solution.py:61
  107.4 24.4 %all_gather.10 = s32[8192]{0:T(1024)S(1)} all-gather(s32[1024]{0:T(1024)S(1)} %reshape_squeeze.7), channel_id=1, replica_groups=mesh['group'=16,'blk'=8] {'blk'}, dimensions={0}, use_global_device_ids=true | all-gather | bytes 36864 | tf_op jit(solution)/shard_map/all_gather | solution.py:62
  131.8 180.1 %all-gather.2.cloned.1.call-done = f32[8192,768]{1,0:T(8,128)} async-done(((f32[1024,768]{1,0:T(8,128)}), f32[8192,768]{1,0:T(8,128)}) %all-gather.2.cloned.1.call-update) | async-done | bytes 25165840 | tf_op jit(solution)/shard_map/all_gather | solution.py:60
  311.9 125.5 %while.11 = (s32[]{:T(128)}, f32[1024]{0:T(1024)S(1)}, s32[16,1,64]{2,1,0:T(1,128)S(1)}, s32[8]{0:T(128)S(1)}, s32[8192]{0:T(1024)S(1)}, /*index=5*/s32[8192]{0:...) while((s32[]{:T(128)}, f32[1024]{0:T(1024)S(1)}, ...), condition=%wide.region_9.10_spmd.clone, body=%wide.region_7.9_spmd.clone.sunk | while | flops 9669969920 | bytes 6375653 | solution.py:75
  313.7 0.6 reduce.25
  314.4 0.6 reduce.26
  315.1 12.4 %fusion.26 = f32[1024]{0:T(1024)S(1)} fusion(f32[1024,768]{1,0:T(8,128)S(1)} %get-tuple-element.200, f32[8192,768]{1,0:T(8,128)} %get-tuple-element.199, s32[]{:T(128)S(6)} %select_n.38, s32[1024]{0:T(1024)S(1)} %lt.62, s32[1024]{0:T(1024)S(1)} %eq.75, s32[1024]{0:T(1024)S(1)} %dynamic_slice.29, s32[1024]{0:T(1024)S(1)} %get-tuple-element.164, ...), kind=kOutput, calls=%fused_computation.5.clone.1 | convolution fusion | flops 9669966848 | bytes 6312964 | tf_op jit(solution)/shard_map/while/body/eval_jaxpr/dot_general | solution.py:12
  327.6 0.6 dynamic_slice.28
  329.4 0.6 reduce.25
  330.1 0.6 reduce.26
  330.8 12.4 %fusion.26 = f32[1024]{0:T(1024)S(1)} fusion(f32[1024,768]{1,0:T(8,128)S(1)} %get-tuple-element.200, f32[8192,768]{1,0:T(8,128)} %get-tuple-element.199, s32[]{:T(128)S(6)} %select_n.38, s32[1024]{0:T(1024)S(1)} %lt.62, s32[1024]{0:T(1024)S(1)} %eq.75, s32[1024]{0:T(1024)S(1)} %dynamic_slice.29, s32[1024]{0:T(1024)S(1)} %get-tuple-element.164, ...), kind=kOutput, calls=%fused_computation.5.clone.1 | convolution fusion | flops 9669966848 | bytes 6312964 | tf_op jit(solution)/shard_map/while/body/eval_jaxpr/dot_general | solution.py:12
  345.1 0.6 reduce.25
  345.8 0.6 reduce.26
  346.5 12.4 %fusion.26 = f32[1024]{0:T(1024)S(1)} fusion(f32[1024,768]{1,0:T(8,128)S(1)} %get-tuple-element.200, f32[8192,768]{1,0:T(8,128)} %get-tuple-element.199, s32[]{:T(128)S(6)} %select_n.38, s32[1024]{0:T(1024)S(1)} %lt.62, s32[1024]{0:T(1024)S(1)} %eq.75, s32[1024]{0:T(1024)S(1)} %dynamic_slice.29, s32[1024]{0:T(1024)S(1)} %get-tuple-element.164, ...), kind=kOutput, calls=%fused_computation.5.clone.1 | convolution fusion | flops 9669966848 | bytes 6312964 | tf_op jit(solution)/shard_map/while/body/eval_jaxpr/dot_general | solution.py:12
  360.8 0.6 reduce.25
  361.5 0.6 reduce.26
  362.2 12.4 %fusion.26 = f32[1024]{0:T(1024)S(1)} fusion(f32[1024,768]{1,0:T(8,128)S(1)} %get-tuple-element.200, f32[8192,768]{1,0:T(8,128)} %get-tuple-element.199, s32[]{:T(128)S(6)} %select_n.38, s32[1024]{0:T(1024)S(1)} %lt.62, s32[1024]{0:T(1024)S(1)} %eq.75, s32[1024]{0:T(1024)S(1)} %dynamic_slice.29, s32[1024]{0:T(1024)S(1)} %get-tuple-element.164, ...), kind=kOutput, calls=%fused_computation.5.clone.1 | convolution fusion | flops 9669966848 | bytes 6312964 | tf_op jit(solution)/shard_map/while/body/eval_jaxpr/dot_general | solution.py:12
  376.5 0.6 reduce.25
  377.2 0.6 reduce.26
  377.9 12.4 %fusion.26 = f32[1024]{0:T(1024)S(1)} fusion(f32[1024,768]{1,0:T(8,128)S(1)} %get-tuple-element.200, f32[8192,768]{1,0:T(8,128)} %get-tuple-element.199, s32[]{:T(128)S(6)} %select_n.38, s32[1024]{0:T(1024)S(1)} %lt.62, s32[1024]{0:T(1024)S(1)} %eq.75, s32[1024]{0:T(1024)S(1)} %dynamic_slice.29, s32[1024]{0:T(1024)S(1)} %get-tuple-element.164, ...), kind=kOutput, calls=%fused_computation.5.clone.1 | convolution fusion | flops 9669966848 | bytes 6312964 | tf_op jit(solution)/shard_map/while/body/eval_jaxpr/dot_general | solution.py:12
  392.1 0.6 reduce.25
  392.9 0.6 reduce.26
  393.6 12.4 %fusion.26 = f32[1024]{0:T(1024)S(1)} fusion(f32[1024,768]{1,0:T(8,128)S(1)} %get-tuple-element.200, f32[8192,768]{1,0:T(8,128)} %get-tuple-element.199, s32[]{:T(128)S(6)} %select_n.38, s32[1024]{0:T(1024)S(1)} %lt.62, s32[1024]{0:T(1024)S(1)} %eq.75, s32[1024]{0:T(1024)S(1)} %dynamic_slice.29, s32[1024]{0:T(1024)S(1)} %get-tuple-element.164, ...), kind=kOutput, calls=%fused_computation.5.clone.1 | convolution fusion | flops 9669966848 | bytes 6312964 | tf_op jit(solution)/shard_map/while/body/eval_jaxpr/dot_general | solution.py:12
  406.1 0.6 dynamic_slice.28
  407.8 0.6 reduce.25
  408.6 0.6 reduce.26
  409.3 12.4 %fusion.26 = f32[1024]{0:T(1024)S(1)} fusion(f32[1024,768]{1,0:T(8,128)S(1)} %get-tuple-element.200, f32[8192,768]{1,0:T(8,128)} %get-tuple-element.199, s32[]{:T(128)S(6)} %select_n.38, s32[1024]{0:T(1024)S(1)} %lt.62, s32[1024]{0:T(1024)S(1)} %eq.75, s32[1024]{0:T(1024)S(1)} %dynamic_slice.29, s32[1024]{0:T(1024)S(1)} %get-tuple-element.164, ...), kind=kOutput, calls=%fused_computation.5.clone.1 | convolution fusion | flops 9669966848 | bytes 6312964 | tf_op jit(solution)/shard_map/while/body/eval_jaxpr/dot_general | solution.py:12
  423.5 0.6 reduce.25
  424.3 0.6 reduce.26
  425.0 12.4 %fusion.26 = f32[1024]{0:T(1024)S(1)} fusion(f32[1024,768]{1,0:T(8,128)S(1)} %get-tuple-element.200, f32[8192,768]{1,0:T(8,128)} %get-tuple-element.199, s32[]{:T(128)S(6)} %select_n.38, s32[1024]{0:T(1024)S(1)} %lt.62, s32[1024]{0:T(1024)S(1)} %eq.75, s32[1024]{0:T(1024)S(1)} %dynamic_slice.29, s32[1024]{0:T(1024)S(1)} %get-tuple-element.164, ...), kind=kOutput, calls=%fused_computation.5.clone.1 | convolution fusion | flops 9669966848 | bytes 6312964 | tf_op jit(solution)/shard_map/while/body/eval_jaxpr/dot_general | solution.py:12
  437.5 0.7 all_to_all.14
  438.1 7.1 %all-to-all-start.2 = ((f32[16,1,64]{2,1,0:T(1,128)}), f32[16,1,64]{2,1,0:T(1,128)S(1)}, u32[]{:S(2)}, u32[]{:S(2)}) async-start(f32[16,1,64]{2,1,0:T(1,128)} %all_to_all.14), calls=%async_computation.2 | async-start | bytes 16384 | tf_op jit(solution)/shard_map/all_to_all | solution.py:76
  445.3 7.0 %all-to-all-done.2 = f32[16,1,64]{2,1,0:T(1,128)S(1)} async-done(((f32[16,1,64]{2,1,0:T(1,128)}), f32[16,1,64]{2,1,0:T(1,128)S(1)}, u32[]{:S(2)}, u32[]{:S(2)}) %all-to-all-start.2) | async-done | bytes 4128 | tf_op jit(solution)/shard_map/all_to_all | solution.py:76
  452.7 0.7 reduce.21
  453.5 3.4 gather_fusion
  (77 shorter events, 11.0 us)
Async XLA Ops:
  6.5 305.4 %all-gather.2.cloned.1.call-start = ((), (), s32[]{:S(2)}) async-start(), calls=%async_computation.3 | async-start | bytes 28311552 | tf_op jit(solution)/shard_map/all_gather | solution.py:60
  63.5 248.4 %copy-start = (f32[16,64,768]{2,1,0:T(8,128)S(1)}, f32[16,64,768]{2,1,0:T(8,128)}, u32[]{:S(2)}) copy-start(f32[16,64,768]{2,1,0:T(8,128)} %all_to_all.19) | copy-start | bytes 9437188
  69.7 11.5 %all-to-all-start = ((s32[16,1,128]{2,1,0:T(1,128)}), s32[16,1,128]{2,1,0:T(1,128)S(1)}, u32[]{:S(2)}, u32[]{:S(2)}) async-start(s32[16,1,128]{2,1,0:T(1,128)} %reshape.128), calls=%async_computation | async-start | bytes 16384 | tf_op jit(solution)/shard_map/all_to_all | solution.py:53
  438.1 14.1 %all-to-all-start.2 = ((f32[16,1,64]{2,1,0:T(1,128)}), f32[16,1,64]{2,1,0:T(1,128)S(1)}, u32[]{:S(2)}, u32[]{:S(2)}) async-start(f32[16,1,64]{2,1,0:T(1,128)} %all_to_all.14), calls=%async_computation.2 | async-start | bytes 16384 | tf_op jit(solution)/shard_map/all_to_all | solution.py:76
Sparse Core Ops, SparseCore 0:
  63.6 248.2 all-gather.1
where the time goes:
time: 464 us
  waiting for transfers between devices  194 us (42%)
  matrix products  99.5 us (21%)
  blocking collectives  96.8 us (21%)
  local copies, waits for them, and re-layouts  22 us (5%)
  other arithmetic  20.8 us (4%)
  between operations  13.5 us (3%)
  starting transfers between devices  11.5 us (2%)
  loops' own time  5.46 us (1%)
    all_gather x1, waiting for transfers between devices, on_device(): cols = lax.all_gather(held, 'blk', axis=0, tiled=True)  180 us
    dot_general x8, matrix products, inner_tile(): lax.dot_general(rows, cols, (((1,), (1,)), ((), ())), precision=lax.Preci...  99.5 us
    all_to_all x1, blocking collectives, on_device(): lax.all_to_all(sending.reshape(groups, capacity, width), 'group', split_a...  47.7 us
    all_gather x1, blocking collectives, on_device(): col_cl = lax.all_gather(held_cl, 'blk', axis=0, tiled=True)  24.6 us
    all_gather x1, blocking collectives, on_device(): col_ix = lax.all_gather(held_ix, 'blk', axis=0, tiled=True)  24.4 us
    while x16, other arithmetic  10.4 us
  transfers between devices with their start and end apart: 3, of which 3 were waited for; matrix products, arithmetic and copies ran while one was open for 2% of the time, Pallas kernels for 0%

commit v1 on v0

v1 whole, which is shorter than its diff:
```python
import functools

import jax
import jax.numpy as jnp
from jax import lax
from jax.experimental import pallas as pl
from jax.experimental.pallas import tpu as pltpu
from jax.sharding import Mesh, PartitionSpec as P

EPS = 1e-06
EMPTY = 1e9
TILE = 256
NT = (((1,), (1,)), ((), ()))
VMEM = pl.BlockSpec(memory_space=pltpu.VMEM)
PARAMS = pltpu.CompilerParams(vmem_limit_bytes=48 * 1024 * 1024)


def split(values):
    high = values.astype(jnp.bfloat16)
    low = (values - high.astype(jnp.float32)).astype(jnp.bfloat16)
    return high, low


def dot_f32(a, b, dims):
    return lax.dot_general(a, b, dims, preferred_element_type=jnp.float32)


def place_kernel(emb_ref, cl_ref, ix_ref, send_ref, rank_ref):
    chips, length, lanes = send_ref.shape
    count, width = emb_ref.shape
    slots = 16
    cl = cl_ref[...]
    ix = ix_ref[...]
    along = jnp.broadcast_to(cl.astype(jnp.float32), (count, count))
    down = along.T
    before = lax.broadcasted_iota(jnp.int32, (count, count), 0) < lax.broadcasted_iota(
        jnp.int32, (count, count), 1
    )
    rank = jnp.sum(
        jnp.where((along == down) & before, 1.0, 0.0), axis=0, keepdims=True
    ).astype(jnp.int32)
    rank_ref[...] = rank
    target = cl * slots + rank
    x = emb_ref[...]
    unit = x * lax.rsqrt(jnp.sum(x * x, axis=1, keepdims=True) + EPS)
    high, low = split(unit)
    mm = (((1,), (0,)), ((), ()))
    rows = chips * slots
    block = 256
    for r in range(0, rows, block):
        place = (
            lax.broadcasted_iota(jnp.int32, (block, count), 0) + r == target
        ).astype(jnp.float32).astype(jnp.bfloat16)
        moved = dot_f32(place, high, mm) + dot_f32(place, low, mm)
        c0, c1 = r // slots, (r + block) // slots
        for k in range(width // lanes):
            send_ref[c0:c1, k * slots : (k + 1) * slots, :] = moved[
                :, k * lanes : (k + 1) * lanes
            ].reshape(c1 - c0, slots, lanes)
    owner = (lax.broadcasted_iota(jnp.int32, (chips, count), 0) == cl).astype(
        jnp.float32
    ).astype(jnp.bfloat16)
    at_rank = lax.broadcasted_iota(jnp.int32, (lanes, count), 0) == rank
    tag = ix + 1
    tag_high = jnp.where(at_rank, (tag // 256).astype(jnp.float32), 0.0).astype(jnp.bfloat16)
    tag_low = jnp.where(at_rank, (tag % 256).astype(jnp.float32), 0.0).astype(jnp.bfloat16)
    tags = 256.0 * dot_f32(owner, tag_high, NT) + dot_f32(owner, tag_low, NT)
    send_ref[:, length - 8 :, :] = jnp.broadcast_to(tags[:, None, :], (chips, 8, lanes))


def unpack(held_ref, high_ref, low_ref):
    chips, length, lanes = held_ref.shape
    slots = 16
    rows = chips * slots
    for k in range((length - 8) // slots):
        part = held_ref[:, k * slots : (k + 1) * slots, :].reshape(rows, lanes)
        high, low = split(part)
        high_ref[:, k * lanes : (k + 1) * lanes] = high
        low_ref[:, k * lanes : (k + 1) * lanes] = low
    tags = held_ref[:, length - 8 : length - 7, :]
    spread = jnp.broadcast_to(tags, (chips, slots, lanes)).reshape(rows, lanes)
    lane = lax.broadcasted_iota(jnp.int32, (rows, lanes), 1)
    row = lax.broadcasted_iota(jnp.int32, (rows, lanes), 0)
    down = jnp.sum(jnp.where(lane == row % slots, spread, 0.0), axis=1, keepdims=True)
    down = jnp.where(down == 0.0, EMPTY, down)
    down = jnp.broadcast_to(down, (rows, lanes))
    return down, down.T[:1, :]


def products(high_i, low_i, high_j, low_j):
    return dot_f32(high_i, high_j, NT) + (
        dot_f32(high_i, low_j, NT) + dot_f32(low_i, high_j, NT)
    )


def lane_max(masked, lanes):
    best = masked[:, :lanes]
    for at in range(lanes, masked.shape[1], lanes):
        best = jnp.maximum(best, masked[:, at : at + lanes])
    return best


def own_kernel(held_ref, high_ref, low_ref, down_ref, best_ref, across_ref):
    down, along = unpack(held_ref, high_ref, low_ref)
    rows, lanes = down.shape
    down_ref[...] = down
    best_ref[...] = jnp.full((rows, lanes), -1.0, jnp.float32)
    across_ref[...] = jnp.full(across_ref.shape, -1.0, jnp.float32)
    for i in range(0, rows, TILE):
        si = slice(i, i + TILE)
        high_i, low_i = high_ref[si, :], low_ref[si, :]
        row_ix = down[si, :1]
        best = best_ref[si, :]
        for j in range(i, rows, TILE):
            sj = slice(j, j + TILE)
            sims = products(high_i, low_i, high_ref[sj, :], low_ref[sj, :])
            col_ix = along[:, sj]
            best = jnp.maximum(best, lane_max(jnp.where(col_ix < row_ix, sims, -1.0), lanes))
            if j > i:
                across_ref[:, sj] = jnp.maximum(
                    across_ref[:, sj],
                    jnp.max(jnp.where(row_ix < col_ix, sims, -1.0), axis=0, keepdims=True),
                )
        best_ref[si, :] = best


def other_kernel(held_ref, high_ref, low_ref, down_ref, best_ref, across_ref, out_ref, high_o, low_o):
    unused, along = unpack(held_ref, high_o, low_o)
    rows, lanes = down_ref.shape
    slots = 16
    total = jnp.broadcast_to(across_ref[:1, :], (lanes, rows)).T
    for i in range(0, rows, TILE):
        si = slice(i, i + TILE)
        high_i, low_i = high_ref[si, :], low_ref[si, :]
        row_ix = down_ref[si, :1]
        best = jnp.maximum(best_ref[si, :], total[si, :])
        for j in range(0, rows, TILE):
            sj = slice(j, j + TILE)
            sims = products(high_i, low_i, high_o[sj, :], low_o[sj, :])
            best = jnp.maximum(
                best, lane_max(jnp.where(along[:, sj] < row_ix, sims, -1.0), lanes)
            )
        best = jnp.max(best, axis=1, keepdims=True)
        lane = lax.broadcasted_iota(jnp.int32, (TILE, lanes), 1)
        row = lax.broadcasted_iota(jnp.int32, (TILE, lanes), 0)
        picked = jnp.where(lane == row % slots, best, -2.0).reshape(TILE // slots, slots, lanes)
        out_ref[i // slots : (i + TILE) // slots, :] = jnp.max(picked, axis=1)


def pick_kernel(answer_ref, cl_ref, rank_ref, out_ref):
    chips, lanes = answer_ref.shape
    count = cl_ref.shape[1]
    owner = (lax.broadcasted_iota(jnp.int32, (chips, count), 0) == cl_ref[...]).astype(
        jnp.float32
    ).astype(jnp.bfloat16)
    tn = (((0,), (0,)), ((), ()))
    answer = answer_ref[...]
    high, rest = split(answer)
    middle, low = split(answer - high.astype(jnp.float32))
    by_rank = dot_f32(high, owner, tn) + (dot_f32(middle, owner, tn) + dot_f32(low, owner, tn))
    at_rank = lax.broadcasted_iota(jnp.int32, (lanes, count), 0) == rank_ref[...]
    out_ref[...] = jnp.sum(jnp.where(at_rank, by_rank, 0.0), axis=0, keepdims=True)


def on_device(embeddings, clusters, indices):
    count, width = embeddings.shape
    chip_axes = ("y", "x_hi", "x_lo", "z")
    chips, slots, lanes = 64, 16, 128
    rows = chips * slots
    length = slots * width // lanes + 8
    cl = clusters.reshape(1, count)
    ix = indices.reshape(1, count)
    f32 = functools.partial(jax.ShapeDtypeStruct, dtype=jnp.float32)
    bf16 = functools.partial(jax.ShapeDtypeStruct, dtype=jnp.bfloat16)
    sending, rank = pl.pallas_call(
        place_kernel,
        out_shape=(f32((chips, length, lanes)), jax.ShapeDtypeStruct((1, count), jnp.int32)),
        in_specs=[VMEM] * 3,
        out_specs=(VMEM, VMEM),
        compiler_params=PARAMS,
        name="place",
    )(embeddings, cl, ix)
    held = lax.all_to_all(sending, chip_axes, split_axis=0, concat_axis=0, tiled=True)
    other = lax.ppermute(held, "core", [(0, 1), (1, 0)])
    flops = 2 * rows * rows * width * 3
    high, low, down, best, across = pl.pallas_call(
        own_kernel,
        out_shape=(
            bf16((rows, width)),
            bf16((rows, width)),
            f32((rows, lanes)),
            f32((rows, lanes)),
            f32((8, rows)),
        ),
        in_specs=[VMEM],
        out_specs=(VMEM,) * 5,
        compiler_params=PARAMS,
        cost_estimate=pl.CostEstimate(flops=flops, bytes_accessed=8 << 20, transcendentals=0),
        name="own",
    )(held)
    result = pl.pallas_call(
        other_kernel,
        out_shape=f32((chips, lanes)),
        in_specs=[VMEM] * 6,
        out_specs=VMEM,
        scratch_shapes=[
            pltpu.VMEM((rows, width), jnp.bfloat16),
            pltpu.VMEM((rows, width), jnp.bfloat16),
        ],
        compiler_params=PARAMS,
        cost_estimate=pl.CostEstimate(flops=flops, bytes_accessed=8 << 20, transcendentals=0),
        name="other",
    )(other, high, low, down, best, across)
    answer = lax.all_to_all(
        result.reshape(chips, 1, lanes), chip_axes, split_axis=0, concat_axis=0, tiled=True
    ).reshape(chips, lanes)
    out = pl.pallas_call(
        pick_kernel,
        out_shape=f32((1, count)),
        in_specs=[VMEM] * 3,
        out_specs=VMEM,
        compiler_params=PARAMS,
        name="pick",
    )(answer, cl, rank)
    return out.reshape(count)


def solution(mesh):
    fine = Mesh(mesh.devices.reshape(4, 2, 2, 2, 4), ("y", "x_hi", "core", "x_lo", "z"))
    points = ("y", "x_hi", "core", "x_lo", "z")
    return jax.shard_map(
        on_device,
        mesh=fine,
        in_specs=(P(points, None), P(points), P(points)),
        out_specs=P(points),
        check_vma=False,
    )
```

time: 464 us -> 91.6 us (0.20)
  waiting for transfers between devices: 194 us -> 0.34 us
  matrix products: 99.5 us -> 0 us
  blocking collectives: 96.8 us -> 67 us
  other arithmetic: 20.8 us -> 0 us
  local copies, waits for them, and re-layouts: 22 us -> 4.49 us
  Pallas kernels: 0 us -> 15.6 us
  between operations: 13.5 us -> 0.03 us
  starting transfers between devices: 11.5 us -> 2.5 us
  loops' own time: 5.46 us -> 0 us
    all_gather x1 -> x0, waiting for transfers between devices: 180 us -> none  [on_device(): cols = lax.all_gather(held, 'blk', axis=0, tiled=True)]
    dot_general x8 -> x0, matrix products: 99.5 us -> none  [inner_tile(): lax.dot_general(rows, cols, (((1,), (1,)), ((), ())), precision=lax.Preci...]
    all_gather x2 -> x0, blocking collectives: 49 us -> none  [the longest x1 24.6 us: on_device(): col_cl = lax.all_gather(held_cl, 'blk', axis=0, tiled=True)]
    all_to_all x1 -> x2, blocking collectives: 47.7 us -> 67 us  [the longest x1 54.1 us: on_device(): lax.all_to_all(sending, chip_axes, split_axis=0, concat_axis=0, tiled=True)]
    pallas_call x0 -> x4, Pallas kernels: none -> 15.6 us  [the longest x1 7.17 us: on_device(): pl.pallas_call(other_kernel, out_shape=f32((chips, lanes)), in_specs=[VME...]
    all_to_all x2 -> x0, waiting for transfers between devices: 14 us -> none  [the longest x1 7.05 us: on_device(): lax.all_to_all(send_tags, 'group', split_axis=0, concat_axis=0, tiled=True)]
    all_to_all x2 -> x0, starting transfers between devices: 11.5 us -> none  [the longest x1 7.11 us: on_device(): lax.all_to_all(result.reshape(groups, capacity), 'group', split_axis=0, c...]
    while x16 -> x0, other arithmetic: 10.4 us -> none
  transfers between devices with their start and end apart: 3 -> 1, of which waited for: 3 -> 1; matrix products, arithmetic and copies ran while one was open for 2% -> 0% of each run, Pallas kernels for 0% -> 6%
where the time goes in v1:
time: 91.6 us; the launch traced here: 89.9 us
  blocking collectives  67 us (73%)
  Pallas kernels  15.6 us (17%)
  local copies, waits for them, and re-layouts  4.49 us (5%)
  starting transfers between devices  2.5 us (3%)
    all_to_all x1, blocking collectives, on_device(): lax.all_to_all(sending, chip_axes, split_axis=0, concat_axis=0, tiled=True)  54.1 us
    all_to_all x1, blocking collectives, on_device(): lax.all_to_all(result.reshape(chips, 1, lanes), chip_axes, split_axis=0,...  12.8 us
    pallas_call x1, Pallas kernels, on_device(): pl.pallas_call(other_kernel, out_shape=f32((chips, lanes)), in_specs=[VME...  7.17 us
    pallas_call x1, Pallas kernels, on_device(): pl.pallas_call(own_kernel, out_shape=(bf16((rows, width)), bf16((rows, wi...  5.31 us
    unnamed x12, local copies, waits for them, and re-layouts  4.49 us
    ppermute x1, starting transfers between devices, on_device(): other = lax.ppermute(held, 'core', [(0, 1), (1, 0)])  2.5 us
    pallas_call x1, Pallas kernels, on_device(): pl.pallas_call(place_kernel, out_shape=(f32((chips, length, lanes)), jax....  2.24 us
  transfers between devices with their start and end apart: 1, of which 1 were waited for; matrix products, arithmetic and copies ran while one was open for 0% of the time, Pallas kernels for 6%

profile of v1, /device:TPU:1, one launch (start us, length us, event | category | flops | bytes accessed | tf_op | source)
XLA Modules:
  0.0 89.9 jit_solution(3938115933095600959)
XLA Ops:
  0.0 0.0 copy-start
  0.0 1.4 %copy-done = f32[512,768]{1,0:T(8,128)S(1)} copy-done((f32[512,768]{1,0:T(8,128)S(1)}, f32[512,768]{1,0:T(8,128)}, u32[]{:S(2)}) %copy-start) | copy-done | bytes 1572888
  1.4 0.0 copy-start.1
  1.4 0.7 copy-done.1
  2.1 0.0 copy-start.3
  2.1 0.7 copy-done.3
  2.8 2.2 %place.1 = (f32[64,104,128]{2,1,0:T(8,128)S(1)}, s32[1,512]{1,0:T(1,128)S(1)}) custom-call(f32[512,768]{1,0:T(8,128)S(1)} %copy-done, s32[1,512]{1,0:T(1,128)S(1)} %bitcast.9, s32[1,512]{1,0:T(1,128)S(1)} %bitcast.11), custom_call_target="tpu_custom_call" | custom-call | tf_op jit(solution)/shard_map/place/pallas_call | solution.py:175
  5.0 54.1 %all_to_all.10.held_ref = f32[64,104,128]{2,1,0:T(8,128)S(1)} all-to-all(f32[64,104,128]{2,1,0:T(8,128)S(1)} %get-tuple-element.12), channel_id=1, replica_groups=mesh['y'=4,'x_hi'=2,'core'=2,'x_lo'=2,'z'=4] {'y','x_hi','x_lo','z'}, dimensions={0} | all-to-all | bytes 6815744 | tf_op jit(solution)/shard_map/all_to_all | solution.py:183
  59.1 0.0 copy-start.4
  59.1 2.5 %collective-permute-start = (f32[64,104,128]{2,1,0:T(8,128)S(1)}, f32[64,104,128]{2,1,0:T(8,128)S(1)}, u32[]{:S(2)}, u32[]{:S(2)}) collective-permute-start(f32[64,104,128]{2,1,0:T(8,128)S(1)} %all_to_all.10.held_ref), channel_id=1, source_target_pairs={{0,8},{8,0},{1,9},{9,1},{2,10},{10,2},{3,11},{11,3},{4,12},{12,4},... | collective-permute-start | bytes 10223624 | tf_op jit(solution)/shard_map/ppermute | solution.py:184
  61.6 0.0 copy-done.4
  61.7 5.3 %own.1 = (bf16[1024,768]{1,0:T(8,128)(2,1)S(1)}, bf16[1024,768]{1,0:T(8,128)(2,1)S(1)}, f32[1024,128]{1,0:T(8,128)S(1)}, f32[1024,128]{1,0:T(8,128)S(1)}, f32[8,1024]{1,0:T(8,128)S(1)}) custom-call(f32[64,104,128]{2,1,0:T(8,128)} %copy-done.4), custom_call_target="tpu_custom_call" | custom-call | flops 4831838208 | bytes 8388608 | tf_op jit(solution)/shard_map/own/pallas_call | solution.py:186
  67.0 0.3 collective-permute-done.held_ref
  67.3 0.0 copy-start.5
  67.3 1.7 %copy-done.5 = f32[64,104,128]{2,1,0:T(8,128)} copy-done((f32[64,104,128]{2,1,0:T(8,128)}, f32[64,104,128]{2,1,0:T(8,128)S(1)}, u32[]{:S(2)}) %copy-start.5) | copy-done | bytes 3407896
  69.0 0.0 copy-start.2
  69.0 7.2 %other.1 = f32[64,128]{1,0:T(8,128)S(1)} custom-call(f32[64,104,128]{2,1,0:T(8,128)} %copy-done.5, bf16[1024,768]{1,0:T(8,128)(2,1)S(1)} %get-tuple-element.13.high_ref, bf16[1024,768]{1,0:T(8,128)(2,1)S(1)} %get-tuple-element.14.low_ref, f32[1024,128]{1,0:T(8,128)S(1)} %get-tuple-element.15.down_ref, f32[1024,128]{1,0:T(8,128)S(1)} %get-tuple-element.16.best_ref, ...), custom_call_target="tpu_custom_call" | custom-call | flops 4831838208 | bytes 8388608 | tf_op jit(solution)/shard_map/other/pallas_call | solution.py:201
  76.2 12.8 %all_to_all.11 = f32[64,1,128]{2,1,0:T(1,128)S(1)} all-to-all(f32[64,1,128]{2,1,0:T(1,128)S(1)} %bitcast.8), channel_id=1, replica_groups=mesh['y'=4,'x_hi'=2,'core'=2,'x_lo'=2,'z'=4] {'y','x_hi','x_lo','z'}, dimensions={0} | all-to-all | bytes 65536 | tf_op jit(solution)/shard_map/all_to_all | solution.py:214
  89.0 0.0 copy-done.2
  89.0 0.9 pick.1
Async XLA Ops:
  0.0 1.4 %copy-start = (f32[512,768]{1,0:T(8,128)S(1)}, f32[512,768]{1,0:T(8,128)}, u32[]{:S(2)}) copy-start(f32[512,768]{1,0:T(8,128)} %emb_ref.1) | copy-start | bytes 4718596
  1.4 0.7 copy-start.1
  2.1 0.7 copy-start.3
  59.1 2.5 %copy-start.4 = (f32[64,104,128]{2,1,0:T(8,128)}, f32[64,104,128]{2,1,0:T(8,128)S(1)}, u32[]{:S(2)}) copy-start(f32[64,104,128]{2,1,0:T(8,128)S(1)} %all_to_all.10.held_ref) | copy-start | bytes 10223620
  59.1 8.2 %collective-permute-start = (f32[64,104,128]{2,1,0:T(8,128)S(1)}, f32[64,104,128]{2,1,0:T(8,128)S(1)}, u32[]{:S(2)}, u32[]{:S(2)}) collective-permute-start(f32[64,104,128]{2,1,0:T(8,128)S(1)} %all_to_all.10.held_ref), channel_id=1, source_target_pairs={{0,8},{8,0},{1,9},{9,1},{2,10},{10,2},{3,11},{11,3},{4,12},{12,4},... | collective-permute-start | bytes 10223624 | tf_op jit(solution)/shard_map/ppermute | solution.py:184
  67.3 1.7 %copy-start.5 = (f32[64,104,128]{2,1,0:T(8,128)}, f32[64,104,128]{2,1,0:T(8,128)S(1)}, u32[]{:S(2)}) copy-start(f32[64,104,128]{2,1,0:T(8,128)S(1)} %collective-permute-done.held_ref) | copy-start | bytes 10223620
  69.0 20.0 %copy-start.2 = (s32[512]{0:T(512)S(1)}, s32[512]{0:T(512)}, u32[]{:S(2)}) copy-start(s32[512]{0:T(512)} %param.4) | copy-start | bytes 6148

commit v2 on v1

v2 whole, which is shorter than its diff:
```python
import functools

import jax
import jax.numpy as jnp
from jax import lax
from jax.experimental import pallas as pl
from jax.experimental.pallas import tpu as pltpu
from jax.sharding import Mesh, PartitionSpec as P

EPS = 1e-06
EMPTY = 1e9
TILE = 256
NT = (((1,), (1,)), ((), ()))
VMEM = pl.BlockSpec(memory_space=pltpu.VMEM)
PARAMS = pltpu.CompilerParams(vmem_limit_bytes=20 * 1024 * 1024)


def split(values):
    high = values.astype(jnp.bfloat16)
    low = (values - high.astype(jnp.float32)).astype(jnp.bfloat16)
    return high, low


def dot_f32(a, b, dims):
    return lax.dot_general(a, b, dims, preferred_element_type=jnp.float32)


def place_kernel(emb_hbm, cl_hbm, ix_hbm, send_ref, rank_ref, emb, cl_ref, ix_ref, emb_sem, cl_sem, ix_sem):
    count, width = emb.shape
    slots, lanes, turn, chips = 16, 128, 8, 64
    parts = 4
    step = count // parts
    copies = [
        pltpu.make_async_copy(
            emb_hbm.at[pl.ds(p * step, step)], emb.at[pl.ds(p * step, step)], emb_sem.at[p]
        )
        for p in range(parts)
    ]
    cl_copy = pltpu.make_async_copy(cl_hbm, cl_ref, cl_sem)
    ix_copy = pltpu.make_async_copy(ix_hbm, ix_ref, ix_sem)
    cl_copy.start()
    ix_copy.start()
    for copy in copies:
        copy.start()
    cl_copy.wait()
    ix_copy.wait()
    cl = cl_ref[...]
    ix = ix_ref[...]
    along = jnp.broadcast_to(cl.astype(jnp.float32), (count, count))
    down = along.T
    before = lax.broadcasted_iota(jnp.int32, (count, count), 0) < lax.broadcasted_iota(
        jnp.int32, (count, count), 1
    )
    rank = jnp.sum(
        jnp.where((along == down) & before, 1.0, 0.0), axis=0, keepdims=True
    ).astype(jnp.int32)
    rank_ref[...] = rank
    target = cl * slots + (rank + cl % turn) % slots
    owner = (lax.broadcasted_iota(jnp.int32, (chips, count), 0) == cl).astype(
        jnp.float32
    ).astype(jnp.bfloat16)
    at_rank = lax.broadcasted_iota(jnp.int32, (lanes, count), 0) == rank
    tag = ix + 1
    tag_high = jnp.where(at_rank, (tag // 256).astype(jnp.float32), 0.0).astype(jnp.bfloat16)
    tag_low = jnp.where(at_rank, (tag % 256).astype(jnp.float32), 0.0).astype(jnp.bfloat16)
    tags = 256.0 * dot_f32(owner, tag_high, NT) + dot_f32(owner, tag_low, NT)
    highs, lows = [], []
    for p in range(parts):
        copies[p].wait()
        x = emb[p * step : (p + 1) * step, :]
        unit = x * lax.rsqrt(jnp.sum(x * x, axis=1, keepdims=True) + EPS)
        high, low = split(unit)
        highs.append(high)
        lows.append(low)
    high = jnp.concatenate(highs, axis=0)
    low = jnp.concatenate(lows, axis=0)
    mm = (((1,), (0,)), ((), ()))
    chunks = width // lanes
    sub = lax.broadcasted_iota(jnp.int32, (8, lanes), 0)
    block = 2 * turn * slots
    for r in range(0, chips * slots, block):
        place = (
            lax.broadcasted_iota(jnp.int32, (block, count), 0) + r == target
        ).astype(jnp.float32).astype(jnp.bfloat16)
        moved = dot_f32(place, high, mm) + dot_f32(place, low, mm)
        for g in range(2):
            base = (r // slots + g * turn) * (chunks * slots + 1)

            def head(a, k):
                at = (g * turn + a) * slots
                return moved[at : at + 8, k * lanes : (k + 1) * lanes]

            def tag_of(a):
                at = r // slots + g * turn + a
                return jnp.broadcast_to(tags[at : at + 1, :], (8, lanes))

            for a in range(turn):
                for k in range(chunks):
                    tile = head(a, k)
                    if k > 0 and a > 0:
                        tile = jnp.where(sub < a, head(a, k - 1), tile)
                    elif k == 0 and a > 0:
                        tile = jnp.where(sub == a - 1, tag_of(a - 1), tile)
                        if a > 1:
                            tile = jnp.where(sub < a - 1, head(a - 1, chunks - 1), tile)
                    at = base + 8 * (12 * a + 2 * k)
                    send_ref[at : at + 8, :] = tile
                    whole = (g * turn + a) * slots + 8
                    send_ref[at + 8 : at + 16, :] = moved[
                        whole : whole + 8, k * lanes : (k + 1) * lanes
                    ]
            at = base + 8 * 12 * turn
            send_ref[at : at + 8, :] = jnp.where(
                sub == turn - 1, tag_of(turn - 1), head(turn - 1, chunks - 1)
            )


def slot_of(rows, lanes):
    row = lax.broadcasted_iota(jnp.int32, (rows, lanes), 0)
    return (row % 16 + 16 - (row // 16) % 8) % 16


def unpack(held_ref, first, chips, high_ref, low_ref, spread_ref):
    slots, lanes, turn = 16, 128, 8
    chunks = high_ref.shape[1] // lanes
    sub = lax.broadcasted_iota(jnp.int32, (8, lanes), 0)
    for s in range(first, first + chips):
        a = s % turn
        base = 97 * (s - a)

        def tile(t):
            at = base + 8 * t
            return held_ref[at : at + 8, :]

        for k in range(chunks):
            t = 12 * a + 2 * k
            top = tile(t)
            if a > 0:
                top = jnp.where(sub < a, tile(t + 2), top)
            high, low = split(jnp.concatenate([top, tile(t + 1)], axis=0))
            high_ref[s * slots : (s + 1) * slots, k * lanes : (k + 1) * lanes] = high
            low_ref[s * slots : (s + 1) * slots, k * lanes : (k + 1) * lanes] = low
        at = base + 97 * a + 96
        spread_ref[s * slots : (s + 1) * slots, :] = jnp.broadcast_to(
            held_ref[at : at + 1, :], (slots, lanes)
        )


def tags_of(spread, slot):
    lanes = spread.shape[1]
    lane = lax.broadcasted_iota(jnp.int32, spread.shape, 1)
    down = jnp.sum(jnp.where(lane == slot, spread, 0.0), axis=1, keepdims=True)
    down = jnp.where(down == 0.0, EMPTY, down)
    return jnp.broadcast_to(down, spread.shape)


def products(high_i, low_i, high_j, low_j):
    return dot_f32(high_i, high_j, NT) + (
        dot_f32(high_i, low_j, NT) + dot_f32(low_i, high_j, NT)
    )


def own_kernel(held_ref, high_ref, low_ref, down_ref, best_ref, across_ref, spread_ref):
    rows, lanes = down_ref.shape
    slot = slot_of(TILE, lanes)
    best_ref[...] = jnp.full((rows, lanes), -1.0, jnp.float32)
    for j in range(0, rows, TILE):
        sj = slice(j, j + TILE)
        unpack(held_ref, j // 16, TILE // 16, high_ref, low_ref, spread_ref)
        down_j = tags_of(spread_ref[sj, :], slot)
        down_ref[sj, :] = down_j
        along = jnp.concatenate(
            [down_j[c : c + lanes, :].T[:1, :] for c in range(0, TILE, lanes)], axis=1
        )
        end = j + TILE
        sims = products(high_ref[:end, :], low_ref[:end, :], high_ref[sj, :], low_ref[sj, :])
        down = down_ref[:end, :]
        best = best_ref[:end, :]
        for c in range(0, TILE, lanes):
            col_ix = along[:, c : c + lanes]
            part = sims[:, c : c + lanes]
            best = jnp.maximum(best, jnp.where(col_ix < down, part, -1.0))
            over = jnp.full((1, lanes), -1.0, jnp.float32)
            if j > 0:
                over = jnp.max(
                    jnp.where(down[:j] < col_ix, part[:j], -1.0), axis=0, keepdims=True
                )
            across_ref[:, j + c : j + c + lanes] = jnp.broadcast_to(over, (8, lanes))
        best_ref[:end, :] = best


def other_kernel(
    held_ref, high_ref, low_ref, down_ref, best_ref, across_ref, out_ref, high_o, low_o, spread_ref, total_ref
):
    rows, lanes = down_ref.shape
    slots = 16
    slot = slot_of(TILE, lanes)
    total_ref[...] = jnp.maximum(
        best_ref[...], jnp.broadcast_to(across_ref[:1, :], (lanes, rows)).T
    )
    for j in range(0, rows, TILE):
        sj = slice(j, j + TILE)
        unpack(held_ref, j // 16, TILE // 16, high_o, low_o, spread_ref)
        down_j = tags_of(spread_ref[sj, :], slot)
        sims = products(high_ref[...], low_ref[...], high_o[sj, :], low_o[sj, :])
        best = total_ref[...]
        for c in range(0, TILE, lanes):
            col_ix = down_j[c : c + lanes, :].T[:1, :]
            best = jnp.maximum(
                best, jnp.where(col_ix < down_ref[...], sims[:, c : c + lanes], -1.0)
            )
        total_ref[...] = best
    lane = lax.broadcasted_iota(jnp.int32, (TILE, lanes), 1)
    for i in range(0, rows, TILE):
        best = jnp.max(total_ref[i : i + TILE, :], axis=1, keepdims=True)
        picked = jnp.where(lane == slot, best, -2.0).reshape(TILE // slots, slots, lanes)
        out_ref[i // slots : (i + TILE) // slots, :] = jnp.max(picked, axis=1)


def pick_kernel(answer_ref, cl_ref, rank_ref, out_ref):
    chips, lanes = answer_ref.shape
    count = cl_ref.shape[1]
    owner = (lax.broadcasted_iota(jnp.int32, (chips, count), 0) == cl_ref[...]).astype(
        jnp.float32
    ).astype(jnp.bfloat16)
    tn = (((0,), (0,)), ((), ()))
    answer = answer_ref[...]
    high, rest = split(answer)
    middle, low = split(answer - high.astype(jnp.float32))
    by_rank = dot_f32(high, owner, tn) + (dot_f32(middle, owner, tn) + dot_f32(low, owner, tn))
    at_rank = lax.broadcasted_iota(jnp.int32, (lanes, count), 0) == rank_ref[...]
    out_ref[...] = jnp.sum(jnp.where(at_rank, by_rank, 0.0), axis=0, keepdims=True)


def on_device(embeddings, clusters, indices):
    count, width = embeddings.shape
    chip_axes = ("y", "x_hi", "x_lo", "z")
    chips, slots, lanes = 64, 16, 128
    rows = chips * slots
    length = slots * width // lanes + 1
    cl = clusters.reshape(1, count)
    ix = indices.reshape(1, count)
    f32 = functools.partial(jax.ShapeDtypeStruct, dtype=jnp.float32)
    bf16 = functools.partial(jax.ShapeDtypeStruct, dtype=jnp.bfloat16)
    dma = pltpu.SemaphoreType.DMA
    sending, rank = pl.pallas_call(
        place_kernel,
        out_shape=(f32((chips * length, lanes)), jax.ShapeDtypeStruct((1, count), jnp.int32)),
        in_specs=[pl.BlockSpec(memory_space=pltpu.HBM)] * 3,
        out_specs=(VMEM, VMEM),
        scratch_shapes=[
            pltpu.VMEM((count, width), jnp.float32),
            pltpu.VMEM((1, count), jnp.int32),
            pltpu.VMEM((1, count), jnp.int32),
            dma((4,)),
            dma,
            dma,
        ],
        compiler_params=PARAMS,
        name="place",
    )(*(pltpu.with_memory_space_constraint(v, pltpu.HBM) for v in (embeddings, cl, ix)))
    held = lax.all_to_all(
        sending.reshape(chips * length, 1, lanes), chip_axes, split_axis=0, concat_axis=0, tiled=True
    )
    other = lax.ppermute(held, "core", [(0, 1), (1, 0)]).reshape(chips * length, lanes)
    held = held.reshape(chips * length, lanes)
    flops = 2 * rows * rows * width * 3
    high, low, down, best, across = pl.pallas_call(
        own_kernel,
        out_shape=(
            bf16((rows, width)),
            bf16((rows, width)),
            f32((rows, lanes)),
            f32((rows, lanes)),
            f32((8, rows)),
        ),
        in_specs=[VMEM],
        out_specs=(VMEM,) * 5,
        scratch_shapes=[pltpu.VMEM((rows, lanes), jnp.float32)],
        compiler_params=PARAMS,
        cost_estimate=pl.CostEstimate(flops=flops, bytes_accessed=8 << 20, transcendentals=0),
        name="own",
    )(held)
    result = pl.pallas_call(
        other_kernel,
        out_shape=f32((chips, lanes)),
        in_specs=[VMEM] * 6,
        out_specs=VMEM,
        scratch_shapes=[
            pltpu.VMEM((rows, width), jnp.bfloat16),
            pltpu.VMEM((rows, width), jnp.bfloat16),
            pltpu.VMEM((rows, lanes), jnp.float32),
            pltpu.VMEM((rows, lanes), jnp.float32),
        ],
        compiler_params=PARAMS,
        cost_estimate=pl.CostEstimate(flops=flops, bytes_accessed=8 << 20, transcendentals=0),
        name="other",
    )(other, high, low, down, best, across)
    answer = lax.all_to_all(
        result.reshape(chips, 1, lanes), chip_axes, split_axis=0, concat_axis=0, tiled=True
    ).reshape(chips, lanes)
    out = pl.pallas_call(
        pick_kernel,
        out_shape=f32((1, count)),
        in_specs=[VMEM] * 3,
        out_specs=VMEM,
        compiler_params=PARAMS,
        name="pick",
    )(answer, cl, rank)
    return out.reshape(count)


def solution(mesh):
    fine = Mesh(mesh.devices.reshape(4, 2, 2, 2, 4), ("y", "x_hi", "core", "x_lo", "z"))
    points = ("y", "x_hi", "core", "x_lo", "z")
    return jax.shard_map(
        on_device,
        mesh=fine,
        in_specs=(P(points, None), P(points), P(points)),
        out_specs=P(points),
        check_vma=False,
    )
```

time: 91.6 us -> 83.2 us (0.908); the launches traced: 89.9 us -> 82.6 us
  local copies, waits for them, and re-layouts: 4.49 us -> 0.01 us
  blocking collectives: 67 us -> 64.6 us
  Pallas kernels: 15.6 us -> 13.7 us
  waiting for transfers between devices: 0.34 us -> 1.93 us
    unnamed x12 -> x2, local copies, waits for them, and re-layouts: 4.49 us -> 0.01 us
    all_to_all x1, blocking collectives: 54.1 us -> 51.8 us  [on_device(): lax.all_to_all(sending.reshape(chips * length, 1, lanes), chip_axes, spli...]
    pallas_call x1, Pallas kernels: 5.31 us -> 3.4 us  [on_device(): pl.pallas_call(own_kernel, out_shape=(bf16((rows, width)), bf16((rows, wi...]
    ppermute x1, waiting for transfers between devices: 0.34 us -> 1.93 us  [on_device(): lax.ppermute(held, 'core', [(0, 1), (1, 0)]).reshape(chips * length, lanes)]
    pallas_call x1, Pallas kernels: 7.17 us -> 5.66 us  [on_device(): pl.pallas_call(other_kernel, out_shape=f32((chips, lanes)), in_specs=[VME...]
    pallas_call x1, Pallas kernels: 2.24 us -> 3.75 us  [on_device(): pl.pallas_call(place_kernel, out_shape=(f32((chips * length, lanes)), jax...]
  transfers between devices with their start and end apart: 1 -> 1, of which waited for: 1 -> 1; matrix products, arithmetic and copies ran while one was open for 0% -> 0% of each run, Pallas kernels for 6% -> 4%
where the time goes in v2:
time: 83.2 us; the launch traced here: 82.6 us
  blocking collectives  64.6 us (78%)
  Pallas kernels  13.7 us (16%)
  starting transfers between devices  2.42 us (3%)
  waiting for transfers between devices  1.93 us (2%)
    all_to_all x1, blocking collectives, on_device(): lax.all_to_all(sending.reshape(chips * length, 1, lanes), chip_axes, spli...  51.8 us
    all_to_all x1, blocking collectives, on_device(): lax.all_to_all(result.reshape(chips, 1, lanes), chip_axes, split_axis=0,...  12.7 us
    pallas_call x1, Pallas kernels, on_device(): pl.pallas_call(other_kernel, out_shape=f32((chips, lanes)), in_specs=[VME...  5.66 us
    pallas_call x1, Pallas kernels, on_device(): pl.pallas_call(place_kernel, out_shape=(f32((chips * length, lanes)), jax...  3.75 us
    pallas_call x1, Pallas kernels, on_device(): pl.pallas_call(own_kernel, out_shape=(bf16((rows, width)), bf16((rows, wi...  3.4 us
    ppermute x1, starting transfers between devices, on_device(): lax.ppermute(held, 'core', [(0, 1), (1, 0)]).reshape(chips * length, lanes)  2.42 us
    ppermute x1, waiting for transfers between devices, on_device(): lax.ppermute(held, 'core', [(0, 1), (1, 0)]).reshape(chips * length, lanes)  1.93 us
  transfers between devices with their start and end apart: 1, of which 1 were waited for; matrix products, arithmetic and copies ran while one was open for 0% of the time, Pallas kernels for 4%

profile of v2, /device:TPU:1, one launch (start us, length us, event | category | flops | bytes accessed | tf_op | source)
XLA Modules:
  0.0 82.6 jit_solution(6729986813936060200)
XLA Ops:
  0.0 3.7 %place.1 = (f32[6208,128]{1,0:T(8,128)S(1)}, s32[1,512]{1,0:T(1,128)S(1)}) custom-call(f32[512,768]{1,0:T(8,128)} %emb_hbm.1, s32[1,512]{1,0:T(1,128)} %bitcast.18, s32[1,512]{1,0:T(1,128)} %bitcast.21), custom_call_target="tpu_custom_call" | custom-call | tf_op jit(solution)/shard_map/place/pallas_call | solution.py:246
  3.8 51.8 %all_to_all.10 = f32[6208,1,128]{2,1,0:T(1,128)S(1)} all-to-all(f32[6208,1,128]{2,1,0:T(1,128)S(1)} %bitcast.15), channel_id=1, replica_groups=mesh['y'=4,'x_hi'=2,'core'=2,'x_lo'=2,'z'=4] {'y','x_hi','x_lo','z'}, dimensions={0} | all-to-all | bytes 6356992 | tf_op jit(solution)/shard_map/all_to_all | solution.py:262
  55.6 2.4 %collective-permute-start = (f32[6208,1,128]{2,0,1:T(8,128)S(1)}, f32[6208,1,128]{2,0,1:T(8,128)S(1)}, u32[]{:S(2)}, u32[]{:S(2)}) collective-permute-start(f32[6208,1,128]{2,0,1:T(8,128)S(1)} %bitcast.13), channel_id=1, source_target_pairs={{0,8},{8,0},{1,9},{9,1},{2,10},{10,2},{3,11},{11,3},{4,12},{12,4},... | collective-permute-start | bytes 9535496 | tf_op jit(solution)/shard_map/ppermute | solution.py:265
  58.0 3.4 %own.1 = (bf16[1024,768]{1,0:T(8,128)(2,1)S(1)}, bf16[1024,768]{1,0:T(8,128)(2,1)S(1)}, f32[1024,128]{1,0:T(8,128)S(1)}, f32[1024,128]{1,0:T(8,128)S(1)}, f32[8,1024]{1,0:T(8,128)S(1)}) custom-call(f32[6208,128]{1,0:T(8,128)S(1)} %bitcast.14), custom_call_target="tpu_custom_call" | custom-call | flops 4831838208 | bytes 8388608 | tf_op jit(solution)/shard_map/own/pallas_call | solution.py:268
  61.4 1.9 %collective-permute-done = f32[6208,1,128]{2,0,1:T(8,128)S(1)} collective-permute-done((f32[6208,1,128]{2,0,1:T(8,128)S(1)}, f32[6208,1,128]{2,0,1:T(8,128)S(1)}, u32[]{:S(2)}, u32[]{:S(2)}) %collective-permute-start) | collective-permute-done | bytes 3178528 | tf_op jit(solution)/shard_map/ppermute | solution.py:265
  63.3 0.0 copy-start
  63.3 5.7 %other.1 = f32[64,128]{1,0:T(8,128)S(1)} custom-call(f32[6208,128]{1,0:T(8,128)S(1)} %bitcast.20, bf16[1024,768]{1,0:T(8,128)(2,1)S(1)} %get-tuple-element.13.high_ref, bf16[1024,768]{1,0:T(8,128)(2,1)S(1)} %get-tuple-element.14.low_ref, f32[1024,128]{1,0:T(8,128)S(1)} %get-tuple-element.15.down_ref, f32[1024,128]{1,0:T(8,128)S(1)} %get-tuple-element.16.best_ref, ...), custom_call_target="tpu_custom_call" | custom-call | flops 4831838208 | bytes 8388608 | tf_op jit(solution)/shard_map/other/pallas_call | solution.py:284
  69.0 12.7 %all_to_all.11 = f32[64,1,128]{2,1,0:T(1,128)S(1)} all-to-all(f32[64,1,128]{2,1,0:T(1,128)S(1)} %bitcast.17), channel_id=1, replica_groups=mesh['y'=4,'x_hi'=2,'core'=2,'x_lo'=2,'z'=4] {'y','x_hi','x_lo','z'}, dimensions={0} | all-to-all | bytes 65536 | tf_op jit(solution)/shard_map/all_to_all | solution.py:299
  81.7 0.0 copy-done
  81.7 0.9 %pick.1 = f32[1,512]{1,0:T(1,128)} custom-call(f32[64,128]{1,0:T(8,128)S(1)} %bitcast.16, s32[1,512]{1,0:T(1,128)S(1)} %bitcast.19, s32[1,512]{1,0:T(1,128)S(1)} %get-tuple-element.18.rank_ref), custom_call_target="tpu_custom_call" | custom-call | tf_op jit(solution)/shard_map/pick/pallas_call | solution.py:302
Async XLA Ops:
  55.6 7.8 %collective-permute-start = (f32[6208,1,128]{2,0,1:T(8,128)S(1)}, f32[6208,1,128]{2,0,1:T(8,128)S(1)}, u32[]{:S(2)}, u32[]{:S(2)}) collective-permute-start(f32[6208,1,128]{2,0,1:T(8,128)S(1)} %bitcast.13), channel_id=1, source_target_pairs={{0,8},{8,0},{1,9},{9,1},{2,10},{10,2},{3,11},{11,3},{4,12},{12,4},... | collective-permute-start | bytes 9535496 | tf_op jit(solution)/shard_map/ppermute | solution.py:265
  63.3 18.4 %copy-start = (s32[512]{0:T(512)S(1)}, s32[512]{0:T(512)}, u32[]{:S(2)}) copy-start(s32[512]{0:T(512)} %param.4) | copy-start | bytes 6148

commit v3 on v2

--- a/solution.py
+++ b/solution.py
@@ -10,6 +10,7 @@
 EPS = 1e-06
 EMPTY = 1e9
 TILE = 256
+POINTS = ("y", "x_hi", "core", "x_lo", "z")
 NT = (((1,), (1,)), ((), ()))
 VMEM = pl.BlockSpec(memory_space=pltpu.VMEM)
 PARAMS = pltpu.CompilerParams(vmem_limit_bytes=20 * 1024 * 1024)
@@ -189,42 +190,67 @@
         best_ref[:end, :] = best
 
 
+def by_slot(best, slot):
+    slots = 16
+    rows, lanes = best.shape
+    lane = lax.broadcasted_iota(jnp.int32, (rows, lanes), 1)
+    picked = jnp.where(lane == slot, best, -2.0).reshape(rows // slots, slots, lanes)
+    return jnp.max(picked, axis=1)
+
+
 def other_kernel(
     held_ref, high_ref, low_ref, down_ref, best_ref, across_ref, out_ref, high_o, low_o, spread_ref, total_ref
 ):
     rows, lanes = down_ref.shape
-    slots = 16
+    half = rows // 2
     slot = slot_of(TILE, lanes)
+    core = lax.axis_index("core")
     total_ref[...] = jnp.maximum(
         best_ref[...], jnp.broadcast_to(across_ref[:1, :], (lanes, rows)).T
     )
+    over = []
     for j in range(0, rows, TILE):
         sj = slice(j, j + TILE)
         unpack(held_ref, j // 16, TILE // 16, high_o, low_o, spread_ref)
         down_j = tags_of(spread_ref[sj, :], slot)
-        sims = products(high_ref[...], low_ref[...], high_o[sj, :], low_o[sj, :])
-        best = total_ref[...]
+        start = core * half if j < half else (1 - core) * half
+        mine = pl.ds(pl.multiple_of(start, half), half)
+        sims = products(high_ref[mine, :], low_ref[mine, :], high_o[sj, :], low_o[sj, :])
+        down = down_ref[mine, :]
+        best = total_ref[mine, :]
         for c in range(0, TILE, lanes):
             col_ix = down_j[c : c + lanes, :].T[:1, :]
-            best = jnp.maximum(
-                best, jnp.where(col_ix < down_ref[...], sims[:, c : c + lanes], -1.0)
-            )
-        total_ref[...] = best
-    lane = lax.broadcasted_iota(jnp.int32, (TILE, lanes), 1)
+            part = sims[:, c : c + lanes]
+            best = jnp.maximum(best, jnp.where(col_ix < down, part, -1.0))
+            over.append(jnp.max(jnp.where(down < col_ix, part, -1.0), axis=0, keepdims=True))
+        total_ref[mine, :] = best
+    per_chip, per_tile = 16, TILE // 16
     for i in range(0, rows, TILE):
-        best = jnp.max(total_ref[i : i + TILE, :], axis=1, keepdims=True)
-        picked = jnp.where(lane == slot, best, -2.0).reshape(TILE // slots, slots, lanes)
-        out_ref[i // slots : (i + TILE) // slots, :] = jnp.max(picked, axis=1)
+        own = by_slot(jnp.max(total_ref[i : i + TILE, :], axis=1, keepdims=True) + jnp.zeros((TILE, lanes), jnp.float32), slot)
+        cols = jnp.concatenate(
+            [
+                jnp.broadcast_to(over[(i + c) // lanes], (lanes, lanes)).T
+                for c in range(0, TILE, lanes)
+            ],
+            axis=0,
+        )
+        other = by_slot(cols, slot)
+        for g in range(0, per_tile, 8):
+            at = 2 * (i // per_chip + g)
+            own_g, other_g = own[g : g + 8, :], other[g : g + 8, :]
+            out_ref[at : at + 8, :] = jnp.where(core == 0, own_g, other_g)
+            out_ref[at + 8 : at + 16, :] = jnp.where(core == 0, other_g, own_g)
 
 
 def pick_kernel(answer_ref, cl_ref, rank_ref, out_ref):
-    chips, lanes = answer_ref.shape
+    lanes = answer_ref.shape[1]
+    chips = answer_ref.shape[0] // 2
     count = cl_ref.shape[1]
     owner = (lax.broadcasted_iota(jnp.int32, (chips, count), 0) == cl_ref[...]).astype(
         jnp.float32
     ).astype(jnp.bfloat16)
     tn = (((0,), (0,)), ((), ()))
-    answer = answer_ref[...]
+    answer = jnp.max(answer_ref[...].reshape(chips // 8, 2, 8, lanes), axis=1).reshape(chips, lanes)
     high, rest = split(answer)
     middle, low = split(answer - high.astype(jnp.float32))
     by_rank = dot_f32(high, owner, tn) + (dot_f32(middle, owner, tn) + dot_f32(low, owner, tn))
@@ -283,7 +309,7 @@
     )(held)
     result = pl.pallas_call(
         other_kernel,
-        out_shape=f32((chips, lanes)),
+        out_shape=f32((2 * chips, lanes)),
         in_specs=[VMEM] * 6,
         out_specs=VMEM,
         scratch_shapes=[
@@ -297,8 +323,8 @@
         name="other",
     )(other, high, low, down, best, across)
     answer = lax.all_to_all(
-        result.reshape(chips, 1, lanes), chip_axes, split_axis=0, concat_axis=0, tiled=True
-    ).reshape(chips, lanes)
+        result.reshape(2 * chips, 1, lanes), POINTS, split_axis=0, concat_axis=0, tiled=True
+    ).reshape(2 * chips, lanes)
     out = pl.pallas_call(
         pick_kernel,
         out_shape=f32((1, count)),
@@ -311,12 +337,11 @@
 
 
 def solution(mesh):
-    fine = Mesh(mesh.devices.reshape(4, 2, 2, 2, 4), ("y", "x_hi", "core", "x_lo", "z"))
-    points = ("y", "x_hi", "core", "x_lo", "z")
+    fine = Mesh(mesh.devices.reshape(4, 2, 2, 2, 4), POINTS)
     return jax.shard_map(
         on_device,
         mesh=fine,
-        in_specs=(P(points, None), P(points), P(points)),
-        out_specs=P(points),
+        in_specs=(P(POINTS, None), P(POINTS), P(POINTS)),
+        out_specs=P(POINTS),
         check_vma=False,
     )

time: 83.2 us -> 81.2 us (0.976)
  Pallas kernels: 13.7 us -> 11.4 us
    pallas_call x1, Pallas kernels: 5.66 us -> 3.4 us  [on_device(): pl.pallas_call(other_kernel, out_shape=f32((2 * chips, lanes)), in_specs=...]
where the time goes in v3:
time: 81.2 us; the launch traced here: 81 us
  blocking collectives  65.2 us (80%)
  Pallas kernels  11.4 us (14%)
  starting transfers between devices  2.42 us (3%)
  waiting for transfers between devices  1.93 us (2%)
    all_to_all x1, blocking collectives, on_device(): lax.all_to_all(sending.reshape(chips * length, 1, lanes), chip_axes, spli...  51.8 us
    all_to_all x1, blocking collectives, on_device(): lax.all_to_all(result.reshape(2 * chips, 1, lanes), POINTS, split_axis=0,...  13.4 us
    pallas_call x1, Pallas kernels, on_device(): pl.pallas_call(place_kernel, out_shape=(f32((chips * length, lanes)), jax...  3.75 us
    pallas_call x1, Pallas kernels, on_device(): pl.pallas_call(other_kernel, out_shape=f32((2 * chips, lanes)), in_specs=...  3.4 us
    pallas_call x1, Pallas kernels, on_device(): pl.pallas_call(own_kernel, out_shape=(bf16((rows, width)), bf16((rows, wi...  3.4 us
    ppermute x1, starting transfers between devices, on_device(): lax.ppermute(held, 'core', [(0, 1), (1, 0)]).reshape(chips * length, lanes)  2.42 us
    ppermute x1, waiting for transfers between devices, on_device(): lax.ppermute(held, 'core', [(0, 1), (1, 0)]).reshape(chips * length, lanes)  1.93 us
  transfers between devices with their start and end apart: 1, of which 1 were waited for; matrix products, arithmetic and copies ran while one was open for 0% of the time, Pallas kernels for 4%

profile of v3, /device:TPU:1, one launch (start us, length us, event | category | flops | bytes accessed | tf_op | source)
XLA Modules:
  0.0 81.0 jit_solution(16725152266924730700)
XLA Ops:
  0.0 3.7 %place.1 = (f32[6208,128]{1,0:T(8,128)S(1)}, s32[1,512]{1,0:T(1,128)S(1)}) custom-call(f32[512,768]{1,0:T(8,128)} %emb_hbm.1, s32[1,512]{1,0:T(1,128)} %bitcast.18, s32[1,512]{1,0:T(1,128)} %bitcast.21), custom_call_target="tpu_custom_call" | custom-call | tf_op jit(solution)/shard_map/place/pallas_call | solution.py:272
  3.8 51.8 %all_to_all.10 = f32[6208,1,128]{2,1,0:T(1,128)S(1)} all-to-all(f32[6208,1,128]{2,1,0:T(1,128)S(1)} %bitcast.15), channel_id=1, replica_groups=mesh['y'=4,'x_hi'=2,'core'=2,'x_lo'=2,'z'=4] {'y','x_hi','x_lo','z'}, dimensions={0} | all-to-all | bytes 6356992 | tf_op jit(solution)/shard_map/all_to_all | solution.py:288
  55.6 2.4 %collective-permute-start = (f32[6208,1,128]{2,0,1:T(8,128)S(1)}, f32[6208,1,128]{2,0,1:T(8,128)S(1)}, u32[]{:S(2)}, u32[]{:S(2)}) collective-permute-start(f32[6208,1,128]{2,0,1:T(8,128)S(1)} %bitcast.13), channel_id=1, source_target_pairs={{0,8},{8,0},{1,9},{9,1},{2,10},{10,2},{3,11},{11,3},{4,12},{12,4},... | collective-permute-start | bytes 9535496 | tf_op jit(solution)/shard_map/ppermute | solution.py:291
  58.0 3.4 %own.1 = (bf16[1024,768]{1,0:T(8,128)(2,1)S(1)}, bf16[1024,768]{1,0:T(8,128)(2,1)S(1)}, f32[1024,128]{1,0:T(8,128)S(1)}, f32[1024,128]{1,0:T(8,128)S(1)}, f32[8,1024]{1,0:T(8,128)S(1)}) custom-call(f32[6208,128]{1,0:T(8,128)S(1)} %bitcast.14), custom_call_target="tpu_custom_call" | custom-call | flops 4831838208 | bytes 8388608 | tf_op jit(solution)/shard_map/own/pallas_call | solution.py:294
  61.4 1.9 %collective-permute-done = f32[6208,1,128]{2,0,1:T(8,128)S(1)} collective-permute-done((f32[6208,1,128]{2,0,1:T(8,128)S(1)}, f32[6208,1,128]{2,0,1:T(8,128)S(1)}, u32[]{:S(2)}, u32[]{:S(2)}) %collective-permute-start) | collective-permute-done | bytes 3178528 | tf_op jit(solution)/shard_map/ppermute | solution.py:291
  63.3 0.0 copy-start
  63.3 3.4 %other.1 = f32[128,128]{1,0:T(8,128)S(1)} custom-call(f32[6208,128]{1,0:T(8,128)S(1)} %bitcast.20, bf16[1024,768]{1,0:T(8,128)(2,1)S(1)} %get-tuple-element.13.high_ref, bf16[1024,768]{1,0:T(8,128)(2,1)S(1)} %get-tuple-element.14.low_ref, f32[1024,128]{1,0:T(8,128)S(1)} %get-tuple-element.15.down_ref, f32[1024,128]{1,0:T(8,128)S(1)} %get-tuple-element.16.best_ref, ...), custom_call_target="tpu_custom_call" | custom-call | flops 4831838208 | bytes 8388608 | tf_op jit(solution)/shard_map/other/pallas_call | solution.py:310
  66.7 13.4 %all_to_all.11 = f32[128,1,128]{2,1,0:T(1,128)S(1)} all-to-all(f32[128,1,128]{2,1,0:T(1,128)S(1)} %bitcast.17), channel_id=1, replica_groups=mesh['y'=4,'x_hi'=2,'core'=2,'x_lo'=2,'z'=4] {'y','x_hi','core','x_lo','z'}, dimensions={0} | all-to-all | bytes 131072 | tf_op jit(solution)/shard_map/all_to_all | solution.py:325
  80.1 0.0 copy-done
  80.2 0.9 %pick.1 = f32[1,512]{1,0:T(1,128)} custom-call(f32[128,128]{1,0:T(8,128)S(1)} %bitcast.16, s32[1,512]{1,0:T(1,128)S(1)} %bitcast.19, s32[1,512]{1,0:T(1,128)S(1)} %get-tuple-element.18.rank_ref), custom_call_target="tpu_custom_call" | custom-call | tf_op jit(solution)/shard_map/pick/pallas_call | solution.py:328
Async XLA Ops:
  55.6 7.8 %collective-permute-start = (f32[6208,1,128]{2,0,1:T(8,128)S(1)}, f32[6208,1,128]{2,0,1:T(8,128)S(1)}, u32[]{:S(2)}, u32[]{:S(2)}) collective-permute-start(f32[6208,1,128]{2,0,1:T(8,128)S(1)} %bitcast.13), channel_id=1, source_target_pairs={{0,8},{8,0},{1,9},{9,1},{2,10},{10,2},{3,11},{11,3},{4,12},{12,4},... | collective-permute-start | bytes 9535496 | tf_op jit(solution)/shard_map/ppermute | solution.py:291
  63.3 16.8 %copy-start = (s32[512]{0:T(512)S(1)}, s32[512]{0:T(512)}, u32[]{:S(2)}) copy-start(s32[512]{0:T(512)} %param.4) | copy-start | bytes 6148

commit v4 on v2

--- a/solution.py
+++ b/solution.py
@@ -10,6 +10,7 @@
 EPS = 1e-06
 EMPTY = 1e9
 TILE = 256
+POINTS = ("y", "x_hi", "core", "x_lo", "z")
 NT = (((1,), (1,)), ((), ()))
 VMEM = pl.BlockSpec(memory_space=pltpu.VMEM)
 PARAMS = pltpu.CompilerParams(vmem_limit_bytes=20 * 1024 * 1024)
@@ -28,7 +29,7 @@
 def place_kernel(emb_hbm, cl_hbm, ix_hbm, send_ref, rank_ref, emb, cl_ref, ix_ref, emb_sem, cl_sem, ix_sem):
     count, width = emb.shape
     slots, lanes, turn, chips = 16, 128, 8, 64
-    parts = 4
+    parts = 2
     step = count // parts
     copies = [
         pltpu.make_async_copy(
@@ -160,71 +161,93 @@
     )
 
 
-def own_kernel(held_ref, high_ref, low_ref, down_ref, best_ref, across_ref, spread_ref):
+def by_slot(best, slot):
+    slots = 16
+    rows, lanes = best.shape
+    lane = lax.broadcasted_iota(jnp.int32, (rows, lanes), 1)
+    picked = jnp.where(lane == slot, best, -2.0).reshape(rows // slots, slots, lanes)
+    return jnp.max(picked, axis=1)
+
+
+def own_kernel(held_ref, high_ref, low_ref, down_ref, best_ref, spread_ref):
     rows, lanes = down_ref.shape
     slot = slot_of(TILE, lanes)
-    best_ref[...] = jnp.full((rows, lanes), -1.0, jnp.float32)
     for j in range(0, rows, TILE):
         sj = slice(j, j + TILE)
         unpack(held_ref, j // 16, TILE // 16, high_ref, low_ref, spread_ref)
         down_j = tags_of(spread_ref[sj, :], slot)
         down_ref[sj, :] = down_j
-        along = jnp.concatenate(
-            [down_j[c : c + lanes, :].T[:1, :] for c in range(0, TILE, lanes)], axis=1
-        )
+        best_ref[sj, :] = jnp.full((TILE, lanes), -1.0, jnp.float32)
         end = j + TILE
         sims = products(high_ref[:end, :], low_ref[:end, :], high_ref[sj, :], low_ref[sj, :])
         down = down_ref[:end, :]
         best = best_ref[:end, :]
+        over = []
         for c in range(0, TILE, lanes):
-            col_ix = along[:, c : c + lanes]
+            col_ix = down_j[c : c + lanes, :].T[:1, :]
             part = sims[:, c : c + lanes]
             best = jnp.maximum(best, jnp.where(col_ix < down, part, -1.0))
-            over = jnp.full((1, lanes), -1.0, jnp.float32)
             if j > 0:
-                over = jnp.max(
+                top = jnp.max(
                     jnp.where(down[:j] < col_ix, part[:j], -1.0), axis=0, keepdims=True
                 )
-            across_ref[:, j + c : j + c + lanes] = jnp.broadcast_to(over, (8, lanes))
-        best_ref[:end, :] = best
+                over.append(jnp.broadcast_to(top, (lanes, lanes)).T)
+        if j > 0:
+            best_ref[:j, :] = best[:j]
+            best_ref[sj, :] = jnp.maximum(best[j:], jnp.concatenate(over, axis=0))
+        else:
+            best_ref[sj, :] = best
 
 
 def other_kernel(
-    held_ref, high_ref, low_ref, down_ref, best_ref, across_ref, out_ref, high_o, low_o, spread_ref, total_ref
+    held_ref, high_ref, low_ref, down_ref, best_ref, out_ref, high_o, low_o, spread_ref, total_ref
 ):
     rows, lanes = down_ref.shape
-    slots = 16
+    half = rows // 2
+    chips = rows // 16
+    per_tile = TILE // 16
     slot = slot_of(TILE, lanes)
-    total_ref[...] = jnp.maximum(
-        best_ref[...], jnp.broadcast_to(across_ref[:1, :], (lanes, rows)).T
-    )
+    core = lax.axis_index("core")
+    mine_at = pl.multiple_of(core * chips, chips)
+    other_at = pl.multiple_of((1 - core) * chips, chips)
     for j in range(0, rows, TILE):
         sj = slice(j, j + TILE)
         unpack(held_ref, j // 16, TILE // 16, high_o, low_o, spread_ref)
         down_j = tags_of(spread_ref[sj, :], slot)
-        sims = products(high_ref[...], low_ref[...], high_o[sj, :], low_o[sj, :])
-        best = total_ref[...]
+        start = core * half if j < half else (1 - core) * half
+        mine = pl.ds(pl.multiple_of(start, half), half)
+        sims = products(high_ref[mine, :], low_ref[mine, :], high_o[sj, :], low_o[sj, :])
+        down = down_ref[mine, :]
+        best = best_ref[mine, :] if j % half == 0 else total_ref[mine, :]
+        over = []
         for c in range(0, TILE, lanes):
             col_ix = down_j[c : c + lanes, :].T[:1, :]
-            best = jnp.maximum(
-                best, jnp.where(col_ix < down_ref[...], sims[:, c : c + lanes], -1.0)
-            )
-        total_ref[...] = best
-    lane = lax.broadcasted_iota(jnp.int32, (TILE, lanes), 1)
-    for i in range(0, rows, TILE):
-        best = jnp.max(total_ref[i : i + TILE, :], axis=1, keepdims=True)
-        picked = jnp.where(lane == slot, best, -2.0).reshape(TILE // slots, slots, lanes)
-        out_ref[i // slots : (i + TILE) // slots, :] = jnp.max(picked, axis=1)
+            part = sims[:, c : c + lanes]
+            best = jnp.maximum(best, jnp.where(col_ix < down, part, -1.0))
+            top = jnp.max(jnp.where(down < col_ix, part, -1.0), axis=0, keepdims=True)
+            over.append(jnp.broadcast_to(top, (lanes, lanes)).T)
+        at = pl.ds(pl.multiple_of(other_at + j // 16, 8), per_tile)
+        out_ref[at, :] = by_slot(jnp.concatenate(over, axis=0), slot)
+        if j % half == 0:
+            total_ref[mine, :] = best
+        else:
+            best = jnp.broadcast_to(jnp.max(best, axis=1, keepdims=True), best.shape)
+            first = pl.multiple_of(mine_at + start // 16, 8)
+            for i in range(0, half, TILE):
+                out_ref[pl.ds(pl.multiple_of(first + i // 16, 8), per_tile), :] = by_slot(
+                    best[i : i + TILE], slot
+                )
 
 
 def pick_kernel(answer_ref, cl_ref, rank_ref, out_ref):
-    chips, lanes = answer_ref.shape
+    lanes = answer_ref.shape[1]
+    chips = answer_ref.shape[0] // 2
     count = cl_ref.shape[1]
     owner = (lax.broadcasted_iota(jnp.int32, (chips, count), 0) == cl_ref[...]).astype(
         jnp.float32
     ).astype(jnp.bfloat16)
     tn = (((0,), (0,)), ((), ()))
-    answer = answer_ref[...]
+    answer = jnp.maximum(answer_ref[:chips, :], answer_ref[chips:, :])
     high, rest = split(answer)
     middle, low = split(answer - high.astype(jnp.float32))
     by_rank = dot_f32(high, owner, tn) + (dot_f32(middle, owner, tn) + dot_f32(low, owner, tn))
@@ -234,7 +257,7 @@
 
 def on_device(embeddings, clusters, indices):
     count, width = embeddings.shape
-    chip_axes = ("y", "x_hi", "x_lo", "z")
+    chip_axes = ("z", "y", "x_hi", "x_lo")
     chips, slots, lanes = 64, 16, 128
     rows = chips * slots
     length = slots * width // lanes + 1
@@ -252,7 +275,7 @@
             pltpu.VMEM((count, width), jnp.float32),
             pltpu.VMEM((1, count), jnp.int32),
             pltpu.VMEM((1, count), jnp.int32),
-            dma((4,)),
+            dma((2,)),
             dma,
             dma,
         ],
@@ -265,17 +288,16 @@
     other = lax.ppermute(held, "core", [(0, 1), (1, 0)]).reshape(chips * length, lanes)
     held = held.reshape(chips * length, lanes)
     flops = 2 * rows * rows * width * 3
-    high, low, down, best, across = pl.pallas_call(
+    high, low, down, best = pl.pallas_call(
         own_kernel,
         out_shape=(
             bf16((rows, width)),
             bf16((rows, width)),
             f32((rows, lanes)),
             f32((rows, lanes)),
-            f32((8, rows)),
         ),
         in_specs=[VMEM],
-        out_specs=(VMEM,) * 5,
+        out_specs=(VMEM,) * 4,
         scratch_shapes=[pltpu.VMEM((rows, lanes), jnp.float32)],
         compiler_params=PARAMS,
         cost_estimate=pl.CostEstimate(flops=flops, bytes_accessed=8 << 20, transcendentals=0),
@@ -283,8 +305,8 @@
     )(held)
     result = pl.pallas_call(
         other_kernel,
-        out_shape=f32((chips, lanes)),
-        in_specs=[VMEM] * 6,
+        out_shape=f32((2 * chips, lanes)),
+        in_specs=[VMEM] * 5,
         out_specs=VMEM,
         scratch_shapes=[
             pltpu.VMEM((rows, width), jnp.bfloat16),
@@ -295,10 +317,10 @@
         compiler_params=PARAMS,
         cost_estimate=pl.CostEstimate(flops=flops, bytes_accessed=8 << 20, transcendentals=0),
         name="other",
-    )(other, high, low, down, best, across)
+    )(other, high, low, down, best)
     answer = lax.all_to_all(
-        result.reshape(chips, 1, lanes), chip_axes, split_axis=0, concat_axis=0, tiled=True
-    ).reshape(chips, lanes)
+        result.reshape(2 * chips, 1, lanes), ("core",) + chip_axes, split_axis=0, concat_axis=0, tiled=True
+    ).reshape(2 * chips, lanes)
     out = pl.pallas_call(
         pick_kernel,
         out_shape=f32((1, count)),
@@ -311,12 +333,11 @@
 
 
 def solution(mesh):
-    fine = Mesh(mesh.devices.reshape(4, 2, 2, 2, 4), ("y", "x_hi", "core", "x_lo", "z"))
-    points = ("y", "x_hi", "core", "x_lo", "z")
+    fine = Mesh(mesh.devices.reshape(4, 2, 2, 2, 4), POINTS)
     return jax.shard_map(
         on_device,
         mesh=fine,
-        in_specs=(P(points, None), P(points), P(points)),
-        out_specs=P(points),
+        in_specs=(P(POINTS, None), P(POINTS), P(POINTS)),
+        out_specs=P(POINTS),
         check_vma=False,
     )

time: 83.2 us -> 80.9 us (0.972)
  Pallas kernels: 13.7 us -> 11.1 us
  blocking collectives: 64.6 us -> 65.6 us
    pallas_call x1, Pallas kernels: 5.66 us -> 3.34 us  [on_device(): pl.pallas_call(other_kernel, out_shape=f32((2 * chips, lanes)), in_specs=...]
where the time goes in v4:
time: 80.9 us; the launch traced here: 80.8 us
  blocking collectives  65.6 us (81%)
  Pallas kernels  11.1 us (14%)
  starting transfers between devices  2.21 us (3%)
  waiting for transfers between devices  1.88 us (2%)
    all_to_all x1, blocking collectives, on_device(): lax.all_to_all(sending.reshape(chips * length, 1, lanes), chip_axes, spli...  52.2 us
    all_to_all x1, blocking collectives, on_device(): lax.all_to_all(result.reshape(2 * chips, 1, lanes), ('core',) + chip_axes...  13.4 us
    pallas_call x1, Pallas kernels, on_device(): pl.pallas_call(own_kernel, out_shape=(bf16((rows, width)), bf16((rows, wi...  3.44 us
    pallas_call x1, Pallas kernels, on_device(): pl.pallas_call(place_kernel, out_shape=(f32((chips * length, lanes)), jax...  3.41 us
    pallas_call x1, Pallas kernels, on_device(): pl.pallas_call(other_kernel, out_shape=f32((2 * chips, lanes)), in_specs=...  3.34 us
    ppermute x1, starting transfers between devices, on_device(): lax.ppermute(held, 'core', [(0, 1), (1, 0)]).reshape(chips * length, lanes)  2.21 us
    ppermute x1, waiting for transfers between devices, on_device(): lax.ppermute(held, 'core', [(0, 1), (1, 0)]).reshape(chips * length, lanes)  1.88 us
  transfers between devices with their start and end apart: 1, of which 1 were waited for; matrix products, arithmetic and copies ran while one was open for 0% of the time, Pallas kernels for 4%

profile of v4, /device:TPU:1, one launch (start us, length us, event | category | flops | bytes accessed | tf_op | source)
XLA Modules:
  0.0 80.8 jit_solution(431018854863374789)
XLA Ops:
  0.0 3.4 %place.1 = (f32[6208,128]{1,0:T(8,128)S(1)}, s32[1,512]{1,0:T(1,128)S(1)}) custom-call(f32[512,768]{1,0:T(8,128)} %emb_hbm.1, s32[1,512]{1,0:T(1,128)} %bitcast.18, s32[1,512]{1,0:T(1,128)} %bitcast.21), custom_call_target="tpu_custom_call" | custom-call | tf_op jit(solution)/shard_map/place/pallas_call | solution.py:269
  3.4 52.2 %all_to_all.10 = f32[6208,1,128]{2,1,0:T(1,128)S(1)} all-to-all(f32[6208,1,128]{2,1,0:T(1,128)S(1)} %bitcast.15), channel_id=1, replica_groups=mesh['y'=4,'x_hi'=2,'core'=2,'x_lo'=2,'z'=4] {'z','y','x_hi','x_lo'}, dimensions={0} | all-to-all | bytes 6356992 | tf_op jit(solution)/shard_map/all_to_all | solution.py:285
  55.6 2.2 %collective-permute-start = (f32[6208,1,128]{2,0,1:T(8,128)S(1)}, f32[6208,1,128]{2,0,1:T(8,128)S(1)}, u32[]{:S(2)}, u32[]{:S(2)}) collective-permute-start(f32[6208,1,128]{2,0,1:T(8,128)S(1)} %bitcast.13), channel_id=1, source_target_pairs={{0,8},{8,0},{1,9},{9,1},{2,10},{10,2},{3,11},{11,3},{4,12},{12,4},... | collective-permute-start | bytes 9535496 | tf_op jit(solution)/shard_map/ppermute | solution.py:288
  57.8 3.4 %own.1 = (bf16[1024,768]{1,0:T(8,128)(2,1)S(1)}, bf16[1024,768]{1,0:T(8,128)(2,1)S(1)}, f32[1024,128]{1,0:T(8,128)S(1)}, f32[1024,128]{1,0:T(8,128)S(1)}) custom-call(f32[6208,128]{1,0:T(8,128)S(1)} %bitcast.14), custom_call_target="tpu_custom_call" | custom-call | flops 4831838208 | bytes 8388608 | tf_op jit(solution)/shard_map/own/pallas_call | solution.py:291
  61.3 1.9 %collective-permute-done = f32[6208,1,128]{2,0,1:T(8,128)S(1)} collective-permute-done((f32[6208,1,128]{2,0,1:T(8,128)S(1)}, f32[6208,1,128]{2,0,1:T(8,128)S(1)}, u32[]{:S(2)}, u32[]{:S(2)}) %collective-permute-start) | collective-permute-done | bytes 3178528 | tf_op jit(solution)/shard_map/ppermute | solution.py:288
  63.2 0.0 copy-start
  63.2 3.3 %other.1 = f32[128,128]{1,0:T(8,128)S(1)} custom-call(f32[6208,128]{1,0:T(8,128)S(1)} %bitcast.20, bf16[1024,768]{1,0:T(8,128)(2,1)S(1)} %get-tuple-element.12.high_ref, bf16[1024,768]{1,0:T(8,128)(2,1)S(1)} %get-tuple-element.13.low_ref, f32[1024,128]{1,0:T(8,128)S(1)} %get-tuple-element.14.down_ref, f32[1024,128]{1,0:T(8,128)S(1)} %get-tuple-element.15.best_ref), custom_call_target="tpu_custom_call" | custom-call | flops 4831838208 | bytes 8388608 | tf_op jit(solution)/shard_map/other/pallas_call | solution.py:306
  66.5 13.4 %all_to_all.11 = f32[128,1,128]{2,1,0:T(1,128)S(1)} all-to-all(f32[128,1,128]{2,1,0:T(1,128)S(1)} %bitcast.17), channel_id=1, replica_groups=mesh['y'=4,'x_hi'=2,'core'=2,'x_lo'=2,'z'=4] {'core','z','y','x_hi','x_lo'}, dimensions={0} | all-to-all | bytes 131072 | tf_op jit(solution)/shard_map/all_to_all | solution.py:321
  79.9 0.0 copy-done
  79.9 0.9 %pick.1 = f32[1,512]{1,0:T(1,128)} custom-call(f32[128,128]{1,0:T(8,128)S(1)} %bitcast.16, s32[1,512]{1,0:T(1,128)S(1)} %bitcast.19, s32[1,512]{1,0:T(1,128)S(1)} %get-tuple-element.16.rank_ref), custom_call_target="tpu_custom_call" | custom-call | tf_op jit(solution)/shard_map/pick/pallas_call | solution.py:324
Async XLA Ops:
  55.6 7.5 %collective-permute-start = (f32[6208,1,128]{2,0,1:T(8,128)S(1)}, f32[6208,1,128]{2,0,1:T(8,128)S(1)}, u32[]{:S(2)}, u32[]{:S(2)}) collective-permute-start(f32[6208,1,128]{2,0,1:T(8,128)S(1)} %bitcast.13), channel_id=1, source_target_pairs={{0,8},{8,0},{1,9},{9,1},{2,10},{10,2},{3,11},{11,3},{4,12},{12,4},... | collective-permute-start | bytes 9535496 | tf_op jit(solution)/shard_map/ppermute | solution.py:288
  63.2 16.7 %copy-start = (s32[512]{0:T(512)S(1)}, s32[512]{0:T(512)}, u32[]{:S(2)}) copy-start(s32[512]{0:T(512)} %param.4) | copy-start | bytes 6148

commit v5 on v4

--- a/solution.py
+++ b/solution.py
@@ -199,26 +199,18 @@
             best_ref[sj, :] = best
 
 
-def other_kernel(
-    held_ref, high_ref, low_ref, down_ref, best_ref, out_ref, high_o, low_o, spread_ref, total_ref
-):
-    rows, lanes = down_ref.shape
-    half = rows // 2
-    chips = rows // 16
-    per_tile = TILE // 16
+def cross(held_ref, high_ref, low_ref, down_ref, start, high_o, low_o, spread_ref, best_ref, total_ref):
+    half, lanes = high_o.shape[0], down_ref.shape[1]
     slot = slot_of(TILE, lanes)
-    core = lax.axis_index("core")
-    mine_at = pl.multiple_of(core * chips, chips)
-    other_at = pl.multiple_of((1 - core) * chips, chips)
-    for j in range(0, rows, TILE):
+    mine = pl.ds(pl.multiple_of(start, half), half)
+    cols = []
+    for j in range(0, half, TILE):
         sj = slice(j, j + TILE)
         unpack(held_ref, j // 16, TILE // 16, high_o, low_o, spread_ref)
         down_j = tags_of(spread_ref[sj, :], slot)
-        start = core * half if j < half else (1 - core) * half
-        mine = pl.ds(pl.multiple_of(start, half), half)
         sims = products(high_ref[mine, :], low_ref[mine, :], high_o[sj, :], low_o[sj, :])
         down = down_ref[mine, :]
-        best = best_ref[mine, :] if j % half == 0 else total_ref[mine, :]
+        best = best_ref[mine, :] if j == 0 else total_ref[...]
         over = []
         for c in range(0, TILE, lanes):
             col_ix = down_j[c : c + lanes, :].T[:1, :]
@@ -226,17 +218,47 @@
             best = jnp.maximum(best, jnp.where(col_ix < down, part, -1.0))
             top = jnp.max(jnp.where(down < col_ix, part, -1.0), axis=0, keepdims=True)
             over.append(jnp.broadcast_to(top, (lanes, lanes)).T)
-        at = pl.ds(pl.multiple_of(other_at + j // 16, 8), per_tile)
-        out_ref[at, :] = by_slot(jnp.concatenate(over, axis=0), slot)
-        if j % half == 0:
-            total_ref[mine, :] = best
-        else:
-            best = jnp.broadcast_to(jnp.max(best, axis=1, keepdims=True), best.shape)
-            first = pl.multiple_of(mine_at + start // 16, 8)
-            for i in range(0, half, TILE):
-                out_ref[pl.ds(pl.multiple_of(first + i // 16, 8), per_tile), :] = by_slot(
-                    best[i : i + TILE], slot
-                )
+        cols.append(by_slot(jnp.concatenate(over, axis=0), slot))
+        total_ref[...] = best
+    rows = []
+    best = jnp.broadcast_to(jnp.max(total_ref[...], axis=1, keepdims=True), (half, lanes))
+    for i in range(0, half, TILE):
+        rows.append(by_slot(best[i : i + TILE], slot))
+    return jnp.concatenate(rows, axis=0), jnp.concatenate(cols, axis=0)
+
+
+def first_kernel(
+    held_ref, high_ref, low_ref, down_ref, best_ref, row_ref, col_ref, high_o, low_o, spread_ref, total_ref
+):
+    start = lax.axis_index("core") * high_o.shape[0]
+    row_ref[...], col_ref[...] = cross(
+        held_ref, high_ref, low_ref, down_ref, start, high_o, low_o, spread_ref, best_ref, total_ref
+    )
+
+
+def second_kernel(
+    held_ref, high_ref, low_ref, down_ref, best_ref, row_ref, col_ref, out_ref, high_o, low_o, spread_ref, total_ref
+):
+    core = lax.axis_index("core")
+    rows, cols = cross(
+        held_ref,
+        high_ref,
+        low_ref,
+        down_ref,
+        (1 - core) * high_o.shape[0],
+        high_o,
+        low_o,
+        spread_ref,
+        best_ref,
+        total_ref,
+    )
+    chips = out_ref.shape[0] // 4
+    first = core == 0
+    own = jnp.where(first, row_ref[...], rows), jnp.where(first, rows, row_ref[...])
+    other = col_ref[...], cols
+    for h in range(2):
+        out_ref[h * chips : (h + 1) * chips, :] = jnp.where(first, own[h], other[h])
+        out_ref[(2 + h) * chips : (3 + h) * chips, :] = jnp.where(first, other[h], own[h])
 
 
 def pick_kernel(answer_ref, cl_ref, rank_ref, out_ref):
@@ -285,7 +307,11 @@
     held = lax.all_to_all(
         sending.reshape(chips * length, 1, lanes), chip_axes, split_axis=0, concat_axis=0, tiled=True
     )
-    other = lax.ppermute(held, "core", [(0, 1), (1, 0)]).reshape(chips * length, lanes)
+    part = chips * length // 2
+    arrived = [
+        lax.ppermute(held[h * part : (h + 1) * part], "core", [(0, 1), (1, 0)]).reshape(part, lanes)
+        for h in range(2)
+    ]
     held = held.reshape(chips * length, lanes)
     flops = 2 * rows * rows * width * 3
     high, low, down, best = pl.pallas_call(
@@ -303,21 +329,34 @@
         cost_estimate=pl.CostEstimate(flops=flops, bytes_accessed=8 << 20, transcendentals=0),
         name="own",
     )(held)
+    half = rows // 2
+    scratch = [
+        pltpu.VMEM((half, width), jnp.bfloat16),
+        pltpu.VMEM((half, width), jnp.bfloat16),
+        pltpu.VMEM((half, lanes), jnp.float32),
+        pltpu.VMEM((half, lanes), jnp.float32),
+    ]
+    cost = pl.CostEstimate(flops=flops // 4, bytes_accessed=2 << 20, transcendentals=0)
+    row, col = pl.pallas_call(
+        first_kernel,
+        out_shape=(f32((chips // 2, lanes)),) * 2,
+        in_specs=[VMEM] * 5,
+        out_specs=(VMEM,) * 2,
+        scratch_shapes=scratch,
+        compiler_params=PARAMS,
+        cost_estimate=cost,
+        name="first",
+    )(arrived[0], high, low, down, best)
     result = pl.pallas_call(
-        other_kernel,
+        second_kernel,
         out_shape=f32((2 * chips, lanes)),
-        in_specs=[VMEM] * 5,
+        in_specs=[VMEM] * 7,
         out_specs=VMEM,
-        scratch_shapes=[
-            pltpu.VMEM((rows, width), jnp.bfloat16),
-            pltpu.VMEM((rows, width), jnp.bfloat16),
-            pltpu.VMEM((rows, lanes), jnp.float32),
-            pltpu.VMEM((rows, lanes), jnp.float32),
-        ],
-        compiler_params=PARAMS,
-        cost_estimate=pl.CostEstimate(flops=flops, bytes_accessed=8 << 20, transcendentals=0),
-        name="other",
-    )(other, high, low, down, best)
+        scratch_shapes=scratch,
+        compiler_params=PARAMS,
+        cost_estimate=cost,
+        name="second",
+    )(arrived[1], high, low, down, best, row, col)
     answer = lax.all_to_all(
         result.reshape(2 * chips, 1, lanes), ("core",) + chip_axes, split_axis=0, concat_axis=0, tiled=True
     ).reshape(2 * chips, lanes)

time: 80.9 us -> 79.8 us (0.986)
  waiting for transfers between devices: 1.88 us -> 0.01 us
    ppermute x1 -> x2, waiting for transfers between devices: 1.88 us -> 0.01 us  [on_device(): lax.ppermute(held[h * part:(h + 1) * part], 'core', [(0, 1), (1, 0)])]
    pallas_call x1 -> x2, Pallas kernels: 3.34 us -> 3.64 us  [the longest x1 1.82 us: on_device(): pl.pallas_call(second_kernel, out_shape=f32((2 * chips, lanes)), in_specs...]
    ppermute x1 -> x2, starting transfers between devices: 2.21 us -> 2.38 us  [on_device(): lax.ppermute(held[h * part:(h + 1) * part], 'core', [(0, 1), (1, 0)])]
  transfers between devices with their start and end apart: 1 -> 2, of which waited for: 1 -> 0; matrix products, arithmetic and copies ran while one was open for 0% -> 0% of each run, Pallas kernels for 4% -> 7%
where the time goes in v5:
time: 79.8 us; the launch traced here: 79.6 us
  blocking collectives  65.6 us (82%)
  Pallas kernels  11.4 us (14%)
  starting transfers between devices  2.38 us (3%)
    all_to_all x1, blocking collectives, on_device(): lax.all_to_all(sending.reshape(chips * length, 1, lanes), chip_axes, spli...  52.2 us
    all_to_all x1, blocking collectives, on_device(): lax.all_to_all(result.reshape(2 * chips, 1, lanes), ('core',) + chip_axes...  13.4 us
    pallas_call x1, Pallas kernels, on_device(): pl.pallas_call(own_kernel, out_shape=(bf16((rows, width)), bf16((rows, wi...  3.45 us
    pallas_call x1, Pallas kernels, on_device(): pl.pallas_call(place_kernel, out_shape=(f32((chips * length, lanes)), jax...  3.41 us
    ppermute x2, starting transfers between devices, on_device(): lax.ppermute(held[h * part:(h + 1) * part], 'core', [(0, 1), (1, 0)])  2.38 us
    pallas_call x1, Pallas kernels, on_device(): pl.pallas_call(second_kernel, out_shape=f32((2 * chips, lanes)), in_specs...  1.82 us
    pallas_call x1, Pallas kernels, on_device(): pl.pallas_call(first_kernel, out_shape=(f32((chips // 2, lanes)),) * 2, i...  1.82 us
  transfers between devices with their start and end apart: 2, of which 0 were waited for; matrix products, arithmetic and copies ran while one was open for 0% of the time, Pallas kernels for 7%

profile of v5, /device:TPU:1, one launch (start us, length us, event | category | flops | bytes accessed | tf_op | source)
XLA Modules:
  0.0 79.6 jit_solution(7531707806022350437)
XLA Ops:
  0.0 3.4 %place.1 = (f32[6208,128]{1,0:T(8,128)S(1)}, s32[1,512]{1,0:T(1,128)S(1)}) custom-call(f32[512,768]{1,0:T(8,128)} %emb_hbm.1, s32[1,512]{1,0:T(1,128)} %bitcast.21, s32[1,512]{1,0:T(1,128)} %bitcast.23), custom_call_target="tpu_custom_call" | custom-call | tf_op jit(solution)/shard_map/place/pallas_call | solution.py:291
  3.4 52.2 %all_to_all.10 = f32[6208,1,128]{2,1,0:T(1,128)S(1)} all-to-all(f32[6208,1,128]{2,1,0:T(1,128)S(1)} %bitcast.16), channel_id=1, replica_groups=mesh['y'=4,'x_hi'=2,'core'=2,'x_lo'=2,'z'=4] {'z','y','x_hi','x_lo'}, dimensions={0} | all-to-all | bytes 6356992 | tf_op jit(solution)/shard_map/all_to_all | solution.py:307
  55.6 0.2 fusion
  55.8 2.3 %collective-permute-start.1 = (f32[3104,1,128]{2,0,1:T(8,128)S(1)}, f32[3104,1,128]{2,0,1:T(8,128)S(1)}, u32[]{:S(2)}, u32[]{:S(2)}) collective-permute-start(f32[3104,1,128]{2,0,1:T(8,128)S(1)} %get-tuple-element.21), channel_id=1, source_target_pairs={{0,8},{8,0},{1,9},{9,1},{2,10},{10,2},{3,11},{11,3},{4,12},{12,4},... | collective-permute-start | bytes 4767752 | tf_op jit(solution)/shard_map/ppermute | solution.py:312
  58.1 0.1 collective-permute-start
  58.2 3.4 %own.1 = (bf16[1024,768]{1,0:T(8,128)(2,1)S(1)}, bf16[1024,768]{1,0:T(8,128)(2,1)S(1)}, f32[1024,128]{1,0:T(8,128)S(1)}, f32[1024,128]{1,0:T(8,128)S(1)}) custom-call(f32[6208,128]{1,0:T(8,128)S(1)} %bitcast.15), custom_call_target="tpu_custom_call" | custom-call | flops 4831838208 | bytes 8388608 | tf_op jit(solution)/shard_map/own/pallas_call | solution.py:317
  61.7 0.0 collective-permute-done.1
  61.7 1.8 %first.1 = (f32[32,128]{1,0:T(8,128)S(1)}, f32[32,128]{1,0:T(8,128)S(1)}) custom-call(f32[3104,128]{1,0:T(8,128)S(1)} %bitcast.18, bf16[1024,768]{1,0:T(8,128)(2,1)S(1)} %get-tuple-element.14.high_ref, bf16[1024,768]{1,0:T(8,128)(2,1)S(1)} %get-tuple-element.15.low_ref, f32[1024,128]{1,0:T(8,128)S(1)} %get-tuple-element.16.down_ref, ...), custom_call_target="tpu_custom_call" | custom-call | flops 1207959552 | bytes 2097152 | tf_op jit(solution)/shard_map/first/pallas_call | solution.py:340
  63.5 0.0 collective-permute-done
  63.5 0.0 copy-start
  63.5 1.8 %second.1 = f32[128,128]{1,0:T(8,128)S(1)} custom-call(f32[3104,128]{1,0:T(8,128)S(1)} %bitcast.17, bf16[1024,768]{1,0:T(8,128)(2,1)S(1)} %get-tuple-element.14.high_ref, bf16[1024,768]{1,0:T(8,128)(2,1)S(1)} %get-tuple-element.15.low_ref, f32[1024,128]{1,0:T(8,128)S(1)} %get-tuple-element.16.down_ref, f32[1024,128]{1,0:T(8,128)S(1)} %get-tuple-element.17.best_ref, ...), custom_call_target="tpu_custom_call" | custom-call | flops 1207959552 | bytes 2097152 | tf_op jit(solution)/shard_map/second/pallas_call | solution.py:350
  65.4 13.4 %all_to_all.11 = f32[128,1,128]{2,1,0:T(1,128)S(1)} all-to-all(f32[128,1,128]{2,1,0:T(1,128)S(1)} %bitcast.19), channel_id=1, replica_groups=mesh['y'=4,'x_hi'=2,'core'=2,'x_lo'=2,'z'=4] {'core','z','y','x_hi','x_lo'}, dimensions={0} | all-to-all | bytes 131072 | tf_op jit(solution)/shard_map/all_to_all | solution.py:360
  78.8 0.0 copy-done
  78.8 0.9 %pick.1 = f32[1,512]{1,0:T(1,128)} custom-call(f32[128,128]{1,0:T(8,128)S(1)} %bitcast.20, s32[1,512]{1,0:T(1,128)S(1)} %bitcast.22, s32[1,512]{1,0:T(1,128)S(1)} %get-tuple-element.20.rank_ref), custom_call_target="tpu_custom_call" | custom-call | tf_op jit(solution)/shard_map/pick/pallas_call | solution.py:363
Async XLA Ops:
  55.8 5.8 %collective-permute-start.1 = (f32[3104,1,128]{2,0,1:T(8,128)S(1)}, f32[3104,1,128]{2,0,1:T(8,128)S(1)}, u32[]{:S(2)}, u32[]{:S(2)}) collective-permute-start(f32[3104,1,128]{2,0,1:T(8,128)S(1)} %get-tuple-element.21), channel_id=1, source_target_pairs={{0,8},{8,0},{1,9},{9,1},{2,10},{10,2},{3,11},{11,3},{4,12},{12,4},... | collective-permute-start | bytes 4767752 | tf_op jit(solution)/shard_map/ppermute | solution.py:312
  58.1 5.4 %collective-permute-start = (f32[3104,1,128]{2,0,1:T(8,128)S(1)}, f32[3104,1,128]{2,0,1:T(8,128)S(1)}, u32[]{:S(2)}, u32[]{:S(2)}) collective-permute-start(f32[3104,1,128]{2,0,1:T(8,128)S(1)} %get-tuple-element.22), channel_id=1, source_target_pairs={{0,8},{8,0},{1,9},{9,1},{2,10},{10,2},{3,11},{11,3},{4,12},{12,4},... | collective-permute-start | bytes 4767752 | tf_op jit(solution)/shard_map/ppermute | solution.py:312
  63.5 15.2 %copy-start = (s32[512]{0:T(512)S(1)}, s32[512]{0:T(512)}, u32[]{:S(2)}) copy-start(s32[512]{0:T(512)} %param.4) | copy-start | bytes 6148

commit v6 on v5

--- a/solution.py
+++ b/solution.py
@@ -202,29 +202,45 @@
 def cross(held_ref, high_ref, low_ref, down_ref, start, high_o, low_o, spread_ref, best_ref, total_ref):
     half, lanes = high_o.shape[0], down_ref.shape[1]
     slot = slot_of(TILE, lanes)
-    mine = pl.ds(pl.multiple_of(start, half), half)
-    cols = []
+    cols, over = {}, {}
+
+    def mine(i):
+        return pl.ds(pl.multiple_of(start + i, TILE), TILE)
+
+    def finish(i, j, sims):
+        down = down_ref[mine(i), :]
+        best = best_ref[mine(i), :] if j == 0 else total_ref[i : i + TILE, :]
+        for n, col_ix in enumerate(cols[j]):
+            part = sims[:, n * lanes : (n + 1) * lanes]
+            best = jnp.maximum(best, jnp.where(col_ix < down, part, -1.0))
+            top = jnp.where(down < col_ix, part, -1.0).reshape(TILE // 8, 8, lanes)
+            top = jnp.max(top, axis=0)
+            over[j, n] = top if i == 0 else jnp.maximum(over[j, n], top)
+        total_ref[i : i + TILE, :] = best
+
+    waiting = None
     for j in range(0, half, TILE):
         sj = slice(j, j + TILE)
         unpack(held_ref, j // 16, TILE // 16, high_o, low_o, spread_ref)
         down_j = tags_of(spread_ref[sj, :], slot)
-        sims = products(high_ref[mine, :], low_ref[mine, :], high_o[sj, :], low_o[sj, :])
-        down = down_ref[mine, :]
-        best = best_ref[mine, :] if j == 0 else total_ref[...]
-        over = []
-        for c in range(0, TILE, lanes):
-            col_ix = down_j[c : c + lanes, :].T[:1, :]
-            part = sims[:, c : c + lanes]
-            best = jnp.maximum(best, jnp.where(col_ix < down, part, -1.0))
-            top = jnp.max(jnp.where(down < col_ix, part, -1.0), axis=0, keepdims=True)
-            over.append(jnp.broadcast_to(top, (lanes, lanes)).T)
-        cols.append(by_slot(jnp.concatenate(over, axis=0), slot))
-        total_ref[...] = best
-    rows = []
-    best = jnp.broadcast_to(jnp.max(total_ref[...], axis=1, keepdims=True), (half, lanes))
+        cols[j] = [down_j[c : c + lanes, :].T[:1, :] for c in range(0, TILE, lanes)]
+        for i in range(0, half, TILE):
+            sims = products(high_ref[mine(i), :], low_ref[mine(i), :], high_o[sj, :], low_o[sj, :])
+            if waiting is not None:
+                finish(*waiting)
+            waiting = i, j, sims
+    finish(*waiting)
+    rows_out, cols_out = [], []
+    for j in range(0, half, TILE):
+        wide = [
+            jnp.broadcast_to(jnp.max(over[j, n], axis=0, keepdims=True), (lanes, lanes)).T
+            for n in range(TILE // lanes)
+        ]
+        cols_out.append(by_slot(jnp.concatenate(wide, axis=0), slot))
     for i in range(0, half, TILE):
-        rows.append(by_slot(best[i : i + TILE], slot))
-    return jnp.concatenate(rows, axis=0), jnp.concatenate(cols, axis=0)
+        best = jnp.max(total_ref[i : i + TILE, :], axis=1, keepdims=True)
+        rows_out.append(by_slot(jnp.broadcast_to(best, (TILE, lanes)), slot))
+    return jnp.concatenate(rows_out, axis=0), jnp.concatenate(cols_out, axis=0)
 
 
 def first_kernel(

time: 79.8 us -> 79.7 us (level)
  no operation moved by 1% of the time
where the time goes in v6:
time: 79.7 us; the launch traced here: 79.5 us
  blocking collectives  65.6 us (82%)
  Pallas kernels  11.2 us (14%)
  starting transfers between devices  2.38 us (3%)
    all_to_all x1, blocking collectives, on_device(): lax.all_to_all(sending.reshape(chips * length, 1, lanes), chip_axes, spli...  52.2 us
    all_to_all x1, blocking collectives, on_device(): lax.all_to_all(result.reshape(2 * chips, 1, lanes), ('core',) + chip_axes...  13.4 us
    pallas_call x1, Pallas kernels, on_device(): pl.pallas_call(own_kernel, out_shape=(bf16((rows, width)), bf16((rows, wi...  3.45 us
    pallas_call x1, Pallas kernels, on_device(): pl.pallas_call(place_kernel, out_shape=(f32((chips * length, lanes)), jax...  3.41 us
    ppermute x2, starting transfers between devices, on_device(): lax.ppermute(held[h * part:(h + 1) * part], 'core', [(0, 1), (1, 0)])  2.38 us
    pallas_call x1, Pallas kernels, on_device(): pl.pallas_call(second_kernel, out_shape=f32((2 * chips, lanes)), in_specs...  1.74 us
    pallas_call x1, Pallas kernels, on_device(): pl.pallas_call(first_kernel, out_shape=(f32((chips // 2, lanes)),) * 2, i...  1.73 us
  transfers between devices with their start and end apart: 2, of which 0 were waited for; matrix products, arithmetic and copies ran while one was open for 0% of the time, Pallas kernels for 7%

profile of v6, /device:TPU:1, one launch (start us, length us, event | category | flops | bytes accessed | tf_op | source)
XLA Modules:
  0.0 79.5 jit_solution(16629278585834103774)
XLA Ops:
  0.0 3.4 %place.1 = (f32[6208,128]{1,0:T(8,128)S(1)}, s32[1,512]{1,0:T(1,128)S(1)}) custom-call(f32[512,768]{1,0:T(8,128)} %emb_hbm.1, s32[1,512]{1,0:T(1,128)} %bitcast.21, s32[1,512]{1,0:T(1,128)} %bitcast.23), custom_call_target="tpu_custom_call" | custom-call | tf_op jit(solution)/shard_map/place/pallas_call | solution.py:307
  3.4 52.2 %all_to_all.10 = f32[6208,1,128]{2,1,0:T(1,128)S(1)} all-to-all(f32[6208,1,128]{2,1,0:T(1,128)S(1)} %bitcast.16), channel_id=1, replica_groups=mesh['y'=4,'x_hi'=2,'core'=2,'x_lo'=2,'z'=4] {'z','y','x_hi','x_lo'}, dimensions={0} | all-to-all | bytes 6356992 | tf_op jit(solution)/shard_map/all_to_all | solution.py:323
  55.6 0.2 fusion
  55.8 2.3 %collective-permute-start.1 = (f32[3104,1,128]{2,0,1:T(8,128)S(1)}, f32[3104,1,128]{2,0,1:T(8,128)S(1)}, u32[]{:S(2)}, u32[]{:S(2)}) collective-permute-start(f32[3104,1,128]{2,0,1:T(8,128)S(1)} %get-tuple-element.21), channel_id=1, source_target_pairs={{0,8},{8,0},{1,9},{9,1},{2,10},{10,2},{3,11},{11,3},{4,12},{12,4},... | collective-permute-start | bytes 4767752 | tf_op jit(solution)/shard_map/ppermute | solution.py:328
  58.1 0.1 collective-permute-start
  58.2 3.4 %own.1 = (bf16[1024,768]{1,0:T(8,128)(2,1)S(1)}, bf16[1024,768]{1,0:T(8,128)(2,1)S(1)}, f32[1024,128]{1,0:T(8,128)S(1)}, f32[1024,128]{1,0:T(8,128)S(1)}) custom-call(f32[6208,128]{1,0:T(8,128)S(1)} %bitcast.15), custom_call_target="tpu_custom_call" | custom-call | flops 4831838208 | bytes 8388608 | tf_op jit(solution)/shard_map/own/pallas_call | solution.py:333
  61.7 0.0 collective-permute-done.1
  61.7 1.7 %first.1 = (f32[32,128]{1,0:T(8,128)S(1)}, f32[32,128]{1,0:T(8,128)S(1)}) custom-call(f32[3104,128]{1,0:T(8,128)S(1)} %bitcast.18, bf16[1024,768]{1,0:T(8,128)(2,1)S(1)} %get-tuple-element.14.high_ref, bf16[1024,768]{1,0:T(8,128)(2,1)S(1)} %get-tuple-element.15.low_ref, f32[1024,128]{1,0:T(8,128)S(1)} %get-tuple-element.16.down_ref, ...), custom_call_target="tpu_custom_call" | custom-call | flops 1207959552 | bytes 2097152 | tf_op jit(solution)/shard_map/first/pallas_call | solution.py:356
  63.4 0.0 collective-permute-done
  63.5 0.0 copy-start
  63.5 1.7 %second.1 = f32[128,128]{1,0:T(8,128)S(1)} custom-call(f32[3104,128]{1,0:T(8,128)S(1)} %bitcast.17, bf16[1024,768]{1,0:T(8,128)(2,1)S(1)} %get-tuple-element.14.high_ref, bf16[1024,768]{1,0:T(8,128)(2,1)S(1)} %get-tuple-element.15.low_ref, f32[1024,128]{1,0:T(8,128)S(1)} %get-tuple-element.16.down_ref, f32[1024,128]{1,0:T(8,128)S(1)} %get-tuple-element.17.best_ref, ...), custom_call_target="tpu_custom_call" | custom-call | flops 1207959552 | bytes 2097152 | tf_op jit(solution)/shard_map/second/pallas_call | solution.py:366
  65.2 13.4 %all_to_all.11 = f32[128,1,128]{2,1,0:T(1,128)S(1)} all-to-all(f32[128,1,128]{2,1,0:T(1,128)S(1)} %bitcast.19), channel_id=1, replica_groups=mesh['y'=4,'x_hi'=2,'core'=2,'x_lo'=2,'z'=4] {'core','z','y','x_hi','x_lo'}, dimensions={0} | all-to-all | bytes 131072 | tf_op jit(solution)/shard_map/all_to_all | solution.py:376
  78.6 0.0 copy-done
  78.6 0.9 %pick.1 = f32[1,512]{1,0:T(1,128)} custom-call(f32[128,128]{1,0:T(8,128)S(1)} %bitcast.20, s32[1,512]{1,0:T(1,128)S(1)} %bitcast.22, s32[1,512]{1,0:T(1,128)S(1)} %get-tuple-element.20.rank_ref), custom_call_target="tpu_custom_call" | custom-call | tf_op jit(solution)/shard_map/pick/pallas_call | solution.py:379
Async XLA Ops:
  55.8 5.8 %collective-permute-start.1 = (f32[3104,1,128]{2,0,1:T(8,128)S(1)}, f32[3104,1,128]{2,0,1:T(8,128)S(1)}, u32[]{:S(2)}, u32[]{:S(2)}) collective-permute-start(f32[3104,1,128]{2,0,1:T(8,128)S(1)} %get-tuple-element.21), channel_id=1, source_target_pairs={{0,8},{8,0},{1,9},{9,1},{2,10},{10,2},{3,11},{11,3},{4,12},{12,4},... | collective-permute-start | bytes 4767752 | tf_op jit(solution)/shard_map/ppermute | solution.py:328
  58.1 5.3 %collective-permute-start = (f32[3104,1,128]{2,0,1:T(8,128)S(1)}, f32[3104,1,128]{2,0,1:T(8,128)S(1)}, u32[]{:S(2)}, u32[]{:S(2)}) collective-permute-start(f32[3104,1,128]{2,0,1:T(8,128)S(1)} %get-tuple-element.22), channel_id=1, source_target_pairs={{0,8},{8,0},{1,9},{9,1},{2,10},{10,2},{3,11},{11,3},{4,12},{12,4},... | collective-permute-start | bytes 4767752 | tf_op jit(solution)/shard_map/ppermute | solution.py:328
  63.5 15.1 %copy-start = (s32[512]{0:T(512)S(1)}, s32[512]{0:T(512)}, u32[]{:S(2)}) copy-start(s32[512]{0:T(512)} %param.4) | copy-start | bytes 6148

commit v7 on v6

--- a/solution.py
+++ b/solution.py
@@ -199,82 +199,117 @@
             best_ref[sj, :] = best
 
 
-def cross(held_ref, high_ref, low_ref, down_ref, start, high_o, low_o, spread_ref, best_ref, total_ref):
+def cross(held_ref, high_ref, low_ref, down_ref, parts, high_o, low_o, spread_ref, get, put):
     half, lanes = high_o.shape[0], down_ref.shape[1]
     slot = slot_of(TILE, lanes)
     cols, over = {}, {}
 
-    def mine(i):
-        return pl.ds(pl.multiple_of(start + i, TILE), TILE)
-
-    def finish(i, j, sims):
-        down = down_ref[mine(i), :]
-        best = best_ref[mine(i), :] if j == 0 else total_ref[i : i + TILE, :]
+    def finish(i, rows, j, sims):
+        down = down_ref[rows, :]
+        best = get(i, j)
         for n, col_ix in enumerate(cols[j]):
             part = sims[:, n * lanes : (n + 1) * lanes]
             best = jnp.maximum(best, jnp.where(col_ix < down, part, -1.0))
             top = jnp.where(down < col_ix, part, -1.0).reshape(TILE // 8, 8, lanes)
             top = jnp.max(top, axis=0)
-            over[j, n] = top if i == 0 else jnp.maximum(over[j, n], top)
-        total_ref[i : i + TILE, :] = best
+            over[j, n] = top if (j, n) not in over else jnp.maximum(over[j, n], top)
+        put(i, j, best)
 
     waiting = None
-    for j in range(0, half, TILE):
-        sj = slice(j, j + TILE)
-        unpack(held_ref, j // 16, TILE // 16, high_o, low_o, spread_ref)
+    for j in range(half // TILE):
+        sj = slice(j * TILE, (j + 1) * TILE)
+        unpack(held_ref, sj.start // 16, TILE // 16, high_o, low_o, spread_ref)
         down_j = tags_of(spread_ref[sj, :], slot)
         cols[j] = [down_j[c : c + lanes, :].T[:1, :] for c in range(0, TILE, lanes)]
-        for i in range(0, half, TILE):
-            sims = products(high_ref[mine(i), :], low_ref[mine(i), :], high_o[sj, :], low_o[sj, :])
+        for i, start in enumerate(parts(j)):
+            rows = pl.ds(pl.multiple_of(start, TILE), TILE)
+            sims = products(high_ref[rows, :], low_ref[rows, :], high_o[sj, :], low_o[sj, :])
             if waiting is not None:
                 finish(*waiting)
-            waiting = i, j, sims
+            waiting = i, rows, j, sims
     finish(*waiting)
-    rows_out, cols_out = [], []
-    for j in range(0, half, TILE):
+    out = []
+    for j in range(half // TILE):
         wide = [
             jnp.broadcast_to(jnp.max(over[j, n], axis=0, keepdims=True), (lanes, lanes)).T
             for n in range(TILE // lanes)
         ]
-        cols_out.append(by_slot(jnp.concatenate(wide, axis=0), slot))
-    for i in range(0, half, TILE):
-        best = jnp.max(total_ref[i : i + TILE, :], axis=1, keepdims=True)
-        rows_out.append(by_slot(jnp.broadcast_to(best, (TILE, lanes)), slot))
-    return jnp.concatenate(rows_out, axis=0), jnp.concatenate(cols_out, axis=0)
+        out.append(by_slot(jnp.concatenate(wide, axis=0), slot))
+    return jnp.concatenate(out, axis=0)
+
+
+def swapped(core, blocks):
+    lanes = blocks[0].shape[1]
+    slot = slot_of(TILE, lanes)
+    one, two = (
+        by_slot(jnp.broadcast_to(jnp.max(best, axis=1, keepdims=True), best.shape), slot)
+        for best in blocks
+    )
+    return jnp.concatenate(
+        [jnp.where(core == 0, one, two), jnp.where(core == 0, two, one)], axis=0
+    )
 
 
 def first_kernel(
-    held_ref, high_ref, low_ref, down_ref, best_ref, row_ref, col_ref, high_o, low_o, spread_ref, total_ref
+    held_ref, high_ref, low_ref, down_ref, best_ref, row_ref, col_ref, total_ref, high_o, low_o, spread_ref
 ):
-    start = lax.axis_index("core") * high_o.shape[0]
-    row_ref[...], col_ref[...] = cross(
-        held_ref, high_ref, low_ref, down_ref, start, high_o, low_o, spread_ref, best_ref, total_ref
-    )
-
-
-def second_kernel(
-    held_ref, high_ref, low_ref, down_ref, best_ref, row_ref, col_ref, out_ref, high_o, low_o, spread_ref, total_ref
-):
+    half = high_o.shape[0]
     core = lax.axis_index("core")
-    rows, cols = cross(
+    shared = [core * TILE, (1 - core) * TILE]
+    done = {}
+
+    def get(i, j):
+        if i == 2:
+            return best_ref[pl.ds(pl.multiple_of(shared[j], TILE), TILE), :]
+        at = i * TILE
+        return best_ref[half + at : half + at + TILE, :] if j == 0 else total_ref[at : at + TILE, :]
+
+    def put(i, j, best):
+        if i == 2:
+            done[j] = best
+        else:
+            total_ref[i * TILE : (i + 1) * TILE, :] = best
+
+    col_ref[...] = cross(
         held_ref,
         high_ref,
         low_ref,
         down_ref,
-        (1 - core) * high_o.shape[0],
+        lambda j: [half, half + TILE, shared[j]],
         high_o,
         low_o,
         spread_ref,
-        best_ref,
-        total_ref,
-    )
+        get,
+        put,
+    )
+    row_ref[...] = swapped(core, [done[0], done[1]])
+
+
+def second_kernel(
+    held_ref, high_ref, low_ref, down_ref, total_ref, row_ref, col_ref, out_ref, high_o, low_o, spread_ref
+):
+    half = high_o.shape[0]
+    core = lax.axis_index("core")
+    shared = [core * TILE, (1 - core) * TILE]
+    done = {}
+    cols = cross(
+        held_ref,
+        high_ref,
+        low_ref,
+        down_ref,
+        lambda j: [half + shared[j]],
+        high_o,
+        low_o,
+        spread_ref,
+        lambda i, j: total_ref[pl.ds(pl.multiple_of(shared[j], TILE), TILE), :],
+        lambda i, j, best: done.update({j: best}),
+    )
+    own = row_ref[...], swapped(core, [done[0], done[1]])
+    other = col_ref[...], cols
     chips = out_ref.shape[0] // 4
-    first = core == 0
-    own = jnp.where(first, row_ref[...], rows), jnp.where(first, rows, row_ref[...])
-    other = col_ref[...], cols
     for h in range(2):
-        out_ref[h * chips : (h + 1) * chips, :] = jnp.where(first, own[h], other[h])
-        out_ref[(2 + h) * chips : (3 + h) * chips, :] = jnp.where(first, other[h], own[h])
+        out_ref[h * chips : (h + 1) * chips, :] = jnp.where(core == 0, own[h], other[h])
+        out_ref[(2 + h) * chips : (3 + h) * chips, :] = jnp.where(core == 0, other[h], own[h])
 
 
 def pick_kernel(answer_ref, cl_ref, rank_ref, out_ref):
@@ -350,17 +385,17 @@
         pltpu.VMEM((half, width), jnp.bfloat16),
         pltpu.VMEM((half, width), jnp.bfloat16),
         pltpu.VMEM((half, lanes), jnp.float32),
-        pltpu.VMEM((half, lanes), jnp.float32),
     ]
-    cost = pl.CostEstimate(flops=flops // 4, bytes_accessed=2 << 20, transcendentals=0)
-    row, col = pl.pallas_call(
+    row, col, total = pl.pallas_call(
         first_kernel,
-        out_shape=(f32((chips // 2, lanes)),) * 2,
+        out_shape=(f32((chips // 2, lanes)), f32((chips // 2, lanes)), f32((half, lanes))),
         in_specs=[VMEM] * 5,
-        out_specs=(VMEM,) * 2,
+        out_specs=(VMEM,) * 3,
         scratch_shapes=scratch,
         compiler_params=PARAMS,
-        cost_estimate=cost,
+        cost_estimate=pl.CostEstimate(
+            flops=3 * flops // 8, bytes_accessed=2 << 20, transcendentals=0
+        ),
         name="first",
     )(arrived[0], high, low, down, best)
     result = pl.pallas_call(
@@ -370,9 +405,9 @@
         out_specs=VMEM,
         scratch_shapes=scratch,
         compiler_params=PARAMS,
-        cost_estimate=cost,
+        cost_estimate=pl.CostEstimate(flops=flops // 8, bytes_accessed=2 << 20, transcendentals=0),
         name="second",
-    )(arrived[1], high, low, down, best, row, col)
+    )(arrived[1], high, low, down, total, row, col)
     answer = lax.all_to_all(
         result.reshape(2 * chips, 1, lanes), ("core",) + chip_axes, split_axis=0, concat_axis=0, tiled=True
     ).reshape(2 * chips, lanes)

time: 79.7 us -> 79.6 us (level)
  no operation moved by 1% of the time
where the time goes in v7:
time: 79.6 us; the launch traced here: 79.5 us
  blocking collectives  65.6 us (82%)
  Pallas kernels  11.2 us (14%)
  starting transfers between devices  2.38 us (3%)
    all_to_all x1, blocking collectives, on_device(): lax.all_to_all(sending.reshape(chips * length, 1, lanes), chip_axes, spli...  52.2 us
    all_to_all x1, blocking collectives, on_device(): lax.all_to_all(result.reshape(2 * chips, 1, lanes), ('core',) + chip_axes...  13.4 us
    pallas_call x1, Pallas kernels, on_device(): pl.pallas_call(own_kernel, out_shape=(bf16((rows, width)), bf16((rows, wi...  3.48 us
    pallas_call x1, Pallas kernels, on_device(): pl.pallas_call(place_kernel, out_shape=(f32((chips * length, lanes)), jax...  3.41 us
    ppermute x2, starting transfers between devices, on_device(): lax.ppermute(held[h * part:(h + 1) * part], 'core', [(0, 1), (1, 0)])  2.38 us
    pallas_call x1, Pallas kernels, on_device(): pl.pallas_call(first_kernel, out_shape=(f32((chips // 2, lanes)), f32((ch...  2.34 us
  transfers between devices with their start and end apart: 2, of which 0 were waited for; matrix products, arithmetic and copies ran while one was open for 0% of the time, Pallas kernels for 7%

profile of v7, /device:TPU:1, one launch (start us, length us, event | category | flops | bytes accessed | tf_op | source)
XLA Modules:
  0.0 79.5 jit_solution(394238222816550033)
XLA Ops:
  0.0 3.4 %place.1 = (f32[6208,128]{1,0:T(8,128)S(1)}, s32[1,512]{1,0:T(1,128)S(1)}) custom-call(f32[512,768]{1,0:T(8,128)} %emb_hbm.1, s32[1,512]{1,0:T(1,128)} %bitcast.20, s32[1,512]{1,0:T(1,128)} %bitcast.23), custom_call_target="tpu_custom_call" | custom-call | tf_op jit(solution)/shard_map/place/pallas_call | solution.py:342
  3.4 52.2 %all_to_all.10 = f32[6208,1,128]{2,1,0:T(1,128)S(1)} all-to-all(f32[6208,1,128]{2,1,0:T(1,128)S(1)} %bitcast.16), channel_id=1, replica_groups=mesh['y'=4,'x_hi'=2,'core'=2,'x_lo'=2,'z'=4] {'z','y','x_hi','x_lo'}, dimensions={0} | all-to-all | bytes 6356992 | tf_op jit(solution)/shard_map/all_to_all | solution.py:358
  55.6 0.2 fusion
  55.8 2.3 %collective-permute-start.1 = (f32[3104,1,128]{2,0,1:T(8,128)S(1)}, f32[3104,1,128]{2,0,1:T(8,128)S(1)}, u32[]{:S(2)}, u32[]{:S(2)}) collective-permute-start(f32[3104,1,128]{2,0,1:T(8,128)S(1)} %get-tuple-element.23), channel_id=1, source_target_pairs={{0,8},{8,0},{1,9},{9,1},{2,10},{10,2},{3,11},{11,3},{4,12},{12,4},... | collective-permute-start | bytes 4767752 | tf_op jit(solution)/shard_map/ppermute | solution.py:363
  58.1 0.1 collective-permute-start
  58.2 3.5 %own.1 = (bf16[1024,768]{1,0:T(8,128)(2,1)S(1)}, bf16[1024,768]{1,0:T(8,128)(2,1)S(1)}, f32[1024,128]{1,0:T(8,128)S(1)}, f32[1024,128]{1,0:T(8,128)S(1)}) custom-call(f32[6208,128]{1,0:T(8,128)S(1)} %bitcast.15), custom_call_target="tpu_custom_call" | custom-call | flops 4831838208 | bytes 8388608 | tf_op jit(solution)/shard_map/own/pallas_call | solution.py:368
  61.7 0.0 collective-permute-done.1
  61.7 2.3 %first.1 = (f32[32,128]{1,0:T(8,128)S(1)}, f32[32,128]{1,0:T(8,128)S(1)}, f32[512,128]{1,0:T(8,128)S(1)}) custom-call(f32[3104,128]{1,0:T(8,128)S(1)} %bitcast.22, bf16[1024,768]{1,0:T(8,128)(2,1)S(1)} %get-tuple-element.15.high_ref, bf16[1024,768]{1,0:T(8,128)(2,1)S(1)} %get-tuple-element.16.low_ref, f32[1024,128]{1,0:T(8,128)S(1)} %get-tuple-element.17.down_ref, ...), custom_call_target="tpu_custom_call" | custom-call | flops 1811939328 | bytes 2097152 | tf_op jit(solution)/shard_map/first/pallas_call | solution.py:389
  64.1 0.0 collective-permute-done
  64.1 0.0 copy-start
  64.1 1.1 %second.1 = f32[128,128]{1,0:T(8,128)S(1)} custom-call(f32[3104,128]{1,0:T(8,128)S(1)} %bitcast.17, bf16[1024,768]{1,0:T(8,128)(2,1)S(1)} %get-tuple-element.15.high_ref, bf16[1024,768]{1,0:T(8,128)(2,1)S(1)} %get-tuple-element.16.low_ref, f32[1024,128]{1,0:T(8,128)S(1)} %get-tuple-element.17.down_ref, f32[512,128]{1,0:T(8,128)S(1)} %get-tuple-element.19.total_ref, ...), custom_call_target="tpu_custom_call" | custom-call | flops 603979776 | bytes 2097152 | tf_op jit(solution)/shard_map/second/pallas_call | solution.py:401
  65.2 13.4 %all_to_all.11 = f32[128,1,128]{2,1,0:T(1,128)S(1)} all-to-all(f32[128,1,128]{2,1,0:T(1,128)S(1)} %bitcast.18), channel_id=1, replica_groups=mesh['y'=4,'x_hi'=2,'core'=2,'x_lo'=2,'z'=4] {'core','z','y','x_hi','x_lo'}, dimensions={0} | all-to-all | bytes 131072 | tf_op jit(solution)/shard_map/all_to_all | solution.py:411
  78.6 0.0 copy-done
  78.6 0.9 %pick.1 = f32[1,512]{1,0:T(1,128)} custom-call(f32[128,128]{1,0:T(8,128)S(1)} %bitcast.19, s32[1,512]{1,0:T(1,128)S(1)} %bitcast.21, s32[1,512]{1,0:T(1,128)S(1)} %get-tuple-element.22.rank_ref), custom_call_target="tpu_custom_call" | custom-call | tf_op jit(solution)/shard_map/pick/pallas_call | solution.py:414
Async XLA Ops:
  55.8 5.9 %collective-permute-start.1 = (f32[3104,1,128]{2,0,1:T(8,128)S(1)}, f32[3104,1,128]{2,0,1:T(8,128)S(1)}, u32[]{:S(2)}, u32[]{:S(2)}) collective-permute-start(f32[3104,1,128]{2,0,1:T(8,128)S(1)} %get-tuple-element.23), channel_id=1, source_target_pairs={{0,8},{8,0},{1,9},{9,1},{2,10},{10,2},{3,11},{11,3},{4,12},{12,4},... | collective-permute-start | bytes 4767752 | tf_op jit(solution)/shard_map/ppermute | solution.py:363
  58.1 5.9 %collective-permute-start = (f32[3104,1,128]{2,0,1:T(8,128)S(1)}, f32[3104,1,128]{2,0,1:T(8,128)S(1)}, u32[]{:S(2)}, u32[]{:S(2)}) collective-permute-start(f32[3104,1,128]{2,0,1:T(8,128)S(1)} %get-tuple-element.24), channel_id=1, source_target_pairs={{0,8},{8,0},{1,9},{9,1},{2,10},{10,2},{3,11},{11,3},{4,12},{12,4},... | collective-permute-start | bytes 4767752 | tf_op jit(solution)/shard_map/ppermute | solution.py:363
  64.1 14.5 %copy-start = (s32[512]{0:T(512)S(1)}, s32[512]{0:T(512)}, u32[]{:S(2)}) copy-start(s32[512]{0:T(512)} %param.4) | copy-start | bytes 6148

commit v8 on v7

--- a/solution.py
+++ b/solution.py
@@ -177,26 +177,27 @@
         unpack(held_ref, j // 16, TILE // 16, high_ref, low_ref, spread_ref)
         down_j = tags_of(spread_ref[sj, :], slot)
         down_ref[sj, :] = down_j
-        best_ref[sj, :] = jnp.full((TILE, lanes), -1.0, jnp.float32)
-        end = j + TILE
-        sims = products(high_ref[:end, :], low_ref[:end, :], high_ref[sj, :], low_ref[sj, :])
-        down = down_ref[:end, :]
-        best = best_ref[:end, :]
-        over = []
-        for c in range(0, TILE, lanes):
-            col_ix = down_j[c : c + lanes, :].T[:1, :]
-            part = sims[:, c : c + lanes]
-            best = jnp.maximum(best, jnp.where(col_ix < down, part, -1.0))
-            if j > 0:
-                top = jnp.max(
-                    jnp.where(down[:j] < col_ix, part[:j], -1.0), axis=0, keepdims=True
-                )
+        cols = [down_j[c : c + lanes, :].T[:1, :] for c in range(0, TILE, lanes)]
+        high_j, low_j = high_ref[sj, :], low_ref[sj, :]
+        mixed = dot_f32(high_j, low_j, NT)
+        square = dot_f32(high_j, high_j, NT) + (mixed + mixed.T)
+        best_j = jnp.full((TILE, lanes), -1.0, jnp.float32)
+        for n, col_ix in enumerate(cols):
+            part = square[:, n * lanes : (n + 1) * lanes]
+            best_j = jnp.maximum(best_j, jnp.where(col_ix < down_j, part, -1.0))
+        if j > 0:
+            sims = products(high_ref[:j, :], low_ref[:j, :], high_j, low_j)
+            down = down_ref[:j, :]
+            best = best_ref[:j, :]
+            over = []
+            for n, col_ix in enumerate(cols):
+                part = sims[:, n * lanes : (n + 1) * lanes]
+                best = jnp.maximum(best, jnp.where(col_ix < down, part, -1.0))
+                top = jnp.max(jnp.where(down < col_ix, part, -1.0), axis=0, keepdims=True)
                 over.append(jnp.broadcast_to(top, (lanes, lanes)).T)
-        if j > 0:
-            best_ref[:j, :] = best[:j]
-            best_ref[sj, :] = jnp.maximum(best[j:], jnp.concatenate(over, axis=0))
-        else:
-            best_ref[sj, :] = best
+            best_ref[:j, :] = best
+            best_j = jnp.maximum(best_j, jnp.concatenate(over, axis=0))
+        best_ref[sj, :] = best_j
 
 
 def cross(held_ref, high_ref, low_ref, down_ref, parts, high_o, low_o, spread_ref, get, put):

time: 79.6 us -> 79.3 us (level)
  no operation moved by 1% of the time
where the time goes in v8:
time: 79.3 us; the launch traced here: 79.1 us
  blocking collectives  65.6 us (83%)
  Pallas kernels  10.9 us (14%)
  starting transfers between devices  2.38 us (3%)
    all_to_all x1, blocking collectives, on_device(): lax.all_to_all(sending.reshape(chips * length, 1, lanes), chip_axes, spli...  52.2 us
    all_to_all x1, blocking collectives, on_device(): lax.all_to_all(result.reshape(2 * chips, 1, lanes), ('core',) + chip_axes...  13.4 us
    pallas_call x1, Pallas kernels, on_device(): pl.pallas_call(place_kernel, out_shape=(f32((chips * length, lanes)), jax...  3.41 us
    pallas_call x1, Pallas kernels, on_device(): pl.pallas_call(own_kernel, out_shape=(bf16((rows, width)), bf16((rows, wi...  3.13 us
    ppermute x2, starting transfers between devices, on_device(): lax.ppermute(held[h * part:(h + 1) * part], 'core', [(0, 1), (1, 0)])  2.38 us
    pallas_call x1, Pallas kernels, on_device(): pl.pallas_call(first_kernel, out_shape=(f32((chips // 2, lanes)), f32((ch...  2.33 us
  transfers between devices with their start and end apart: 2, of which 0 were waited for; matrix products, arithmetic and copies ran while one was open for 0% of the time, Pallas kernels for 7%

profile of v8, /device:TPU:1, one launch (start us, length us, event | category | flops | bytes accessed | tf_op | source)
XLA Modules:
  0.0 79.1 jit_solution(14823323983923647767)
XLA Ops:
  0.0 3.4 %place.1 = (f32[6208,128]{1,0:T(8,128)S(1)}, s32[1,512]{1,0:T(1,128)S(1)}) custom-call(f32[512,768]{1,0:T(8,128)} %emb_hbm.1, s32[1,512]{1,0:T(1,128)} %bitcast.20, s32[1,512]{1,0:T(1,128)} %bitcast.23), custom_call_target="tpu_custom_call" | custom-call | tf_op jit(solution)/shard_map/place/pallas_call | solution.py:343
  3.4 52.2 %all_to_all.10 = f32[6208,1,128]{2,1,0:T(1,128)S(1)} all-to-all(f32[6208,1,128]{2,1,0:T(1,128)S(1)} %bitcast.16), channel_id=1, replica_groups=mesh['y'=4,'x_hi'=2,'core'=2,'x_lo'=2,'z'=4] {'z','y','x_hi','x_lo'}, dimensions={0} | all-to-all | bytes 6356992 | tf_op jit(solution)/shard_map/all_to_all | solution.py:359
  55.6 0.2 fusion
  55.8 2.3 %collective-permute-start.1 = (f32[3104,1,128]{2,0,1:T(8,128)S(1)}, f32[3104,1,128]{2,0,1:T(8,128)S(1)}, u32[]{:S(2)}, u32[]{:S(2)}) collective-permute-start(f32[3104,1,128]{2,0,1:T(8,128)S(1)} %get-tuple-element.23), channel_id=1, source_target_pairs={{0,8},{8,0},{1,9},{9,1},{2,10},{10,2},{3,11},{11,3},{4,12},{12,4},... | collective-permute-start | bytes 4767752 | tf_op jit(solution)/shard_map/ppermute | solution.py:364
  58.1 0.1 collective-permute-start
  58.2 3.1 %own.1 = (bf16[1024,768]{1,0:T(8,128)(2,1)S(1)}, bf16[1024,768]{1,0:T(8,128)(2,1)S(1)}, f32[1024,128]{1,0:T(8,128)S(1)}, f32[1024,128]{1,0:T(8,128)S(1)}) custom-call(f32[6208,128]{1,0:T(8,128)S(1)} %bitcast.15), custom_call_target="tpu_custom_call" | custom-call | flops 4831838208 | bytes 8388608 | tf_op jit(solution)/shard_map/own/pallas_call | solution.py:369
  61.4 0.0 collective-permute-done.1
  61.4 2.3 %first.1 = (f32[32,128]{1,0:T(8,128)S(1)}, f32[32,128]{1,0:T(8,128)S(1)}, f32[512,128]{1,0:T(8,128)S(1)}) custom-call(f32[3104,128]{1,0:T(8,128)S(1)} %bitcast.22, bf16[1024,768]{1,0:T(8,128)(2,1)S(1)} %get-tuple-element.15.high_ref, bf16[1024,768]{1,0:T(8,128)(2,1)S(1)} %get-tuple-element.16.low_ref, f32[1024,128]{1,0:T(8,128)S(1)} %get-tuple-element.17.down_ref, ...), custom_call_target="tpu_custom_call" | custom-call | flops 1811939328 | bytes 2097152 | tf_op jit(solution)/shard_map/first/pallas_call | solution.py:390
  63.7 0.0 collective-permute-done
  63.7 0.0 copy-start
  63.7 1.1 %second.1 = f32[128,128]{1,0:T(8,128)S(1)} custom-call(f32[3104,128]{1,0:T(8,128)S(1)} %bitcast.17, bf16[1024,768]{1,0:T(8,128)(2,1)S(1)} %get-tuple-element.15.high_ref, bf16[1024,768]{1,0:T(8,128)(2,1)S(1)} %get-tuple-element.16.low_ref, f32[1024,128]{1,0:T(8,128)S(1)} %get-tuple-element.17.down_ref, f32[512,128]{1,0:T(8,128)S(1)} %get-tuple-element.19.total_ref, ...), custom_call_target="tpu_custom_call" | custom-call | flops 603979776 | bytes 2097152 | tf_op jit(solution)/shard_map/second/pallas_call | solution.py:402
  64.8 13.4 %all_to_all.11 = f32[128,1,128]{2,1,0:T(1,128)S(1)} all-to-all(f32[128,1,128]{2,1,0:T(1,128)S(1)} %bitcast.18), channel_id=1, replica_groups=mesh['y'=4,'x_hi'=2,'core'=2,'x_lo'=2,'z'=4] {'core','z','y','x_hi','x_lo'}, dimensions={0} | all-to-all | bytes 131072 | tf_op jit(solution)/shard_map/all_to_all | solution.py:412
  78.2 0.0 copy-done
  78.2 0.9 %pick.1 = f32[1,512]{1,0:T(1,128)} custom-call(f32[128,128]{1,0:T(8,128)S(1)} %bitcast.19, s32[1,512]{1,0:T(1,128)S(1)} %bitcast.21, s32[1,512]{1,0:T(1,128)S(1)} %get-tuple-element.22.rank_ref), custom_call_target="tpu_custom_call" | custom-call | tf_op jit(solution)/shard_map/pick/pallas_call | solution.py:415
Async XLA Ops:
  55.8 5.5 %collective-permute-start.1 = (f32[3104,1,128]{2,0,1:T(8,128)S(1)}, f32[3104,1,128]{2,0,1:T(8,128)S(1)}, u32[]{:S(2)}, u32[]{:S(2)}) collective-permute-start(f32[3104,1,128]{2,0,1:T(8,128)S(1)} %get-tuple-element.23), channel_id=1, source_target_pairs={{0,8},{8,0},{1,9},{9,1},{2,10},{10,2},{3,11},{11,3},{4,12},{12,4},... | collective-permute-start | bytes 4767752 | tf_op jit(solution)/shard_map/ppermute | solution.py:364
  58.1 5.6 %collective-permute-start = (f32[3104,1,128]{2,0,1:T(8,128)S(1)}, f32[3104,1,128]{2,0,1:T(8,128)S(1)}, u32[]{:S(2)}, u32[]{:S(2)}) collective-permute-start(f32[3104,1,128]{2,0,1:T(8,128)S(1)} %get-tuple-element.24), channel_id=1, source_target_pairs={{0,8},{8,0},{1,9},{9,1},{2,10},{10,2},{3,11},{11,3},{4,12},{12,4},... | collective-permute-start | bytes 4767752 | tf_op jit(solution)/shard_map/ppermute | solution.py:364
  63.7 14.5 %copy-start = (s32[512]{0:T(512)S(1)}, s32[512]{0:T(512)}, u32[]{:S(2)}) copy-start(s32[512]{0:T(512)} %param.4) | copy-start | bytes 6148

commit v9 on v8

--- a/solution.py
+++ b/solution.py
@@ -78,13 +78,13 @@
     mm = (((1,), (0,)), ((), ()))
     chunks = width // lanes
     sub = lax.broadcasted_iota(jnp.int32, (8, lanes), 0)
-    block = 2 * turn * slots
+    block = 8 * turn * slots
     for r in range(0, chips * slots, block):
         place = (
             lax.broadcasted_iota(jnp.int32, (block, count), 0) + r == target
         ).astype(jnp.float32).astype(jnp.bfloat16)
         moved = dot_f32(place, high, mm) + dot_f32(place, low, mm)
-        for g in range(2):
+        for g in range(8):
             base = (r // slots + g * turn) * (chunks * slots + 1)
 
             def head(a, k):
@@ -211,7 +211,7 @@
         for n, col_ix in enumerate(cols[j]):
             part = sims[:, n * lanes : (n + 1) * lanes]
             best = jnp.maximum(best, jnp.where(col_ix < down, part, -1.0))
-            top = jnp.where(down < col_ix, part, -1.0).reshape(TILE // 8, 8, lanes)
+            top = jnp.where(down < col_ix, part, -1.0).reshape(part.shape[0] // 8, 8, lanes)
             top = jnp.max(top, axis=0)
             over[j, n] = top if (j, n) not in over else jnp.maximum(over[j, n], top)
         put(i, j, best)
@@ -222,8 +222,8 @@
         unpack(held_ref, sj.start // 16, TILE // 16, high_o, low_o, spread_ref)
         down_j = tags_of(spread_ref[sj, :], slot)
         cols[j] = [down_j[c : c + lanes, :].T[:1, :] for c in range(0, TILE, lanes)]
-        for i, start in enumerate(parts(j)):
-            rows = pl.ds(pl.multiple_of(start, TILE), TILE)
+        for i, (start, size) in enumerate(parts(j)):
+            rows = pl.ds(pl.multiple_of(start, TILE), size)
             sims = products(high_ref[rows, :], low_ref[rows, :], high_o[sj, :], low_o[sj, :])
             if waiting is not None:
                 finish(*waiting)
@@ -260,23 +260,22 @@
     done = {}
 
     def get(i, j):
-        if i == 2:
+        if i == 1:
             return best_ref[pl.ds(pl.multiple_of(shared[j], TILE), TILE), :]
-        at = i * TILE
-        return best_ref[half + at : half + at + TILE, :] if j == 0 else total_ref[at : at + TILE, :]
+        return best_ref[half:, :] if j == 0 else total_ref[...]
 
     def put(i, j, best):
-        if i == 2:
+        if i == 1:
             done[j] = best
         else:
-            total_ref[i * TILE : (i + 1) * TILE, :] = best
+            total_ref[...] = best
 
     col_ref[...] = cross(
         held_ref,
         high_ref,
         low_ref,
         down_ref,
-        lambda j: [half, half + TILE, shared[j]],
+        lambda j: [(half, half), (shared[j], TILE)],
         high_o,
         low_o,
         spread_ref,
@@ -298,7 +297,7 @@
         high_ref,
         low_ref,
         down_ref,
-        lambda j: [half + shared[j]],
+        lambda j: [(half + shared[j], TILE)],
         high_o,
         low_o,
         spread_ref,

time: 79.3 us -> 79.2 us (level)
  no operation moved by 1% of the time
where the time goes in v9:
time: 79.2 us; the launch traced here: 79 us
  blocking collectives  65.6 us (83%)
  Pallas kernels  10.8 us (14%)
  starting transfers between devices  2.38 us (3%)
    all_to_all x1, blocking collectives, on_device(): lax.all_to_all(sending.reshape(chips * length, 1, lanes), chip_axes, spli...  52.2 us
    all_to_all x1, blocking collectives, on_device(): lax.all_to_all(result.reshape(2 * chips, 1, lanes), ('core',) + chip_axes...  13.4 us
    pallas_call x1, Pallas kernels, on_device(): pl.pallas_call(place_kernel, out_shape=(f32((chips * length, lanes)), jax...  3.34 us
    pallas_call x1, Pallas kernels, on_device(): pl.pallas_call(own_kernel, out_shape=(bf16((rows, width)), bf16((rows, wi...  3.13 us
    ppermute x2, starting transfers between devices, on_device(): lax.ppermute(held[h * part:(h + 1) * part], 'core', [(0, 1), (1, 0)])  2.38 us
    pallas_call x1, Pallas kernels, on_device(): pl.pallas_call(first_kernel, out_shape=(f32((chips // 2, lanes)), f32((ch...  2.31 us
  transfers between devices with their start and end apart: 2, of which 0 were waited for; matrix products, arithmetic and copies ran while one was open for 0% of the time, Pallas kernels for 7%

profile of v9, /device:TPU:1, one launch (start us, length us, event | category | flops | bytes accessed | tf_op | source)
XLA Modules:
  0.0 79.0 jit_solution(8058456273185521953)
XLA Ops:
  0.0 3.3 %place.1 = (f32[6208,128]{1,0:T(8,128)S(1)}, s32[1,512]{1,0:T(1,128)S(1)}) custom-call(f32[512,768]{1,0:T(8,128)} %emb_hbm.1, s32[1,512]{1,0:T(1,128)} %bitcast.20, s32[1,512]{1,0:T(1,128)} %bitcast.23), custom_call_target="tpu_custom_call" | custom-call | tf_op jit(solution)/shard_map/place/pallas_call | solution.py:342
  3.3 52.2 %all_to_all.10 = f32[6208,1,128]{2,1,0:T(1,128)S(1)} all-to-all(f32[6208,1,128]{2,1,0:T(1,128)S(1)} %bitcast.16), channel_id=1, replica_groups=mesh['y'=4,'x_hi'=2,'core'=2,'x_lo'=2,'z'=4] {'z','y','x_hi','x_lo'}, dimensions={0} | all-to-all | bytes 6356992 | tf_op jit(solution)/shard_map/all_to_all | solution.py:358
  55.6 0.2 fusion
  55.8 2.3 %collective-permute-start.1 = (f32[3104,1,128]{2,0,1:T(8,128)S(1)}, f32[3104,1,128]{2,0,1:T(8,128)S(1)}, u32[]{:S(2)}, u32[]{:S(2)}) collective-permute-start(f32[3104,1,128]{2,0,1:T(8,128)S(1)} %get-tuple-element.23), channel_id=1, source_target_pairs={{0,8},{8,0},{1,9},{9,1},{2,10},{10,2},{3,11},{11,3},{4,12},{12,4},... | collective-permute-start | bytes 4767752 | tf_op jit(solution)/shard_map/ppermute | solution.py:363
  58.1 0.1 collective-permute-start
  58.2 3.1 %own.1 = (bf16[1024,768]{1,0:T(8,128)(2,1)S(1)}, bf16[1024,768]{1,0:T(8,128)(2,1)S(1)}, f32[1024,128]{1,0:T(8,128)S(1)}, f32[1024,128]{1,0:T(8,128)S(1)}) custom-call(f32[6208,128]{1,0:T(8,128)S(1)} %bitcast.15), custom_call_target="tpu_custom_call" | custom-call | flops 4831838208 | bytes 8388608 | tf_op jit(solution)/shard_map/own/pallas_call | solution.py:368
  61.3 0.0 collective-permute-done.1
  61.3 2.3 %first.1 = (f32[32,128]{1,0:T(8,128)S(1)}, f32[32,128]{1,0:T(8,128)S(1)}, f32[512,128]{1,0:T(8,128)S(1)}) custom-call(f32[3104,128]{1,0:T(8,128)S(1)} %bitcast.22, bf16[1024,768]{1,0:T(8,128)(2,1)S(1)} %get-tuple-element.15.high_ref, bf16[1024,768]{1,0:T(8,128)(2,1)S(1)} %get-tuple-element.16.low_ref, f32[1024,128]{1,0:T(8,128)S(1)} %get-tuple-element.17.down_ref, ...), custom_call_target="tpu_custom_call" | custom-call | flops 1811939328 | bytes 2097152 | tf_op jit(solution)/shard_map/first/pallas_call | solution.py:389
  63.6 0.0 collective-permute-done
  63.6 0.0 copy-start
  63.6 1.1 %second.1 = f32[128,128]{1,0:T(8,128)S(1)} custom-call(f32[3104,128]{1,0:T(8,128)S(1)} %bitcast.17, bf16[1024,768]{1,0:T(8,128)(2,1)S(1)} %get-tuple-element.15.high_ref, bf16[1024,768]{1,0:T(8,128)(2,1)S(1)} %get-tuple-element.16.low_ref, f32[1024,128]{1,0:T(8,128)S(1)} %get-tuple-element.17.down_ref, f32[512,128]{1,0:T(8,128)S(1)} %get-tuple-element.19.total_ref, ...), custom_call_target="tpu_custom_call" | custom-call | flops 603979776 | bytes 2097152 | tf_op jit(solution)/shard_map/second/pallas_call | solution.py:401
  64.7 13.4 %all_to_all.11 = f32[128,1,128]{2,1,0:T(1,128)S(1)} all-to-all(f32[128,1,128]{2,1,0:T(1,128)S(1)} %bitcast.18), channel_id=1, replica_groups=mesh['y'=4,'x_hi'=2,'core'=2,'x_lo'=2,'z'=4] {'core','z','y','x_hi','x_lo'}, dimensions={0} | all-to-all | bytes 131072 | tf_op jit(solution)/shard_map/all_to_all | solution.py:411
  78.1 0.0 copy-done
  78.1 0.9 %pick.1 = f32[1,512]{1,0:T(1,128)} custom-call(f32[128,128]{1,0:T(8,128)S(1)} %bitcast.19, s32[1,512]{1,0:T(1,128)S(1)} %bitcast.21, s32[1,512]{1,0:T(1,128)S(1)} %get-tuple-element.22.rank_ref), custom_call_target="tpu_custom_call" | custom-call | tf_op jit(solution)/shard_map/pick/pallas_call | solution.py:414
Async XLA Ops:
  55.8 5.5 %collective-permute-start.1 = (f32[3104,1,128]{2,0,1:T(8,128)S(1)}, f32[3104,1,128]{2,0,1:T(8,128)S(1)}, u32[]{:S(2)}, u32[]{:S(2)}) collective-permute-start(f32[3104,1,128]{2,0,1:T(8,128)S(1)} %get-tuple-element.23), channel_id=1, source_target_pairs={{0,8},{8,0},{1,9},{9,1},{2,10},{10,2},{3,11},{11,3},{4,12},{12,4},... | collective-permute-start | bytes 4767752 | tf_op jit(solution)/shard_map/ppermute | solution.py:363
  58.1 5.6 %collective-permute-start = (f32[3104,1,128]{2,0,1:T(8,128)S(1)}, f32[3104,1,128]{2,0,1:T(8,128)S(1)}, u32[]{:S(2)}, u32[]{:S(2)}) collective-permute-start(f32[3104,1,128]{2,0,1:T(8,128)S(1)} %get-tuple-element.24), channel_id=1, source_target_pairs={{0,8},{8,0},{1,9},{9,1},{2,10},{10,2},{3,11},{11,3},{4,12},{12,4},... | collective-permute-start | bytes 4767752 | tf_op jit(solution)/shard_map/ppermute | solution.py:363
  63.6 14.5 %copy-start = (s32[512]{0:T(512)S(1)}, s32[512]{0:T(512)}, u32[]{:S(2)}) copy-start(s32[512]{0:T(512)} %param.4) | copy-start | bytes 6148

commit v10 on v9

--- a/solution.py
+++ b/solution.py
@@ -306,10 +306,13 @@
     )
     own = row_ref[...], swapped(core, [done[0], done[1]])
     other = col_ref[...], cols
-    chips = out_ref.shape[0] // 4
+    layer = out_ref.shape[0] // 8
     for h in range(2):
-        out_ref[h * chips : (h + 1) * chips, :] = jnp.where(core == 0, own[h], other[h])
-        out_ref[(2 + h) * chips : (3 + h) * chips, :] = jnp.where(core == 0, other[h], own[h])
+        for z in range(2):
+            mine, its = (v[h][z * layer : (z + 1) * layer, :] for v in (own, other))
+            at = 2 * layer * (2 * h + z)
+            out_ref[at : at + layer, :] = jnp.where(core == 0, mine, its)
+            out_ref[at + layer : at + 2 * layer, :] = jnp.where(core == 0, its, mine)
 
 
 def pick_kernel(answer_ref, cl_ref, rank_ref, out_ref):
@@ -320,7 +323,8 @@
         jnp.float32
     ).astype(jnp.bfloat16)
     tn = (((0,), (0,)), ((), ()))
-    answer = jnp.maximum(answer_ref[:chips, :], answer_ref[chips:, :])
+    answer = jnp.max(answer_ref[...].reshape(4, 2, chips // 4, lanes), axis=1)
+    answer = answer.reshape(chips, lanes)
     high, rest = split(answer)
     middle, low = split(answer - high.astype(jnp.float32))
     by_rank = dot_f32(high, owner, tn) + (dot_f32(middle, owner, tn) + dot_f32(low, owner, tn))
@@ -409,7 +413,7 @@
         name="second",
     )(arrived[1], high, low, down, total, row, col)
     answer = lax.all_to_all(
-        result.reshape(2 * chips, 1, lanes), ("core",) + chip_axes, split_axis=0, concat_axis=0, tiled=True
+        result.reshape(2 * chips, 1, lanes), chip_axes[:1] + ("core",) + chip_axes[1:], split_axis=0, concat_axis=0, tiled=True
     ).reshape(2 * chips, lanes)
     out = pl.pallas_call(
         pick_kernel,

time: 79.2 us -> 79.3 us (level)
  no operation moved by 1% of the time
where the time goes in v10:
time: 79.3 us; the launch traced here: 79.1 us
  blocking collectives  65.7 us (83%)
  Pallas kernels  10.8 us (14%)
  starting transfers between devices  2.38 us (3%)
    all_to_all x1, blocking collectives, on_device(): lax.all_to_all(sending.reshape(chips * length, 1, lanes), chip_axes, spli...  52.2 us
    all_to_all x1, blocking collectives, on_device(): lax.all_to_all(result.reshape(2 * chips, 1, lanes), chip_axes[:1] + ('cor...  13.5 us
    pallas_call x1, Pallas kernels, on_device(): pl.pallas_call(place_kernel, out_shape=(f32((chips * length, lanes)), jax...  3.34 us
    pallas_call x1, Pallas kernels, on_device(): pl.pallas_call(own_kernel, out_shape=(bf16((rows, width)), bf16((rows, wi...  3.13 us
    ppermute x2, starting transfers between devices, on_device(): lax.ppermute(held[h * part:(h + 1) * part], 'core', [(0, 1), (1, 0)])  2.38 us
    pallas_call x1, Pallas kernels, on_device(): pl.pallas_call(first_kernel, out_shape=(f32((chips // 2, lanes)), f32((ch...  2.31 us
  transfers between devices with their start and end apart: 2, of which 0 were waited for; matrix products, arithmetic and copies ran while one was open for 0% of the time, Pallas kernels for 7%

profile of v10, /device:TPU:1, one launch (start us, length us, event | category | flops | bytes accessed | tf_op | source)
XLA Modules:
  0.0 79.1 jit_solution(1333174125988309513)
XLA Ops:
  0.0 3.3 %place.1 = (f32[6208,128]{1,0:T(8,128)S(1)}, s32[1,512]{1,0:T(1,128)S(1)}) custom-call(f32[512,768]{1,0:T(8,128)} %emb_hbm.1, s32[1,512]{1,0:T(1,128)} %bitcast.20, s32[1,512]{1,0:T(1,128)} %bitcast.23), custom_call_target="tpu_custom_call" | custom-call | tf_op jit(solution)/shard_map/place/pallas_call | solution.py:346
  3.3 52.2 %all_to_all.10 = f32[6208,1,128]{2,1,0:T(1,128)S(1)} all-to-all(f32[6208,1,128]{2,1,0:T(1,128)S(1)} %bitcast.16), channel_id=1, replica_groups=mesh['y'=4,'x_hi'=2,'core'=2,'x_lo'=2,'z'=4] {'z','y','x_hi','x_lo'}, dimensions={0} | all-to-all | bytes 6356992 | tf_op jit(solution)/shard_map/all_to_all | solution.py:362
  55.6 0.2 fusion
  55.8 2.3 %collective-permute-start.1 = (f32[3104,1,128]{2,0,1:T(8,128)S(1)}, f32[3104,1,128]{2,0,1:T(8,128)S(1)}, u32[]{:S(2)}, u32[]{:S(2)}) collective-permute-start(f32[3104,1,128]{2,0,1:T(8,128)S(1)} %get-tuple-element.23), channel_id=1, source_target_pairs={{0,8},{8,0},{1,9},{9,1},{2,10},{10,2},{3,11},{11,3},{4,12},{12,4},... | collective-permute-start | bytes 4767752 | tf_op jit(solution)/shard_map/ppermute | solution.py:367
  58.1 0.1 collective-permute-start
  58.2 3.1 %own.1 = (bf16[1024,768]{1,0:T(8,128)(2,1)S(1)}, bf16[1024,768]{1,0:T(8,128)(2,1)S(1)}, f32[1024,128]{1,0:T(8,128)S(1)}, f32[1024,128]{1,0:T(8,128)S(1)}) custom-call(f32[6208,128]{1,0:T(8,128)S(1)} %bitcast.15), custom_call_target="tpu_custom_call" | custom-call | flops 4831838208 | bytes 8388608 | tf_op jit(solution)/shard_map/own/pallas_call | solution.py:372
  61.3 0.0 collective-permute-done.1
  61.3 2.3 %first.1 = (f32[32,128]{1,0:T(8,128)S(1)}, f32[32,128]{1,0:T(8,128)S(1)}, f32[512,128]{1,0:T(8,128)S(1)}) custom-call(f32[3104,128]{1,0:T(8,128)S(1)} %bitcast.22, bf16[1024,768]{1,0:T(8,128)(2,1)S(1)} %get-tuple-element.15.high_ref, bf16[1024,768]{1,0:T(8,128)(2,1)S(1)} %get-tuple-element.16.low_ref, f32[1024,128]{1,0:T(8,128)S(1)} %get-tuple-element.17.down_ref, ...), custom_call_target="tpu_custom_call" | custom-call | flops 1811939328 | bytes 2097152 | tf_op jit(solution)/shard_map/first/pallas_call | solution.py:393
  63.6 0.0 collective-permute-done
  63.6 0.0 copy-start
  63.6 1.1 %second.1 = f32[128,128]{1,0:T(8,128)S(1)} custom-call(f32[3104,128]{1,0:T(8,128)S(1)} %bitcast.17, bf16[1024,768]{1,0:T(8,128)(2,1)S(1)} %get-tuple-element.15.high_ref, bf16[1024,768]{1,0:T(8,128)(2,1)S(1)} %get-tuple-element.16.low_ref, f32[1024,128]{1,0:T(8,128)S(1)} %get-tuple-element.17.down_ref, f32[512,128]{1,0:T(8,128)S(1)} %get-tuple-element.19.total_ref, ...), custom_call_target="tpu_custom_call" | custom-call | flops 603979776 | bytes 2097152 | tf_op jit(solution)/shard_map/second/pallas_call | solution.py:405
  64.7 13.5 %all_to_all.11 = f32[128,1,128]{2,1,0:T(1,128)S(1)} all-to-all(f32[128,1,128]{2,1,0:T(1,128)S(1)} %bitcast.18), channel_id=1, replica_groups=mesh['y'=4,'x_hi'=2,'core'=2,'x_lo'=2,'z'=4] {'z','core','y','x_hi','x_lo'}, dimensions={0} | all-to-all | bytes 131072 | tf_op jit(solution)/shard_map/all_to_all | solution.py:415
  78.2 0.0 copy-done
  78.2 0.9 %pick.1 = f32[1,512]{1,0:T(1,128)} custom-call(f32[128,128]{1,0:T(8,128)S(1)} %bitcast.19, s32[1,512]{1,0:T(1,128)S(1)} %bitcast.21, s32[1,512]{1,0:T(1,128)S(1)} %get-tuple-element.22.rank_ref), custom_call_target="tpu_custom_call" | custom-call | tf_op jit(solution)/shard_map/pick/pallas_call | solution.py:418
Async XLA Ops:
  55.8 5.5 %collective-permute-start.1 = (f32[3104,1,128]{2,0,1:T(8,128)S(1)}, f32[3104,1,128]{2,0,1:T(8,128)S(1)}, u32[]{:S(2)}, u32[]{:S(2)}) collective-permute-start(f32[3104,1,128]{2,0,1:T(8,128)S(1)} %get-tuple-element.23), channel_id=1, source_target_pairs={{0,8},{8,0},{1,9},{9,1},{2,10},{10,2},{3,11},{11,3},{4,12},{12,4},... | collective-permute-start | bytes 4767752 | tf_op jit(solution)/shard_map/ppermute | solution.py:367
  58.1 5.6 %collective-permute-start = (f32[3104,1,128]{2,0,1:T(8,128)S(1)}, f32[3104,1,128]{2,0,1:T(8,128)S(1)}, u32[]{:S(2)}, u32[]{:S(2)}) collective-permute-start(f32[3104,1,128]{2,0,1:T(8,128)S(1)} %get-tuple-element.24), channel_id=1, source_target_pairs={{0,8},{8,0},{1,9},{9,1},{2,10},{10,2},{3,11},{11,3},{4,12},{12,4},... | collective-permute-start | bytes 4767752 | tf_op jit(solution)/shard_map/ppermute | solution.py:367
  63.6 14.6 %copy-start = (s32[512]{0:T(512)S(1)}, s32[512]{0:T(512)}, u32[]{:S(2)}) copy-start(s32[512]{0:T(512)} %param.4) | copy-start | bytes 6148

commit v11 on v9

--- a/solution.py
+++ b/solution.py
@@ -359,9 +359,10 @@
         sending.reshape(chips * length, 1, lanes), chip_axes, split_axis=0, concat_axis=0, tiled=True
     )
     part = chips * length // 2
+    swap = [(0, 1), (1, 0)]
+    half_1, later = lax.optimization_barrier((held[:part], held))
     arrived = [
-        lax.ppermute(held[h * part : (h + 1) * part], "core", [(0, 1), (1, 0)]).reshape(part, lanes)
-        for h in range(2)
+        lax.ppermute(half, "core", swap).reshape(part, lanes) for half in (half_1, later[part:])
     ]
     held = held.reshape(chips * length, lanes)
     flops = 2 * rows * rows * width * 3

time: 79.2 us -> 79.3 us (level)
  no operation moved by 1% of the time
where the time goes in v11:
time: 79.3 us; the launch traced here: 79.1 us
  blocking collectives  65.7 us (83%)
  Pallas kernels  10.8 us (14%)
  starting transfers between devices  2.39 us (3%)
    all_to_all x1, blocking collectives, on_device(): lax.all_to_all(sending.reshape(chips * length, 1, lanes), chip_axes, spli...  52.2 us
    all_to_all x1, blocking collectives, on_device(): lax.all_to_all(result.reshape(2 * chips, 1, lanes), ('core',) + chip_axes...  13.5 us
    pallas_call x1, Pallas kernels, on_device(): pl.pallas_call(place_kernel, out_shape=(f32((chips * length, lanes)), jax...  3.34 us
    pallas_call x1, Pallas kernels, on_device(): pl.pallas_call(own_kernel, out_shape=(bf16((rows, width)), bf16((rows, wi...  3.13 us
    ppermute x2, starting transfers between devices, on_device(): lax.ppermute(half, 'core', swap).reshape(part, lanes)  2.39 us
    pallas_call x1, Pallas kernels, on_device(): pl.pallas_call(first_kernel, out_shape=(f32((chips // 2, lanes)), f32((ch...  2.31 us
  transfers between devices with their start and end apart: 2, of which 0 were waited for; matrix products, arithmetic and copies ran while one was open for 0% of the time, Pallas kernels for 7%

profile of v11, /device:TPU:1, one launch (start us, length us, event | category | flops | bytes accessed | tf_op | source)
XLA Modules:
  0.0 79.1 jit_solution(2131370443493889471)
XLA Ops:
  0.0 3.3 %place.1 = (f32[6208,128]{1,0:T(8,128)S(1)}, s32[1,512]{1,0:T(1,128)S(1)}) custom-call(f32[512,768]{1,0:T(8,128)} %emb_hbm.1, s32[1,512]{1,0:T(1,128)} %bitcast.22, s32[1,512]{1,0:T(1,128)} %bitcast.25), custom_call_target="tpu_custom_call" | custom-call | tf_op jit(solution)/shard_map/place/pallas_call | solution.py:342
  3.3 52.2 %all_to_all.10 = f32[6208,1,128]{2,1,0:T(1,128)S(1)} all-to-all(f32[6208,1,128]{2,1,0:T(1,128)S(1)} %bitcast.18), channel_id=1, replica_groups=mesh['y'=4,'x_hi'=2,'core'=2,'x_lo'=2,'z'=4] {'z','y','x_hi','x_lo'}, dimensions={0} | all-to-all | bytes 6356992 | tf_op jit(solution)/shard_map/all_to_all | solution.py:358
  55.6 0.1 slice.8
  55.7 2.3 %collective-permute-start.1 = (f32[3104,1,128]{2,0,1:T(8,128)S(1)}, f32[3104,1,128]{2,0,1:T(8,128)S(1)}, u32[]{:S(2)}, u32[]{:S(2)}) collective-permute-start(f32[3104,1,128]{2,0,1:T(8,128)S(1)} %slice.8), channel_id=1, source_target_pairs={{0,8},{8,0},{1,9},{9,1},{2,10},{10,2},{3,11},{11,3},{4,12},{12,4},... | collective-permute-start | bytes 4767752 | tf_op jit(solution)/shard_map/ppermute | solution.py:365
  58.0 0.1 slice.9
  58.1 0.1 collective-permute-start
  58.2 3.1 %own.1 = (bf16[1024,768]{1,0:T(8,128)(2,1)S(1)}, bf16[1024,768]{1,0:T(8,128)(2,1)S(1)}, f32[1024,128]{1,0:T(8,128)S(1)}, f32[1024,128]{1,0:T(8,128)S(1)}) custom-call(f32[6208,128]{1,0:T(8,128)S(1)} %bitcast.17), custom_call_target="tpu_custom_call" | custom-call | flops 4831838208 | bytes 8388608 | tf_op jit(solution)/shard_map/own/pallas_call | solution.py:369
  61.3 0.0 collective-permute-done.1
  61.3 2.3 %first.1 = (f32[32,128]{1,0:T(8,128)S(1)}, f32[32,128]{1,0:T(8,128)S(1)}, f32[512,128]{1,0:T(8,128)S(1)}) custom-call(f32[3104,128]{1,0:T(8,128)S(1)} %bitcast.24, bf16[1024,768]{1,0:T(8,128)(2,1)S(1)} %get-tuple-element.18.high_ref, bf16[1024,768]{1,0:T(8,128)(2,1)S(1)} %get-tuple-element.19.low_ref, f32[1024,128]{1,0:T(8,128)S(1)} %get-tuple-element.20.down_ref, ...), custom_call_target="tpu_custom_call" | custom-call | flops 1811939328 | bytes 2097152 | tf_op jit(solution)/shard_map/first/pallas_call | solution.py:390
  63.6 0.0 collective-permute-done
  63.6 0.0 copy-start
  63.6 1.1 %second.1 = f32[128,128]{1,0:T(8,128)S(1)} custom-call(f32[3104,128]{1,0:T(8,128)S(1)} %bitcast.19, bf16[1024,768]{1,0:T(8,128)(2,1)S(1)} %get-tuple-element.18.high_ref, bf16[1024,768]{1,0:T(8,128)(2,1)S(1)} %get-tuple-element.19.low_ref, f32[1024,128]{1,0:T(8,128)S(1)} %get-tuple-element.20.down_ref, f32[512,128]{1,0:T(8,128)S(1)} %get-tuple-element.23.total_ref, ...), custom_call_target="tpu_custom_call" | custom-call | flops 603979776 | bytes 2097152 | tf_op jit(solution)/shard_map/second/pallas_call | solution.py:402
  64.7 13.5 %all_to_all.11 = f32[128,1,128]{2,1,0:T(1,128)S(1)} all-to-all(f32[128,1,128]{2,1,0:T(1,128)S(1)} %bitcast.20), channel_id=1, replica_groups=mesh['y'=4,'x_hi'=2,'core'=2,'x_lo'=2,'z'=4] {'core','z','y','x_hi','x_lo'}, dimensions={0} | all-to-all | bytes 131072 | tf_op jit(solution)/shard_map/all_to_all | solution.py:412
  78.2 0.0 copy-done
  78.2 0.9 %pick.1 = f32[1,512]{1,0:T(1,128)} custom-call(f32[128,128]{1,0:T(8,128)S(1)} %bitcast.21, s32[1,512]{1,0:T(1,128)S(1)} %bitcast.23, s32[1,512]{1,0:T(1,128)S(1)} %get-tuple-element.26.rank_ref), custom_call_target="tpu_custom_call" | custom-call | tf_op jit(solution)/shard_map/pick/pallas_call | solution.py:415
Async XLA Ops:
  55.7 5.6 %collective-permute-start.1 = (f32[3104,1,128]{2,0,1:T(8,128)S(1)}, f32[3104,1,128]{2,0,1:T(8,128)S(1)}, u32[]{:S(2)}, u32[]{:S(2)}) collective-permute-start(f32[3104,1,128]{2,0,1:T(8,128)S(1)} %slice.8), channel_id=1, source_target_pairs={{0,8},{8,0},{1,9},{9,1},{2,10},{10,2},{3,11},{11,3},{4,12},{12,4},... | collective-permute-start | bytes 4767752 | tf_op jit(solution)/shard_map/ppermute | solution.py:365
  58.1 5.6 %collective-permute-start = (f32[3104,1,128]{2,0,1:T(8,128)S(1)}, f32[3104,1,128]{2,0,1:T(8,128)S(1)}, u32[]{:S(2)}, u32[]{:S(2)}) collective-permute-start(f32[3104,1,128]{2,0,1:T(8,128)S(1)} %slice.9), channel_id=1, source_target_pairs={{0,8},{8,0},{1,9},{9,1},{2,10},{10,2},{3,11},{11,3},{4,12},{12,4},... | collective-permute-start | bytes 4767752 | tf_op jit(solution)/shard_map/ppermute | solution.py:365
  63.6 14.6 %copy-start = (s32[512]{0:T(512)S(1)}, s32[512]{0:T(512)}, u32[]{:S(2)}) copy-start(s32[512]{0:T(512)} %param.4) | copy-start | bytes 6148

commit v12 on v9

--- a/solution.py
+++ b/solution.py
@@ -321,9 +321,8 @@
     ).astype(jnp.bfloat16)
     tn = (((0,), (0,)), ((), ()))
     answer = jnp.maximum(answer_ref[:chips, :], answer_ref[chips:, :])
-    high, rest = split(answer)
-    middle, low = split(answer - high.astype(jnp.float32))
-    by_rank = dot_f32(high, owner, tn) + (dot_f32(middle, owner, tn) + dot_f32(low, owner, tn))
+    high, low = split(answer)
+    by_rank = dot_f32(high, owner, tn) + dot_f32(low, owner, tn)
     at_rank = lax.broadcasted_iota(jnp.int32, (lanes, count), 0) == rank_ref[...]
     out_ref[...] = jnp.sum(jnp.where(at_rank, by_rank, 0.0), axis=0, keepdims=True)
 

time: 79.2 us -> 79.2 us (level)
  no operation moved by 1% of the time
where the time goes in v12:
time: 79.2 us; the launch traced here: 79 us
  blocking collectives  65.6 us (83%)
  Pallas kernels  10.7 us (14%)
  starting transfers between devices  2.38 us (3%)
    all_to_all x1, blocking collectives, on_device(): lax.all_to_all(sending.reshape(chips * length, 1, lanes), chip_axes, spli...  52.2 us
    all_to_all x1, blocking collectives, on_device(): lax.all_to_all(result.reshape(2 * chips, 1, lanes), ('core',) + chip_axes...  13.4 us
    pallas_call x1, Pallas kernels, on_device(): pl.pallas_call(place_kernel, out_shape=(f32((chips * length, lanes)), jax...  3.34 us
    pallas_call x1, Pallas kernels, on_device(): pl.pallas_call(own_kernel, out_shape=(bf16((rows, width)), bf16((rows, wi...  3.13 us
    ppermute x2, starting transfers between devices, on_device(): lax.ppermute(held[h * part:(h + 1) * part], 'core', [(0, 1), (1, 0)])  2.38 us
    pallas_call x1, Pallas kernels, on_device(): pl.pallas_call(first_kernel, out_shape=(f32((chips // 2, lanes)), f32((ch...  2.31 us
  transfers between devices with their start and end apart: 2, of which 0 were waited for; matrix products, arithmetic and copies ran while one was open for 0% of the time, Pallas kernels for 7%

profile of v12, /device:TPU:1, one launch (start us, length us, event | category | flops | bytes accessed | tf_op | source)
XLA Modules:
  0.0 79.0 jit_solution(13196694320618944996)
XLA Ops:
  0.0 3.3 %place.1 = (f32[6208,128]{1,0:T(8,128)S(1)}, s32[1,512]{1,0:T(1,128)S(1)}) custom-call(f32[512,768]{1,0:T(8,128)} %emb_hbm.1, s32[1,512]{1,0:T(1,128)} %bitcast.20, s32[1,512]{1,0:T(1,128)} %bitcast.23), custom_call_target="tpu_custom_call" | custom-call | tf_op jit(solution)/shard_map/place/pallas_call | solution.py:341
  3.3 52.2 %all_to_all.10 = f32[6208,1,128]{2,1,0:T(1,128)S(1)} all-to-all(f32[6208,1,128]{2,1,0:T(1,128)S(1)} %bitcast.16), channel_id=1, replica_groups=mesh['y'=4,'x_hi'=2,'core'=2,'x_lo'=2,'z'=4] {'z','y','x_hi','x_lo'}, dimensions={0} | all-to-all | bytes 6356992 | tf_op jit(solution)/shard_map/all_to_all | solution.py:357
  55.6 0.2 fusion
  55.8 2.3 %collective-permute-start.1 = (f32[3104,1,128]{2,0,1:T(8,128)S(1)}, f32[3104,1,128]{2,0,1:T(8,128)S(1)}, u32[]{:S(2)}, u32[]{:S(2)}) collective-permute-start(f32[3104,1,128]{2,0,1:T(8,128)S(1)} %get-tuple-element.23), channel_id=1, source_target_pairs={{0,8},{8,0},{1,9},{9,1},{2,10},{10,2},{3,11},{11,3},{4,12},{12,4},... | collective-permute-start | bytes 4767752 | tf_op jit(solution)/shard_map/ppermute | solution.py:362
  58.1 0.1 collective-permute-start
  58.2 3.1 %own.1 = (bf16[1024,768]{1,0:T(8,128)(2,1)S(1)}, bf16[1024,768]{1,0:T(8,128)(2,1)S(1)}, f32[1024,128]{1,0:T(8,128)S(1)}, f32[1024,128]{1,0:T(8,128)S(1)}) custom-call(f32[6208,128]{1,0:T(8,128)S(1)} %bitcast.15), custom_call_target="tpu_custom_call" | custom-call | flops 4831838208 | bytes 8388608 | tf_op jit(solution)/shard_map/own/pallas_call | solution.py:367
  61.3 0.0 collective-permute-done.1
  61.3 2.3 %first.1 = (f32[32,128]{1,0:T(8,128)S(1)}, f32[32,128]{1,0:T(8,128)S(1)}, f32[512,128]{1,0:T(8,128)S(1)}) custom-call(f32[3104,128]{1,0:T(8,128)S(1)} %bitcast.22, bf16[1024,768]{1,0:T(8,128)(2,1)S(1)} %get-tuple-element.15.high_ref, bf16[1024,768]{1,0:T(8,128)(2,1)S(1)} %get-tuple-element.16.low_ref, f32[1024,128]{1,0:T(8,128)S(1)} %get-tuple-element.17.down_ref, ...), custom_call_target="tpu_custom_call" | custom-call | flops 1811939328 | bytes 2097152 | tf_op jit(solution)/shard_map/first/pallas_call | solution.py:388
  63.6 0.0 collective-permute-done
  63.6 0.0 copy-start
  63.6 1.1 %second.1 = f32[128,128]{1,0:T(8,128)S(1)} custom-call(f32[3104,128]{1,0:T(8,128)S(1)} %bitcast.17, bf16[1024,768]{1,0:T(8,128)(2,1)S(1)} %get-tuple-element.15.high_ref, bf16[1024,768]{1,0:T(8,128)(2,1)S(1)} %get-tuple-element.16.low_ref, f32[1024,128]{1,0:T(8,128)S(1)} %get-tuple-element.17.down_ref, f32[512,128]{1,0:T(8,128)S(1)} %get-tuple-element.19.total_ref, ...), custom_call_target="tpu_custom_call" | custom-call | flops 603979776 | bytes 2097152 | tf_op jit(solution)/shard_map/second/pallas_call | solution.py:400
  64.7 13.4 %all_to_all.11 = f32[128,1,128]{2,1,0:T(1,128)S(1)} all-to-all(f32[128,1,128]{2,1,0:T(1,128)S(1)} %bitcast.18), channel_id=1, replica_groups=mesh['y'=4,'x_hi'=2,'core'=2,'x_lo'=2,'z'=4] {'core','z','y','x_hi','x_lo'}, dimensions={0} | all-to-all | bytes 131072 | tf_op jit(solution)/shard_map/all_to_all | solution.py:410
  78.1 0.0 copy-done
  78.1 0.8 %pick.1 = f32[1,512]{1,0:T(1,128)} custom-call(f32[128,128]{1,0:T(8,128)S(1)} %bitcast.19, s32[1,512]{1,0:T(1,128)S(1)} %bitcast.21, s32[1,512]{1,0:T(1,128)S(1)} %get-tuple-element.22.rank_ref), custom_call_target="tpu_custom_call" | custom-call | tf_op jit(solution)/shard_map/pick/pallas_call | solution.py:413
Async XLA Ops:
  55.8 5.5 %collective-permute-start.1 = (f32[3104,1,128]{2,0,1:T(8,128)S(1)}, f32[3104,1,128]{2,0,1:T(8,128)S(1)}, u32[]{:S(2)}, u32[]{:S(2)}) collective-permute-start(f32[3104,1,128]{2,0,1:T(8,128)S(1)} %get-tuple-element.23), channel_id=1, source_target_pairs={{0,8},{8,0},{1,9},{9,1},{2,10},{10,2},{3,11},{11,3},{4,12},{12,4},... | collective-permute-start | bytes 4767752 | tf_op jit(solution)/shard_map/ppermute | solution.py:362
  58.1 5.6 %collective-permute-start = (f32[3104,1,128]{2,0,1:T(8,128)S(1)}, f32[3104,1,128]{2,0,1:T(8,128)S(1)}, u32[]{:S(2)}, u32[]{:S(2)}) collective-permute-start(f32[3104,1,128]{2,0,1:T(8,128)S(1)} %get-tuple-element.24), channel_id=1, source_target_pairs={{0,8},{8,0},{1,9},{9,1},{2,10},{10,2},{3,11},{11,3},{4,12},{12,4},... | collective-permute-start | bytes 4767752 | tf_op jit(solution)/shard_map/ppermute | solution.py:362
  63.6 14.5 %copy-start = (s32[512]{0:T(512)S(1)}, s32[512]{0:T(512)}, u32[]{:S(2)}) copy-start(s32[512]{0:T(512)} %param.4) | copy-start | bytes 6148

commit v13 on v12

--- a/solution.py
+++ b/solution.py
@@ -322,7 +322,9 @@
     tn = (((0,), (0,)), ((), ()))
     answer = jnp.maximum(answer_ref[:chips, :], answer_ref[chips:, :])
     high, low = split(answer)
-    by_rank = dot_f32(high, owner, tn) + dot_f32(low, owner, tn)
+    by_rank = dot_f32(
+        jnp.concatenate([high, low], axis=0), jnp.concatenate([owner, owner], axis=0), tn
+    )
     at_rank = lax.broadcasted_iota(jnp.int32, (lanes, count), 0) == rank_ref[...]
     out_ref[...] = jnp.sum(jnp.where(at_rank, by_rank, 0.0), axis=0, keepdims=True)
 

time: 79.2 us -> 79.1 us (level)
  no operation moved by 1% of the time
where the time goes in v13:
time: 79.1 us; the launch traced here: 78.9 us
  blocking collectives  65.6 us (83%)
  Pallas kernels  10.7 us (14%)
  starting transfers between devices  2.38 us (3%)
    all_to_all x1, blocking collectives, on_device(): lax.all_to_all(sending.reshape(chips * length, 1, lanes), chip_axes, spli...  52.2 us
    all_to_all x1, blocking collectives, on_device(): lax.all_to_all(result.reshape(2 * chips, 1, lanes), ('core',) + chip_axes...  13.4 us
    pallas_call x1, Pallas kernels, on_device(): pl.pallas_call(place_kernel, out_shape=(f32((chips * length, lanes)), jax...  3.34 us
    pallas_call x1, Pallas kernels, on_device(): pl.pallas_call(own_kernel, out_shape=(bf16((rows, width)), bf16((rows, wi...  3.13 us
    ppermute x2, starting transfers between devices, on_device(): lax.ppermute(held[h * part:(h + 1) * part], 'core', [(0, 1), (1, 0)])  2.38 us
    pallas_call x1, Pallas kernels, on_device(): pl.pallas_call(first_kernel, out_shape=(f32((chips // 2, lanes)), f32((ch...  2.31 us
  transfers between devices with their start and end apart: 2, of which 0 were waited for; matrix products, arithmetic and copies ran while one was open for 0% of the time, Pallas kernels for 7%

profile of v13, /device:TPU:1, one launch (start us, length us, event | category | flops | bytes accessed | tf_op | source)
XLA Modules:
  0.0 78.9 jit_solution(944970392020881941)
XLA Ops:
  0.0 3.3 %place.1 = (f32[6208,128]{1,0:T(8,128)S(1)}, s32[1,512]{1,0:T(1,128)S(1)}) custom-call(f32[512,768]{1,0:T(8,128)} %emb_hbm.1, s32[1,512]{1,0:T(1,128)} %bitcast.20, s32[1,512]{1,0:T(1,128)} %bitcast.23), custom_call_target="tpu_custom_call" | custom-call | tf_op jit(solution)/shard_map/place/pallas_call | solution.py:343
  3.3 52.2 %all_to_all.10 = f32[6208,1,128]{2,1,0:T(1,128)S(1)} all-to-all(f32[6208,1,128]{2,1,0:T(1,128)S(1)} %bitcast.16), channel_id=1, replica_groups=mesh['y'=4,'x_hi'=2,'core'=2,'x_lo'=2,'z'=4] {'z','y','x_hi','x_lo'}, dimensions={0} | all-to-all | bytes 6356992 | tf_op jit(solution)/shard_map/all_to_all | solution.py:359
  55.6 0.2 fusion
  55.8 2.3 %collective-permute-start.1 = (f32[3104,1,128]{2,0,1:T(8,128)S(1)}, f32[3104,1,128]{2,0,1:T(8,128)S(1)}, u32[]{:S(2)}, u32[]{:S(2)}) collective-permute-start(f32[3104,1,128]{2,0,1:T(8,128)S(1)} %get-tuple-element.23), channel_id=1, source_target_pairs={{0,8},{8,0},{1,9},{9,1},{2,10},{10,2},{3,11},{11,3},{4,12},{12,4},... | collective-permute-start | bytes 4767752 | tf_op jit(solution)/shard_map/ppermute | solution.py:364
  58.1 0.1 collective-permute-start
  58.2 3.1 %own.1 = (bf16[1024,768]{1,0:T(8,128)(2,1)S(1)}, bf16[1024,768]{1,0:T(8,128)(2,1)S(1)}, f32[1024,128]{1,0:T(8,128)S(1)}, f32[1024,128]{1,0:T(8,128)S(1)}) custom-call(f32[6208,128]{1,0:T(8,128)S(1)} %bitcast.15), custom_call_target="tpu_custom_call" | custom-call | flops 4831838208 | bytes 8388608 | tf_op jit(solution)/shard_map/own/pallas_call | solution.py:369
  61.3 0.0 collective-permute-done.1
  61.3 2.3 %first.1 = (f32[32,128]{1,0:T(8,128)S(1)}, f32[32,128]{1,0:T(8,128)S(1)}, f32[512,128]{1,0:T(8,128)S(1)}) custom-call(f32[3104,128]{1,0:T(8,128)S(1)} %bitcast.22, bf16[1024,768]{1,0:T(8,128)(2,1)S(1)} %get-tuple-element.15.high_ref, bf16[1024,768]{1,0:T(8,128)(2,1)S(1)} %get-tuple-element.16.low_ref, f32[1024,128]{1,0:T(8,128)S(1)} %get-tuple-element.17.down_ref, ...), custom_call_target="tpu_custom_call" | custom-call | flops 1811939328 | bytes 2097152 | tf_op jit(solution)/shard_map/first/pallas_call | solution.py:390
  63.6 0.0 collective-permute-done
  63.6 0.0 copy-start
  63.6 1.1 %second.1 = f32[128,128]{1,0:T(8,128)S(1)} custom-call(f32[3104,128]{1,0:T(8,128)S(1)} %bitcast.17, bf16[1024,768]{1,0:T(8,128)(2,1)S(1)} %get-tuple-element.15.high_ref, bf16[1024,768]{1,0:T(8,128)(2,1)S(1)} %get-tuple-element.16.low_ref, f32[1024,128]{1,0:T(8,128)S(1)} %get-tuple-element.17.down_ref, f32[512,128]{1,0:T(8,128)S(1)} %get-tuple-element.19.total_ref, ...), custom_call_target="tpu_custom_call" | custom-call | flops 603979776 | bytes 2097152 | tf_op jit(solution)/shard_map/second/pallas_call | solution.py:402
  64.7 13.4 %all_to_all.11 = f32[128,1,128]{2,1,0:T(1,128)S(1)} all-to-all(f32[128,1,128]{2,1,0:T(1,128)S(1)} %bitcast.18), channel_id=1, replica_groups=mesh['y'=4,'x_hi'=2,'core'=2,'x_lo'=2,'z'=4] {'core','z','y','x_hi','x_lo'}, dimensions={0} | all-to-all | bytes 131072 | tf_op jit(solution)/shard_map/all_to_all | solution.py:412
  78.1 0.0 copy-done
  78.1 0.8 %pick.1 = f32[1,512]{1,0:T(1,128)} custom-call(f32[128,128]{1,0:T(8,128)S(1)} %bitcast.19, s32[1,512]{1,0:T(1,128)S(1)} %bitcast.21, s32[1,512]{1,0:T(1,128)S(1)} %get-tuple-element.22.rank_ref), custom_call_target="tpu_custom_call" | custom-call | tf_op jit(solution)/shard_map/pick/pallas_call | solution.py:415
Async XLA Ops:
  55.8 5.5 %collective-permute-start.1 = (f32[3104,1,128]{2,0,1:T(8,128)S(1)}, f32[3104,1,128]{2,0,1:T(8,128)S(1)}, u32[]{:S(2)}, u32[]{:S(2)}) collective-permute-start(f32[3104,1,128]{2,0,1:T(8,128)S(1)} %get-tuple-element.23), channel_id=1, source_target_pairs={{0,8},{8,0},{1,9},{9,1},{2,10},{10,2},{3,11},{11,3},{4,12},{12,4},... | collective-permute-start | bytes 4767752 | tf_op jit(solution)/shard_map/ppermute | solution.py:364
  58.1 5.6 %collective-permute-start = (f32[3104,1,128]{2,0,1:T(8,128)S(1)}, f32[3104,1,128]{2,0,1:T(8,128)S(1)}, u32[]{:S(2)}, u32[]{:S(2)}) collective-permute-start(f32[3104,1,128]{2,0,1:T(8,128)S(1)} %get-tuple-element.24), channel_id=1, source_target_pairs={{0,8},{8,0},{1,9},{9,1},{2,10},{10,2},{3,11},{11,3},{4,12},{12,4},... | collective-permute-start | bytes 4767752 | tf_op jit(solution)/shard_map/ppermute | solution.py:364
  63.6 14.5 %copy-start = (s32[512]{0:T(512)S(1)}, s32[512]{0:T(512)}, u32[]{:S(2)}) copy-start(s32[512]{0:T(512)} %param.4) | copy-start | bytes 6148

commit v14 on v13

--- a/solution.py
+++ b/solution.py
@@ -325,8 +325,9 @@
     by_rank = dot_f32(
         jnp.concatenate([high, low], axis=0), jnp.concatenate([owner, owner], axis=0), tn
     )
-    at_rank = lax.broadcasted_iota(jnp.int32, (lanes, count), 0) == rank_ref[...]
-    out_ref[...] = jnp.sum(jnp.where(at_rank, by_rank, 0.0), axis=0, keepdims=True)
+    slots = 16
+    at_rank = lax.broadcasted_iota(jnp.int32, (slots, count), 0) == rank_ref[...]
+    out_ref[...] = jnp.sum(jnp.where(at_rank, by_rank[:slots, :], 0.0), axis=0, keepdims=True)
 
 
 def on_device(embeddings, clusters, indices):

time: 79.1 us -> 79.1 us (level)
  no operation moved by 1% of the time
where the time goes in v14:
time: 79.1 us; the launch traced here: 78.9 us
  blocking collectives  65.6 us (83%)
  Pallas kernels  10.6 us (13%)
  starting transfers between devices  2.38 us (3%)
    all_to_all x1, blocking collectives, on_device(): lax.all_to_all(sending.reshape(chips * length, 1, lanes), chip_axes, spli...  52.2 us
    all_to_all x1, blocking collectives, on_device(): lax.all_to_all(result.reshape(2 * chips, 1, lanes), ('core',) + chip_axes...  13.4 us
    pallas_call x1, Pallas kernels, on_device(): pl.pallas_call(place_kernel, out_shape=(f32((chips * length, lanes)), jax...  3.34 us
    pallas_call x1, Pallas kernels, on_device(): pl.pallas_call(own_kernel, out_shape=(bf16((rows, width)), bf16((rows, wi...  3.13 us
    ppermute x2, starting transfers between devices, on_device(): lax.ppermute(held[h * part:(h + 1) * part], 'core', [(0, 1), (1, 0)])  2.38 us
    pallas_call x1, Pallas kernels, on_device(): pl.pallas_call(first_kernel, out_shape=(f32((chips // 2, lanes)), f32((ch...  2.31 us
  transfers between devices with their start and end apart: 2, of which 0 were waited for; matrix products, arithmetic and copies ran while one was open for 0% of the time, Pallas kernels for 7%

profile of v14, /device:TPU:1, one launch (start us, length us, event | category | flops | bytes accessed | tf_op | source)
XLA Modules:
  0.0 78.9 jit_solution(13906627471380440811)
XLA Ops:
  0.0 3.3 %place.1 = (f32[6208,128]{1,0:T(8,128)S(1)}, s32[1,512]{1,0:T(1,128)S(1)}) custom-call(f32[512,768]{1,0:T(8,128)} %emb_hbm.1, s32[1,512]{1,0:T(1,128)} %bitcast.20, s32[1,512]{1,0:T(1,128)} %bitcast.23), custom_call_target="tpu_custom_call" | custom-call | tf_op jit(solution)/shard_map/place/pallas_call | solution.py:344
  3.3 52.2 %all_to_all.10 = f32[6208,1,128]{2,1,0:T(1,128)S(1)} all-to-all(f32[6208,1,128]{2,1,0:T(1,128)S(1)} %bitcast.16), channel_id=1, replica_groups=mesh['y'=4,'x_hi'=2,'core'=2,'x_lo'=2,'z'=4] {'z','y','x_hi','x_lo'}, dimensions={0} | all-to-all | bytes 6356992 | tf_op jit(solution)/shard_map/all_to_all | solution.py:360
  55.6 0.2 fusion
  55.8 2.3 %collective-permute-start.1 = (f32[3104,1,128]{2,0,1:T(8,128)S(1)}, f32[3104,1,128]{2,0,1:T(8,128)S(1)}, u32[]{:S(2)}, u32[]{:S(2)}) collective-permute-start(f32[3104,1,128]{2,0,1:T(8,128)S(1)} %get-tuple-element.23), channel_id=1, source_target_pairs={{0,8},{8,0},{1,9},{9,1},{2,10},{10,2},{3,11},{11,3},{4,12},{12,4},... | collective-permute-start | bytes 4767752 | tf_op jit(solution)/shard_map/ppermute | solution.py:365
  58.1 0.1 collective-permute-start
  58.2 3.1 %own.1 = (bf16[1024,768]{1,0:T(8,128)(2,1)S(1)}, bf16[1024,768]{1,0:T(8,128)(2,1)S(1)}, f32[1024,128]{1,0:T(8,128)S(1)}, f32[1024,128]{1,0:T(8,128)S(1)}) custom-call(f32[6208,128]{1,0:T(8,128)S(1)} %bitcast.15), custom_call_target="tpu_custom_call" | custom-call | flops 4831838208 | bytes 8388608 | tf_op jit(solution)/shard_map/own/pallas_call | solution.py:370
  61.3 0.0 collective-permute-done.1
  61.3 2.3 %first.1 = (f32[32,128]{1,0:T(8,128)S(1)}, f32[32,128]{1,0:T(8,128)S(1)}, f32[512,128]{1,0:T(8,128)S(1)}) custom-call(f32[3104,128]{1,0:T(8,128)S(1)} %bitcast.22, bf16[1024,768]{1,0:T(8,128)(2,1)S(1)} %get-tuple-element.15.high_ref, bf16[1024,768]{1,0:T(8,128)(2,1)S(1)} %get-tuple-element.16.low_ref, f32[1024,128]{1,0:T(8,128)S(1)} %get-tuple-element.17.down_ref, ...), custom_call_target="tpu_custom_call" | custom-call | flops 1811939328 | bytes 2097152 | tf_op jit(solution)/shard_map/first/pallas_call | solution.py:391
  63.6 0.0 collective-permute-done
  63.6 0.0 copy-start
  63.6 1.1 %second.1 = f32[128,128]{1,0:T(8,128)S(1)} custom-call(f32[3104,128]{1,0:T(8,128)S(1)} %bitcast.17, bf16[1024,768]{1,0:T(8,128)(2,1)S(1)} %get-tuple-element.15.high_ref, bf16[1024,768]{1,0:T(8,128)(2,1)S(1)} %get-tuple-element.16.low_ref, f32[1024,128]{1,0:T(8,128)S(1)} %get-tuple-element.17.down_ref, f32[512,128]{1,0:T(8,128)S(1)} %get-tuple-element.19.total_ref, ...), custom_call_target="tpu_custom_call" | custom-call | flops 603979776 | bytes 2097152 | tf_op jit(solution)/shard_map/second/pallas_call | solution.py:403
  64.7 13.4 %all_to_all.11 = f32[128,1,128]{2,1,0:T(1,128)S(1)} all-to-all(f32[128,1,128]{2,1,0:T(1,128)S(1)} %bitcast.18), channel_id=1, replica_groups=mesh['y'=4,'x_hi'=2,'core'=2,'x_lo'=2,'z'=4] {'core','z','y','x_hi','x_lo'}, dimensions={0} | all-to-all | bytes 131072 | tf_op jit(solution)/shard_map/all_to_all | solution.py:413
  78.1 0.0 copy-done
  78.1 0.8 pick.1
Async XLA Ops:
  55.8 5.5 %collective-permute-start.1 = (f32[3104,1,128]{2,0,1:T(8,128)S(1)}, f32[3104,1,128]{2,0,1:T(8,128)S(1)}, u32[]{:S(2)}, u32[]{:S(2)}) collective-permute-start(f32[3104,1,128]{2,0,1:T(8,128)S(1)} %get-tuple-element.23), channel_id=1, source_target_pairs={{0,8},{8,0},{1,9},{9,1},{2,10},{10,2},{3,11},{11,3},{4,12},{12,4},... | collective-permute-start | bytes 4767752 | tf_op jit(solution)/shard_map/ppermute | solution.py:365
  58.1 5.6 %collective-permute-start = (f32[3104,1,128]{2,0,1:T(8,128)S(1)}, f32[3104,1,128]{2,0,1:T(8,128)S(1)}, u32[]{:S(2)}, u32[]{:S(2)}) collective-permute-start(f32[3104,1,128]{2,0,1:T(8,128)S(1)} %get-tuple-element.24), channel_id=1, source_target_pairs={{0,8},{8,0},{1,9},{9,1},{2,10},{10,2},{3,11},{11,3},{4,12},{12,4},... | collective-permute-start | bytes 4767752 | tf_op jit(solution)/shard_map/ppermute | solution.py:365
  63.6 14.5 %copy-start = (s32[512]{0:T(512)S(1)}, s32[512]{0:T(512)}, u32[]{:S(2)}) copy-start(s32[512]{0:T(512)} %param.4) | copy-start | bytes 6148
